TPU v7x, 512 devices: a whole 4x4x16 slice. The times are simulated.
512 devices in a mesh: basin: 64 (over z, x), reach: 8 (over y, core).
Axes of the slice: x: 4, y: 4, z: 16, core: 2. Of those that a mesh axis runs over, the one named last changes fastest.
Arguments:
- reach_residual: float32 [384, 24, 128], P('basin', 'reach'), may hold values from -4 to 4
- chain_inv: float32 [384, 24, 128, 128], P('basin', 'reach'), may hold values from -1 to 2
- chain_link: float32 [384, 24, 128, 128], P('basin', 'reach'), may hold values from -1 to 1
- outlet_link: float32 [384, 128, 128], P('basin'), may hold values from -0.5 to 0.5
- junction_inv: float32 [384, 128, 128], P('basin'), may hold values from -1 to 1
- junction_residual: float32 [384, 128], P('basin'), may hold values from -6 to 6
- upper_junction: int32 [384], P('basin'), may hold values from 0 to 383
- lower_junction: int32 [384], P('basin'), may hold values from 0 to 383
- cell_cotangent: float32 [384, 24, 128], P('basin', 'reach'), may hold values from -4 to 4
- junction_cotangent: float32 [384, 128], P('basin'), may hold values from -6 to 6
Outputs:
- cell_update: float32 [384, 24, 128], P('basin', 'reach')
- section_update: float32 [384, 128], P('basin')
- cell_adjoint: float32 [384, 24, 128], P('basin', 'reach')
- junction_adjoint: float32 [384, 128], P('basin')
Inputs may be any that keep to these rules, and one draw needn't show every extreme that they name: `upper_junction`: junction ids. `lower_junction`: junction ids.
All inputs are finite; a program needn't handle non-finite values.
Results may differ from a plain program's by a relative error of at most 0.00014.
Values sent between devices are 32-bit elements; how exact they have to be, the bound alone decides.
No kernel may reach another device: no remote copies, remote signals or barrier semaphores. Data moves between devices by JAX's collectives and lax.ppermute only.
A program may use at most 64 MiB of HBM per device.

v0:
```python
import jax
import jax.numpy as jnp
from jax import lax
from jax.sharding import PartitionSpec as P

SWEEPS = 4


precise = lax.Precision.HIGHEST


def entering(x, axis, combine, identity, reverse):
    length, place = (lax.axis_size(axis), lax.axis_index(axis))
    everything = jax.tree.map(lambda part: lax.all_gather(part, axis), x)
    start = jax.tree.map(
        lambda part, zero: jnp.broadcast_to(jnp.asarray(zero, part.dtype), part.shape), x, identity
    )

    def lap(k, before):
        at = length - 1 - k if reverse else k
        reached = at > place if reverse else at < place
        new = combine(before, jax.tree.map(lambda part: part[at], everything))
        return jax.tree.map(lambda a, b: jnp.where(reached, a, b), new, before)

    return lax.fori_loop(0, length, lap, start)


def from_root(block, axis, holder):
    block = jnp.where(lax.axis_index(axis) == holder, block, jnp.zeros_like(block))
    return lax.psum(block, axis)


def product(former, latter):
    return jnp.einsum("sij,sjk->sik", former, latter, precision=precise)


def applied(matrix, vector):
    return jnp.einsum("sij,sj->si", matrix, vector, precision=precise)


def applied_transposed(matrix, vector):
    return jnp.einsum("sji,sj->si", matrix, vector, precision=precise)


def compose(former, latter):
    return (product(latter[0], former[0]), applied(latter[0], former[1]) + latter[1])


def identity_map(members, tile_width):
    eye_block = jnp.broadcast_to(
        jnp.eye(tile_width, dtype=jnp.float32), (members, tile_width, tile_width)
    )
    return (eye_block, jnp.zeros((members, tile_width), jnp.float32))


def entry_maps(local_map, neutral):
    return entering(local_map, "reach", compose, neutral, False)


def exit_maps(local_map, neutral):
    return entering(local_map, "reach", compose, neutral, True)


def shards(
    reach_residual,
    chain_inv,
    chain_link,
    outlet_link,
    junction_inv,
    junction_residual,
    upper_junction,
    lower_junction,
    cell_cotangent,
    junction_cotangent,
):
    members, blocks, tile_width = reach_residual.shape
    owned_rows = junction_inv.shape[0]
    junctions = owned_rows * lax.axis_size("basin")
    final_reach = lax.axis_size("reach") - 1
    multiplier = jnp.einsum("skij,skjl->skil", chain_inv, chain_link, precision=precise)
    forced = jnp.einsum("skij,skj->ski", chain_inv, reach_residual, precision=precise)
    local_matrix = multiplier[:, 0]
    local_vector = forced[:, 0]
    for number in range(1, blocks):
        local_matrix = product(multiplier[:, number], local_matrix)
        local_vector = applied(multiplier[:, number], local_vector) + forced[:, number]
    neutral = identity_map(members, tile_width)
    entry_map = entry_maps((local_matrix, local_vector), neutral)
    outlet = compose(entry_map, (local_matrix, local_vector))
    schur_tile = product(outlet_link, outlet[0])
    outlet_push = applied(outlet_link, outlet[1])
    schur_tile, outlet_push = (
        from_root(schur_tile, "reach", final_reach),
        from_root(outlet_push, "reach", final_reach),
    )
    backward = cell_cotangent[:, blocks - 1]
    for number in range(blocks - 2, -1, -1):
        backward = cell_cotangent[:, number] + applied_transposed(
            multiplier[:, number + 1], backward
        )
    local_back = applied_transposed(multiplier[:, 0], backward)
    reverse_local = (jnp.swapaxes(local_matrix, 1, 2), local_back)
    leaving = exit_maps(reverse_local, neutral)
    head_value = applied(reverse_local[0], leaving[1]) + local_back
    upward = from_root(head_value, "reach", 0)
    junction_rows = jnp.arange(junctions, dtype=jnp.int32)[:, None]
    lower_onehot = (junction_rows == lower_junction[None, :]).astype(jnp.float32)
    upper_onehot = (junction_rows == upper_junction[None, :]).astype(jnp.float32)

    def section_terms(section_all):
        return outlet_push + applied(schur_tile, section_all[upper_junction])

    def adjoint_terms(relief_all):
        return upward + applied_transposed(schur_tile, relief_all[lower_junction])

    sections = jnp.zeros((owned_rows, tile_width), jnp.float32)
    adjoint = jnp.zeros((owned_rows, tile_width), jnp.float32)

    def gather_sections(values):
        return lax.all_gather(values, "basin", axis=0, tiled=True)

    def gather_relief(values):
        return lax.all_gather(values, "basin", axis=0, tiled=True)

    for sweep_index in range(SWEEPS):
        inflow_terms = outlet_push if sweep_index == 0 else section_terms(gather_sections(sections))
        placed = jnp.dot(lower_onehot, inflow_terms, precision=precise)
        inflow = lax.psum_scatter(placed, "basin", scatter_dimension=0, tiled=True)
        sections = applied(junction_inv, junction_residual + inflow)
    for sweep_index in range(SWEEPS):
        return_terms = (
            upward
            if sweep_index == 0
            else adjoint_terms(gather_relief(applied_transposed(junction_inv, adjoint)))
        )
        placed = jnp.dot(upper_onehot, return_terms, precision=precise)
        adjoint = junction_cotangent + lax.psum_scatter(
            placed, "basin", scatter_dimension=0, tiled=True
        )
    section_all = gather_sections(sections)
    relief_all = gather_relief(applied_transposed(junction_inv, adjoint))
    head_sections = section_all[upper_junction]
    tail_relief = relief_all[lower_junction]
    carried = applied(entry_map[0], head_sections) + entry_map[1]
    cell_rows = []
    for number in range(blocks):
        carried = applied(multiplier[:, number], carried) + forced[:, number]
        cell_rows.append(carried)
    cell_update = jnp.stack(cell_rows, axis=1)
    incoming = applied_transposed(outlet_link, tail_relief)
    carried = cell_cotangent[:, blocks - 1] + applied(leaving[0], incoming) + leaving[1]
    collected = [carried]
    for number in range(blocks - 2, -1, -1):
        carried = cell_cotangent[:, number] + applied_transposed(multiplier[:, number + 1], carried)
        collected.append(carried)
    cell_adjoint = jnp.stack(collected[::-1], axis=1)
    return (cell_update, sections, cell_adjoint, adjoint)


def solution(mesh):
    placed = (
        P("basin", "reach", None),
        P("basin", "reach", None, None),
        P("basin", "reach", None, None),
        P("basin", None, None),
        P("basin", None, None),
        P("basin", None),
        P("basin"),
        P("basin"),
        P("basin", "reach", None),
        P("basin", None),
    )
    return jax.shard_map(
        shards,
        mesh=mesh,
        in_specs=placed,
        out_specs=(
            P("basin", "reach", None),
            P("basin", None),
            P("basin", "reach", None),
            P("basin", None),
        ),
        check_vma=False,
    )
```

profile of v0, /device:TPU:8, one launch (start us, length us, event | category | flops | bytes accessed | tf_op | source)
XLA Modules:
  0.0 1940.1 jit_solution(3543780025443325133)
XLA Ops:
  8.4 2.5 fusion.138
  15.3 16.4 all-gather.9
  31.7 1.9 fusion.48
  35.1 13.7 all-gather.4
  52.1 32.2 %while.35 = (s32[]{:T(128)}, f32[6,128,128]{2,1,0:T(8,128)S(1)}, f32[6,128]{1,0:T(8,128)S(1)}, s32[]{:T(128)}, f32[8,6,128,128]{3,2,1,0:T(8,128)}, /*index=5*/f3...) while((s32[]{:T(128)}, f32[6,128,128]{2,1,0:T(8,128)S(1)}, ...), condition=%wide.region_9.10_spmd.clone, body=%wide.region_8.9_spmd.clone.sunk | while | flops 152275968 | bytes 2777269 | solution.py:25
  52.1 1.7 fusion.194
  56.2 1.7 fusion.194
  60.2 1.7 fusion.194
  64.2 1.7 fusion.194
  68.2 1.7 fusion.194
  72.2 1.7 fusion.194
  76.3 1.7 fusion.194
  80.3 1.7 fusion.194
  82.7 1.6 convolution_select_fusion.6
  85.3 4.5 all-gather.17.cloned.1.call-done
  90.7 32.1 %while.34 = (s32[]{:T(128)}, f32[6,128,128]{2,1,0:T(8,128)S(1)}, f32[6,128]{1,0:T(8,128)S(1)}, s32[]{:T(128)}, f32[8,6,128,128]{3,2,1,0:T(8,128)}, /*index=5*/f32[8,6,128]{2,1,0:T(8,128)}, s32[]{:T(128)}, s32[]{:T(128)}) while((s32[]{:T(128)}, f32[6,128,128]{2,1,0:T(8,128)S(1)}, f32[6,128]{1,0:T(8,128)S(1)}, s32[]{:T(128)}, ...), condition=%wide.region_1.2_spmd.clone, body=%wide.region_0.1_spmd.clone.sunk | while | flops 152275968 | bytes 2778223 | solution.py:25
  90.7 1.7 fusion.188
  94.7 1.7 fusion.188
  98.7 1.7 fusion.188
  102.7 1.7 fusion.188
  106.8 1.7 fusion.188
  110.8 1.7 fusion.188
  114.8 1.7 fusion.188
  118.8 1.7 fusion.188
  124.9 1.7 fusion.122
  126.6 12.1 all-reduce.12
  138.8 1.6 fusion.34
  142.2 1.8 fusion.139
  144.1 2.7 fusion.18
  146.8 261.6 %all-reduce.27.cloned.1.call-done = (f32[384,128]{1,0:T(8,128)}, f32[384,128]{1,0:T(8,128)}) async-done(((f32[384,128]{1,0:T(8,128)}, f32[384,128]{1,0:T(8,128)}), (f32[384,128]{1,0:T(8,128)}, f32[384,128]{1,0:T(8,128)})) %all-reduce.27.cloned.1.call-update) | async-done | bytes 393232
  410.2 85.1 %all-gather.10 = f32[64,6,128]{2,1,0:T(8,128)} all-gather(f32[1,6,128]{2,1,0:T(8,128)S(1)} %bitcast.365), channel_id=1, replica_groups=mesh['basin'=64,'reach'=8] {'basin'}, dimensions={0}, use_global_device_ids=true | all-gather | bytes 199680 | tf_op jit(solution)/shard_map/all_gather | solution.py:123
  495.3 1.6 reshape.99
  497.0 2.2 gather_fusion.4
  499.2 1.7 fusion.94
  500.9 1.6 fusion.33
  503.9 86.5 %all-gather.5 = f32[64,6,128]{2,1,0:T(8,128)} all-gather(f32[1,6,128]{2,1,0:T(8,128)S(1)} %bitcast.366), channel_id=1, replica_groups=mesh['basin'=64,'reach'=8] {'basin'}, dimensions={0}, use_global_device_ids=true | all-gather | bytes 199680 | tf_op jit(solution)/shard_map/all_gather | solution.py:120
  590.4 1.7 reshape.89
  592.1 2.2 gather_fusion
  595.7 1.6 fusion.37
  597.4 259.3 %all-reduce.25.cloned.1.call-done = (f32[384,128]{1,0:T(8,128)}, f32[384,128]{1,0:T(8,128)}) async-done(((f32[384,128]{1,0:T(8,128)}, f32[384,128]{1,0:T(8,128)}), (f32[384,128]{1,0:T(8,128)}, f32[384,128]{1,0:T(8,128)})) %all-reduce.25.cloned.1.call-update) | async-done | bytes 393232
  857.8 85.1 %all-gather.11 = f32[64,6,128]{2,1,0:T(8,128)} all-gather(f32[1,6,128]{2,1,0:T(8,128)S(1)} %bitcast.367), channel_id=1, replica_groups=mesh['basin'=64,'reach'=8] {'basin'}, dimensions={0}, use_global_device_ids=true | all-gather | bytes 199680 | tf_op jit(solution)/shard_map/all_gather | solution.py:123
  942.9 1.7 reshape.101
  944.5 2.2 gather_fusion.5
  946.7 1.7 fusion.90
  948.4 1.6 fusion.32
  951.5 86.5 %all-gather.6 = f32[64,6,128]{2,1,0:T(8,128)} all-gather(f32[1,6,128]{2,1,0:T(8,128)S(1)} %bitcast.368), channel_id=1, replica_groups=mesh['basin'=64,'reach'=8] {'basin'}, dimensions={0}, use_global_device_ids=true | all-gather | bytes 199680 | tf_op jit(solution)/shard_map/all_gather | solution.py:120
  1037.9 1.7 reshape.91
  1039.6 2.2 gather_fusion.1
  1043.2 1.6 fusion.36
  1044.9 259.3 %all-reduce.23.cloned.1.call-done = (f32[384,128]{1,0:T(8,128)}, f32[384,128]{1,0:T(8,128)}) async-done(((f32[384,128]{1,0:T(8,128)}, f32[384,128]{1,0:T(8,128)}), (f32[384,128]{1,0:T(8,128)}, f32[384,128]{1,0:T(8,128)})) %all-reduce.23.cloned.1.call-update) | async-done | bytes 393232
  1305.4 85.1 %all-gather.12 = f32[64,6,128]{2,1,0:T(8,128)} all-gather(f32[1,6,128]{2,1,0:T(8,128)S(1)} %bitcast.369), channel_id=1, replica_groups=mesh['basin'=64,'reach'=8] {'basin'}, dimensions={0}, use_global_device_ids=true | all-gather | bytes 199680 | tf_op jit(solution)/shard_map/all_gather | solution.py:123
  1390.5 1.7 reshape.103
  1392.2 2.2 gather_fusion.6
  1394.4 1.7 fusion.86
  1396.1 1.6 fusion.31
  1399.2 86.7 %all-gather.7 = f32[64,6,128]{2,1,0:T(8,128)} all-gather(f32[1,6,128]{2,1,0:T(8,128)S(1)} %bitcast.370), channel_id=1, replica_groups=mesh['basin'=64,'reach'=8] {'basin'}, dimensions={0}, use_global_device_ids=true | all-gather | bytes 199680 | tf_op jit(solution)/shard_map/all_gather | solution.py:120
  1485.9 1.7 reshape.93
  1487.5 2.2 gather_fusion.2
  1491.1 1.6 fusion.35
  1492.8 259.4 %all-reduce.21.cloned.1.call-done = (f32[384,128]{1,0:T(8,128)}, f32[384,128]{1,0:T(8,128)}) async-done(((f32[384,128]{1,0:T(8,128)}, f32[384,128]{1,0:T(8,128)}), (f32[384,128]{1,0:T(8,128)}, f32[384,128]{1,0:T(8,128)})) %all-reduce.21.cloned.1.call-update) | async-done | bytes 393232
  1753.9 85.1 %all-gather.13 = f32[64,6,128]{2,1,0:T(8,128)} all-gather(f32[1,6,128]{2,1,0:T(8,128)S(1)} %bitcast.371), channel_id=1, replica_groups=mesh['basin'=64,'reach'=8] {'basin'}, dimensions={0}, use_global_device_ids=true | all-gather | bytes 199680 | tf_op jit(solution)/shard_map/all_gather | solution.py:123
  1839.0 1.7 reshape.105
  1840.6 2.2 gather_fusion.7
  1848.0 81.0 %all-gather.8 = f32[64,6,128]{2,1,0:T(8,128)S(1)} all-gather(f32[1,6,128]{2,1,0:T(8,128)S(1)} %bitcast.363), channel_id=1, replica_groups=mesh['basin'=64,'reach'=8] {'basin'}, dimensions={0}, use_global_device_ids=true | all-gather | bytes 199680 | tf_op jit(solution)/shard_map/all_gather | solution.py:120
  (208 shorter events, 73.8 us)
Async XLA Ops:
  7.2 1.3 copy-start
  7.2 44.8 %all-gather.19.cloned.1.call-start = ((), (), s32[]{:S(2)}) async-start(), calls=%async_computation.2 | async-start | bytes 3538944 | tf_op jit(solution)/shard_map/all_gather | solution.py:14
  11.5 2.3 copy-start.23
  12.0 1.0 copy-start.2
  13.0 18.8 copy-start.22
  13.0 76.8 %all-gather.17.cloned.1.call-start = ((), (), s32[]{:S(2)}) async-start(), calls=%async_computation.1 | async-start | bytes 3538944 | tf_op jit(solution)/shard_map/all_gather | solution.py:14
  13.7 394.7 %all-reduce.27.cloned.1.call-start = ((), (), s32[]{:S(2)}) async-start(), calls=%async_computation.6 | async-start | bytes 786432
  13.8 38.2 %copy-start.4 = (f32[128,128]{1,0:T(8,128)}, f32[128,128]{1,0:T(8,128)S(1)}, u32[]{:S(2)}) copy-start(f32[128,128]{1,0:T(8,128)S(1)} %fusion.47) | copy-start | bytes 196612
  13.9 17.8 copy-start.12
  13.9 17.8 copy-start.14
  13.9 17.8 copy-start.16
  14.8 34.0 %copy-start.21 = (s32[6]{0:T(128)S(1)}, s32[6]{0:T(128)}, u32[]{:S(2)}) copy-start(s32[6]{0:T(128)} %param.21) | copy-start | bytes 76
  14.8 34.6 %copy-start.20 = (s32[6]{0:T(128)S(1)}, s32[6]{0:T(128)}, u32[]{:S(2)}) copy-start(s32[6]{0:T(128)} %param.20) | copy-start | bytes 76
  33.7 18.4 copy-start.5
  35.1 17.0 copy-start.11
  52.1 32.2 %copy-start.3 = (f32[6,128,128]{2,1,0:T(8,128)S(1)}, f32[6,128,128]{2,1,0:T(8,128)}, u32[]{:S(2)}) copy-start(f32[6,128,128]{2,1,0:T(8,128)} %copy-done.2) | copy-start | bytes 1179652
  138.7 3.4 copy-start.9
  138.8 3.4 copy-start.10
  141.9 357.2 %all-reduce.19.cloned.1.call-start = ((), (), s32[]{:S(2)}) async-start(), calls=%async_computation | async-start | bytes 786432 | tf_op jit(solution)/shard_map/psum | solution.py:30
  142.2 266.2 %copy-start.7 = (f32[6,128]{1,0:T(8,128)S(1)}, f32[6,128]{1,0:T(8,128)}, u32[]{:S(2)}) copy-start(f32[6,128]{1,0:T(8,128)} %param.23) | copy-start | bytes 9220
  142.2 266.2 %copy-start.8 = (f32[6,128]{1,0:T(8,128)S(1)}, f32[6,128]{1,0:T(8,128)}, u32[]{:S(2)}) copy-start(f32[6,128]{1,0:T(8,128)} %param.19) | copy-start | bytes 9220
  142.2 267.5 %copy-start.1 = (f32[6,128,128]{2,1,0:T(8,128)S(1)}, f32[6,128,128]{2,1,0:T(8,128)}, u32[]{:S(2)}) copy-start(f32[6,128,128]{2,1,0:T(8,128)} %param.18) | copy-start | bytes 1179652
  146.8 709.9 %all-reduce.25.cloned.1.call-start = ((), (), s32[]{:S(2)}) async-start(), calls=%async_computation.5 | async-start | bytes 786432
  597.3 707.0 %all-reduce.23.cloned.1.call-start = ((), (), s32[]{:S(2)}) async-start(), calls=%async_computation.4 | async-start | bytes 786432
  1044.9 707.3 %all-reduce.21.cloned.1.call-start = ((), (), s32[]{:S(2)}) async-start(), calls=%async_computation.3 | async-start | bytes 786432
  1752.9 0.6 copy-start.19
  1752.9 92.1 %copy-start.13 = (f32[6,1,128]{2,1,0:T(1,128)S(1)}, f32[6,1,128]{2,1,0:T(1,128)}, u32[]{:S(2)}) copy-start(f32[6,1,128]{2,1,0:T(1,128)} %copy-done.12) | copy-start | bytes 9220
  1842.8 2.6 copy-start.15
  1842.8 3.1 copy-start.17
  1845.5 85.7 %copy-start.6 = (f32[6,3,1,128]{3,0,1,2:T(8,128)S(1)}, f32[6,3,1,128]{3,0,1,2:T(8,128)}, u32[]{:S(2)}) copy-start(f32[6,3,1,128]{3,0,1,2:T(8,128)} %copy-done.5) | copy-start | bytes 27652
  1848.0 84.6 %copy-start.18 = (f32[6,1,128]{2,0,1:T(8,128)}, f32[6,1,128]{2,0,1:T(8,128)S(1)}, u32[]{:S(2)}) copy-start(f32[6,1,128]{2,0,1:T(8,128)S(1)} %copy.279) | copy-start | bytes 9220
Sparse Core Ops, SparseCore 0:
  13.1 38.8 all-gather.18
  54.1 35.6 all-gather.16
  142.1 266.3 all-reduce.26
  410.6 68.1 all-reduce.18
  597.5 259.1 all-reduce.24
  1045.0 259.2 all-reduce.22
  1492.9 259.2 all-reduce.20
where the time goes:
time: 1940 us
  waiting for transfers between devices  1040 us (54%)
  blocking collectives  723 us (37%)
  matrix products  102 us (5%)
  local copies, waits for them, and re-layouts  34.4 us (2%)
  other arithmetic  19.5 us (1%)
    unnamed x11, waiting for transfers between devices  1040 us
    all_gather x4, blocking collectives, gather_sections(): return lax.all_gather(values, 'basin', axis=0, tiled=True)  341 us
    all_gather x4, blocking collectives, gather_relief(): return lax.all_gather(values, 'basin', axis=0, tiled=True)  340 us
    dot_general x33, matrix products, applied(): return jnp.einsum('sij,sj->si', matrix, vector, precision=precise)  43.8 us
  transfers between devices with their start and end apart: 7, of which 5 were waited for; matrix products, arithmetic and copies ran while one was open for 3% of the time, Pallas kernels for 0%

commit v1 on v0

v1 whole, which is shorter than its diff:
```python
import jax
import jax.numpy as jnp
from jax import lax
from jax.experimental import pallas as pl
from jax.experimental.pallas import tpu as pltpu
from jax.sharding import Mesh, PartitionSpec as P

SWEEPS = 4

precise = lax.Precision.HIGHEST


def product(left, right):
    return jnp.einsum("sij,sjk->sik", left, right, precision=precise)


def applied(matrix, vector):
    return jnp.einsum("sij,sj->si", matrix, vector, precision=precise)


def applied_transposed(matrix, vector):
    return jnp.einsum("sji,sj->si", matrix, vector, precision=precise)


def everyone(values, axis):
    count = lax.axis_size(axis)
    spread = jnp.broadcast_to(values[None], (count,) + values.shape)
    return lax.all_to_all(spread, axis, 0, 0, tiled=False)


def all_basins(rows):
    along_z = everyone(rows, "z")
    along_x = everyone(along_z, "x")
    return jnp.swapaxes(along_x, 0, 1).reshape((-1,) + rows.shape)


def packed(matrix, *vectors):
    members, _, width = matrix.shape
    rows = [matrix] + [v[:, None, :] for v in vectors]
    pad = -len(vectors) % 8
    return jnp.concatenate(rows + [jnp.zeros((members, pad, width), matrix.dtype)], axis=1)


def pick(table, rows, keep):
    count = rows.shape[0]

    def kernel(rows_ref, keep_ref, table_ref, out_ref):
        for k in range(count):
            out_ref[k] = jnp.where(keep_ref[k] > 0, table_ref[rows_ref[k]], 0.0)

    smem = pl.BlockSpec(memory_space=pltpu.SMEM)
    vmem = pl.BlockSpec(memory_space=pltpu.VMEM)
    return pl.pallas_call(
        kernel,
        out_shape=jax.ShapeDtypeStruct((count,) + table.shape[1:], table.dtype),
        in_specs=[smem, smem, vmem],
        out_specs=vmem,
    )(rows, keep, table)


def shards(
    reach_residual,
    chain_inv,
    chain_link,
    outlet_link,
    junction_inv,
    junction_residual,
    upper_junction,
    lower_junction,
    cell_cotangent,
    junction_cotangent,
):
    members, blocks, width = reach_residual.shape
    owned = junction_inv.shape[0]
    zs, xs, ys = lax.axis_size("z"), lax.axis_size("x"), lax.axis_size("y")
    z, x, y, c = (lax.axis_index(a) for a in ("z", "x", "y", "c"))
    half = members // 2
    piece = width // ys

    def mine(array):
        return lax.dynamic_slice_in_dim(array, c * half, half, 0)

    part = lax.dynamic_slice_in_dim(junction_inv, y * piece, piece, 1)
    table = lax.all_gather(packed(part, junction_residual, junction_cotangent), "z")
    table = table.reshape((zs * owned,) + table.shape[2:])

    multiplier = jnp.einsum("skij,skjl->skil", chain_inv, chain_link, precision=precise)
    forced = jnp.einsum("skij,skj->ski", chain_inv, reach_residual, precision=precise)
    local_map = multiplier[:, 0]
    local_vector = forced[:, 0]
    for number in range(1, blocks):
        local_map = product(multiplier[:, number], local_map)
        local_vector = applied(multiplier[:, number], local_vector) + forced[:, number]
    backward = cell_cotangent[:, blocks - 1]
    for number in range(blocks - 2, -1, -1):
        backward = cell_cotangent[:, number] + applied_transposed(
            multiplier[:, number + 1], backward
        )
    local_back = applied_transposed(multiplier[:, 0], backward)

    pair = lax.all_gather(packed(local_map, local_vector, local_back), "c")
    first, second = mine(pair[0]), mine(pair[1])
    first_map, second_map = first[:, :width], second[:, :width]
    chip_map = product(second_map, first_map)
    chip_vector = applied(second_map, first[:, width]) + second[:, width]
    chip_back = applied_transposed(first_map, second[:, width + 1]) + first[:, width + 1]

    chips = lax.all_gather(packed(chip_map, chip_vector, chip_back), "y")
    maps, vectors, backs = chips[:, :, :width], chips[:, :, width], chips[:, :, width + 1]
    eye = jnp.broadcast_to(jnp.eye(width, dtype=jnp.float32), (half, width, width))
    before, before_vector = eye, jnp.zeros((half, width), jnp.float32)
    reached, reached_vector = before, before_vector
    for k in range(ys):
        reached_vector = applied(maps[k], reached_vector) + vectors[k] if k else vectors[0]
        if k < ys - 1:
            reached = product(maps[k], reached) if k else maps[0]
            before = jnp.where(y == k + 1, reached, before)
            before_vector = jnp.where(y == k + 1, reached_vector, before_vector)
    outlet = mine(outlet_link)
    schur, after = outlet, outlet
    upward = jnp.zeros((half, width), jnp.float32)
    after_vector = upward
    for k in range(ys - 1, -1, -1):
        after = jnp.where(y == k, schur, after)
        after_vector = jnp.where(y == k, upward, after_vector)
        schur = product(schur, maps[k])
        upward = applied_transposed(maps[k], upward) + backs[k]
    push = applied(outlet, reached_vector)

    ends = lax.all_gather(jnp.stack([push, upward]), "c")
    push_all = jnp.concatenate([ends[0, 0], ends[1, 0]])
    upward_all = jnp.concatenate([ends[0, 1], ends[1, 1]])

    lanes = jnp.zeros((width - 2 * members,), jnp.float32)
    ids = jnp.concatenate(
        [lower_junction.astype(jnp.float32), upper_junction.astype(jnp.float32), lanes]
    )[None]
    pad = jnp.zeros((-(2 * members + 1) % 8, width), jnp.float32)
    terms = all_basins(jnp.concatenate([push_all, upward_all, ids, pad]))
    lower_all = terms[:, 2 * members, :members].reshape(-1).astype(jnp.int32)
    upper_all = terms[:, 2 * members, members : 2 * members].reshape(-1).astype(jnp.int32)

    def meeting(ids_here, ids_all):
        return (ids_here[:, None] == ids_all[None, :]).astype(jnp.float32)

    into_head = meeting(upper_junction, lower_all)
    into_tail = meeting(lower_junction, upper_all)

    plane = lax.dynamic_slice_in_dim(
        jnp.stack([upper_all, lower_all]).reshape(2, zs, xs, members), z, 1, 1
    )[:, 0]
    plane = lax.dynamic_slice_in_dim(plane, c * half, half, 2)
    wanted = jnp.transpose(plane, (1, 0, 2))
    basin, place = wanted // owned, wanted % owned
    here = (basin % xs == x).astype(jnp.int32)
    rows = (basin // xs) * owned + place
    picked = pick(table, rows.reshape(-1), here.reshape(-1))
    picked = picked.reshape(rows.shape + table.shape[1:])
    arrived = lax.all_to_all(picked, "x", 0, 0, tiled=False).sum(0)
    ends_of = lax.all_gather(arrived, "y")
    tiles = jnp.transpose(ends_of[:, :, :, :piece], (1, 2, 0, 3, 4)).reshape(2, half, width, width)
    head_inv, tail_inv = tiles[0], tiles[1]
    head_residual, tail_cotangent = ends_of[0, 0, :, piece], ends_of[0, 1, :, piece + 1]

    down = product(schur, head_inv)
    up = product(tail_inv, schur)
    push_base = push + applied(down, head_residual)
    up_base = upward + applied_transposed(up, tail_cotangent)
    both = lax.all_gather(jnp.stack([packed(down, push_base), packed(up, up_base)]), "c")
    both = jnp.concatenate([both[0], both[1]], axis=1)
    down_all, push_base = both[0, :, :width], both[0, :, width]
    up_all, up_base = both[1, :, :width], both[1, :, width]

    def split(gathered):
        return (
            gathered[:, :members].reshape(-1, width),
            gathered[:, members : 2 * members].reshape(-1, width),
        )

    for sweep in range(1, SWEEPS):
        t_all, a_all = split(terms)
        inflow = jnp.dot(into_head, t_all, precision=precise)
        outflow = jnp.dot(into_tail, a_all, precision=precise)
        t = push_base + applied(down_all, inflow)
        a = up_base + applied_transposed(up_all, outflow)
        pad = jnp.zeros((-2 * members % 8, width), jnp.float32)
        terms = all_basins(jnp.concatenate([t, a, pad]))
    t_all, a_all = split(terms)

    owned_ids = (z * xs + x) * owned + jnp.arange(owned, dtype=jnp.int32)
    sections = applied(
        junction_inv,
        junction_residual + jnp.dot(meeting(owned_ids, lower_all), t_all, precision=precise),
    )
    adjoint = junction_cotangent + jnp.dot(
        meeting(owned_ids, upper_all), a_all, precision=precise
    )

    head = applied(head_inv, head_residual + jnp.dot(mine(into_head), t_all, precision=precise))
    relief = applied_transposed(
        tail_inv, tail_cotangent + jnp.dot(mine(into_tail), a_all, precision=precise)
    )
    enter = applied(before, head) + before_vector
    leave = applied_transposed(after, relief) + after_vector
    shared = lax.all_gather(jnp.stack([enter, leave]), "c")
    enter = jnp.concatenate([shared[0, 0], shared[1, 0]])
    leave = jnp.concatenate([shared[0, 1], shared[1, 1]])
    enter = jnp.where(c == 1, applied(pair[0, :, :width], enter) + pair[0, :, width], enter)
    leave = jnp.where(
        c == 0, applied_transposed(pair[1, :, :width], leave) + pair[1, :, width + 1], leave
    )

    cell_rows = []
    for number in range(blocks):
        enter = applied(multiplier[:, number], enter) + forced[:, number]
        cell_rows.append(enter)
    cell_update = jnp.stack(cell_rows, axis=1)
    carried = cell_cotangent[:, blocks - 1] + leave
    collected = [carried]
    for number in range(blocks - 2, -1, -1):
        carried = cell_cotangent[:, number] + applied_transposed(multiplier[:, number + 1], carried)
        collected.append(carried)
    cell_adjoint = jnp.stack(collected[::-1], axis=1)
    return (cell_update, sections, cell_adjoint, adjoint)


def solution(mesh):
    basins = mesh.shape["basin"]
    grid = Mesh(mesh.devices.reshape(basins // 4, 4, 4, 2), ("z", "x", "y", "c"))
    b, r = ("z", "x"), ("y", "c")
    return jax.shard_map(
        shards,
        mesh=grid,
        in_specs=(
            P(b, r, None),
            P(b, r, None, None),
            P(b, r, None, None),
            P(b, None, None),
            P(b, None, None),
            P(b, None),
            P(b),
            P(b),
            P(b, r, None),
            P(b, None),
        ),
        out_specs=(P(b, r, None), P(b, None), P(b, r, None), P(b, None)),
        check_vma=False,
    )
```

time: 1940 us -> 276 us (0.14)
  the two profiles are of different devices: /device:TPU:8 before, /device:TPU:1 now
where the time goes in v1:
time: 276 us; the launch traced here: 275 us
  blocking collectives  103 us (37%)
  matrix products  47 us (17%)
  local copies, waits for them, and re-layouts  36.2 us (13%)
  waiting for transfers between devices  35.3 us (13%)
  starting transfers between devices  30.5 us (11%)
  between operations  15.4 us (6%)
  other arithmetic  5.44 us (2%)
    all_to_all x3, blocking collectives, everyone(): return lax.all_to_all(spread, axis, 0, 0, tiled=False)  48.8 us
    all_to_all x5, waiting for transfers between devices, everyone(): return lax.all_to_all(spread, axis, 0, 0, tiled=False)  35.2 us
    all_to_all x5, starting transfers between devices, everyone(): return lax.all_to_all(spread, axis, 0, 0, tiled=False)  26.2 us
    dot_general x18, matrix products, applied(): return jnp.einsum('sij,sj->si', matrix, vector, precision=precise)  15.2 us
    all_gather x1, blocking collectives, shards(): chips = lax.all_gather(packed(chip_map, chip_vector, chip_back), 'y')  11.9 us
    dot_general x17, matrix products, applied_transposed(): return jnp.einsum('sji,sj->si', matrix, vector, precision=precise)  11.1 us
    all_gather x1, blocking collectives, shards(): lax.all_gather(jnp.stack([packed(down, push_base), packed(up, up_base)]),...  10.9 us
    all_gather x1, blocking collectives, shards(): ends_of = lax.all_gather(arrived, 'y')  9.96 us
  transfers between devices with their start and end apart: 7, of which 6 were waited for; matrix products, arithmetic and copies ran while one was open for 14% of the time, Pallas kernels for 0%

profile of v1, /device:TPU:1, one launch (start us, length us, event | category | flops | bytes accessed | tf_op | source)
XLA Modules:
  0.0 274.8 jit_solution(17356280630229654390)
XLA Ops:
  8.7 0.9 constant_dynamic-slice_fusion.2
  10.4 2.7 fusion.59
  13.1 1.3 fusion.209
  18.4 8.9 %all-gather = f32[12,136,128]{2,1,0:T(8,128)S(1)} all-gather(f32[6,136,128]{2,1,0:T(8,128)S(1)} %pad_maximum_fusion), channel_id=2, replica_groups=mesh['z'=16,'x'=4,'y'=4,'c'=2] {'c'}, dimensions={0}, use_global_device_ids=true | all-gather | bytes 1253376 | tf_op jit(solution)/shard_map/all_gather | solution.py:101
  27.3 1.0 fusion.201
  28.4 1.3 fusion.28
  29.7 1.2 fusion.24
  31.7 1.4 fusion.26
  33.3 11.9 %all-gather.1 = f32[12,136,128]{2,1,0:T(8,128)S(1)} all-gather(f32[3,136,128]{2,1,0:T(8,128)S(1)} %maximum_maximum_fusion), channel_id=3, replica_groups=mesh['z'=16,'x'=4,'y'=4,'c'=2] {'y'}, dimensions={0}, use_global_device_ids=true | all-gather | bytes 1044480 | tf_op jit(solution)/shard_map/all_gather | solution.py:108
  49.4 4.5 %all-gather.2 = f32[4,3,128]{2,1,0:T(4,128)S(1)} all-gather(f32[2,3,128]{2,1,0:T(4,128)S(1)} %pad_maximum_fusion.6), channel_id=4, replica_groups=mesh['z'=16,'x'=4,'y'=4,'c'=2] {'c'}, dimensions={0}, use_global_device_ids=true | all-gather | bytes 9216 | tf_op jit(solution)/shard_map/all_gather | solution.py:130
  54.8 9.2 %all-to-all-start = ((f32[16,16,128]{2,1,0:T(8,128)}), f32[16,16,128]{2,1,0:T(8,128)S(1)}, u32[]{:S(2)}, u32[]{:S(2)}) async-start(f32[16,16,128]{2,1,0:T(8,128)} %broadcast_in_dim.48), calls=%async_computation | async-start | bytes 262144 | tf_op jit(solution)/shard_map/all_to_all | solution.py:28
  65.2 1.3 fusion.31
  67.5 9.3 %all-to-all-done = f32[16,16,128]{2,1,0:T(8,128)S(1)} async-done(((f32[16,16,128]{2,1,0:T(8,128)}), f32[16,16,128]{2,1,0:T(8,128)S(1)}, u32[]{:S(2)}, u32[]{:S(2)}) %all-to-all-start) | async-done | bytes 131104 | tf_op jit(solution)/shard_map/all_to_all | solution.py:28
  76.8 0.9 broadcast_in_dim.49
  77.6 4.1 %all-to-all-start.1 = ((f32[4,16,16,128]{3,2,1,0:T(8,128)}), f32[4,16,16,128]{3,2,1,0:T(8,128)}, u32[]{:S(2)}, u32[]{:S(2)}) async-start(f32[4,16,16,128]{3,2,1,0:T(8,128)} %broadcast_in_dim.49), calls=%async_computation.1 | async-start | bytes 1048576 | tf_op jit(solution)/shard_map/all_to_all | solution.py:28
  82.8 1.0 fusion.45
  83.9 4.9 %all-to-all-done.1 = f32[4,16,16,128]{3,2,1,0:T(8,128)} async-done(((f32[4,16,16,128]{3,2,1,0:T(8,128)}), f32[4,16,16,128]{3,2,1,0:T(8,128)}, u32[]{:S(2)}, u32[]{:S(2)}) %all-to-all-start.1) | async-done | bytes 524320 | tf_op jit(solution)/shard_map/all_to_all | solution.py:28
  88.8 1.1 copy.174
  89.9 0.8 copy-done.6
  91.2 1.2 slice_convert_fusion.1
  94.4 2.4 shard_map.129
  96.9 4.3 %all-to-all-start.2 = ((f32[4,2,3,40,128]{4,3,2,1,0:T(8,128)}), f32[4,2,3,40,128]{4,3,2,1,0:T(8,128)}, u32[]{:S(2)}, u32[]{:S(2)}) async-start(f32[4,2,3,40,128]{4,3,2,1,0:T(8,128)} %bitcast.578), calls=%async_computation.2 | async-start | bytes 983040 | tf_op jit(solution)/shard_map/all_to_all | solution.py:159
  101.2 1.9 fusion.205
  103.1 1.6 reshape.146
  105.4 1.1 convolution_bitcast_fusion.5
  106.6 1.1 convolution_bitcast_fusion.4
  107.8 1.1 reduce_sum.9
  108.9 10.0 %all-gather.4 = f32[8,3,40,128]{3,2,1,0:T(8,128)S(1)} all-gather(f32[2,3,40,128]{3,2,1,0:T(8,128)S(1)} %reduce_sum.9), channel_id=6, replica_groups=mesh['z'=16,'x'=4,'y'=4,'c'=2] {'y'}, dimensions={0}, use_global_device_ids=true | all-gather | bytes 614400 | tf_op jit(solution)/shard_map/all_gather | solution.py:160
  121.5 10.9 %all-gather.5 = f32[4,3,136,128]{3,2,1,0:T(8,128)S(1)} all-gather(f32[2,3,136,128]{3,2,1,0:T(8,128)S(1)} %pad_maximum_fusion.1), channel_id=7, replica_groups=mesh['z'=16,'x'=4,'y'=4,'c'=2] {'c'}, dimensions={0}, use_global_device_ids=true | all-gather | bytes 1253376 | tf_op jit(solution)/shard_map/all_gather | solution.py:169
  133.9 19.5 %all_to_all.45 = f32[16,16,128]{2,1,0:T(8,128)S(1)} all-to-all(f32[16,16,128]{2,1,0:T(8,128)S(1)} %broadcast_in_dim.106), channel_id=1, replica_groups=mesh['z'=16,'x'=4,'y'=4,'c'=2] {'z'}, dimensions={0} | all-to-all | bytes 262144 | tf_op jit(solution)/shard_map/all_to_all | solution.py:28
  153.5 9.3 %all_to_all.46 = f32[4,16,16,128]{3,2,1,0:T(8,128)S(1)} all-to-all(f32[4,16,16,128]{3,2,1,0:T(8,128)S(1)} %broadcast_in_dim.107), channel_id=1, replica_groups=mesh['z'=16,'x'=4,'y'=4,'c'=2] {'x'}, dimensions={0} | all-to-all | bytes 1048576 | tf_op jit(solution)/shard_map/all_to_all | solution.py:28
  162.9 0.8 fusion.204
  163.7 1.7 reshape.149
  165.4 1.1 convolution_bitcast_fusion.3
  166.5 1.7 fusion.121
  168.3 1.7 reshape.150
  170.0 1.1 convolution_bitcast_fusion.2
  171.1 1.4 fusion.119
  172.6 20.0 %all_to_all.47 = f32[16,16,128]{2,1,0:T(8,128)S(1)} all-to-all(f32[16,16,128]{2,1,0:T(8,128)S(1)} %broadcast_in_dim.108), channel_id=1, replica_groups=mesh['z'=16,'x'=4,'y'=4,'c'=2] {'z'}, dimensions={0} | all-to-all | bytes 262144 | tf_op jit(solution)/shard_map/all_to_all | solution.py:28
  192.6 0.8 broadcast_in_dim.109
  193.5 4.1 %all-to-all-start.6 = ((f32[4,16,16,128]{3,2,1,0:T(8,128)}), f32[4,16,16,128]{3,2,1,0:T(8,128)}, u32[]{:S(2)}, u32[]{:S(2)}) async-start(f32[4,16,16,128]{3,2,1,0:T(8,128)} %broadcast_in_dim.109), calls=%async_computation.6 | async-start | bytes 1048576 | tf_op jit(solution)/shard_map/all_to_all | solution.py:28
  198.3 1.3 fusion.198
  199.6 5.0 %all-to-all-done.6 = f32[4,16,16,128]{3,2,1,0:T(8,128)} async-done(((f32[4,16,16,128]{3,2,1,0:T(8,128)}), f32[4,16,16,128]{3,2,1,0:T(8,128)}, u32[]{:S(2)}, u32[]{:S(2)}) %all-to-all-start.6) | async-done | bytes 524320 | tf_op jit(solution)/shard_map/all_to_all | solution.py:28
  204.6 1.1 copy.192
  205.7 0.8 fusion.203
  206.6 1.7 reshape.152
  208.2 1.1 convolution_bitcast_fusion.1
  209.4 1.7 fusion.117
  211.1 1.7 reshape.153
  212.8 1.1 convolution_bitcast_fusion
  213.9 1.4 fusion.115
  216.2 5.3 %all-to-all-start.7 = ((f32[16,16,128]{2,1,0:T(8,128)}), f32[16,16,128]{2,1,0:T(8,128)S(1)}, u32[]{:S(2)}, u32[]{:S(2)}) async-start(f32[16,16,128]{2,1,0:T(8,128)} %broadcast_in_dim.110), calls=%async_computation.7 | async-start | bytes 262144 | tf_op jit(solution)/shard_map/all_to_all | solution.py:28
  222.3 1.9 convolution_select_fusion
  224.2 9.2 %all-to-all-done.7 = f32[16,16,128]{2,1,0:T(8,128)S(1)} async-done(((f32[16,16,128]{2,1,0:T(8,128)}), f32[16,16,128]{2,1,0:T(8,128)S(1)}, u32[]{:S(2)}, u32[]{:S(2)}) %all-to-all-start.7) | async-done | bytes 131104 | tf_op jit(solution)/shard_map/all_to_all | solution.py:28
  233.4 0.8 broadcast_in_dim.111
  234.3 3.5 %all-to-all-start.8 = ((f32[4,16,16,128]{3,2,1,0:T(8,128)}), f32[4,16,16,128]{3,2,1,0:T(8,128)S(1)}, u32[]{:S(2)}, u32[]{:S(2)}) async-start(f32[4,16,16,128]{3,2,1,0:T(8,128)} %broadcast_in_dim.111), calls=%async_computation.8 | async-start | bytes 1048576 | tf_op jit(solution)/shard_map/all_to_all | solution.py:28
  237.9 6.7 %all-to-all-done.8 = f32[4,16,16,128]{3,2,1,0:T(8,128)S(1)} async-done(((f32[4,16,16,128]{3,2,1,0:T(8,128)}), f32[4,16,16,128]{3,2,1,0:T(8,128)S(1)}, u32[]{:S(2)}, u32[]{:S(2)}) %all-to-all-start.8) | async-done | bytes 524320 | tf_op jit(solution)/shard_map/all_to_all | solution.py:28
  246.4 1.8 fusion.109
  248.2 1.3 fusion.169
  250.3 1.0 reshape.156
  251.2 0.8 convolution_add_fusion
  252.3 1.2 fusion.167
  253.5 1.3 fusion.20
  254.9 7.4 %all-gather.6 = f32[4,3,128]{2,1,0:T(4,128)S(1)} all-gather(f32[2,3,128]{2,1,0:T(4,128)S(1)} %pad_maximum_fusion.7), channel_id=8, replica_groups=mesh['z'=16,'x'=4,'y'=4,'c'=2] {'c'}, dimensions={0}, use_global_device_ids=true | all-gather | bytes 9216 | tf_op jit(solution)/shard_map/all_gather | solution.py:205
  (279 shorter events, 33.1 us)
Async XLA Ops:
  7.2 3.2 %copy-start = (f32[6,3,128,128]{3,2,1,0:T(8,128)S(1)}, f32[6,3,128,128]{3,2,1,0:T(8,128)}, u32[]{:S(2)}) copy-start(f32[6,3,128,128]{3,2,1,0:T(8,128)} %param.11) | copy-start | bytes 3538948
  7.2 5.9 %copy-start.56 = (f32[6,3,128]{2,1,0:T(4,128)S(1)}, f32[6,3,128]{2,1,0:T(4,128)}, u32[]{:S(2)}) copy-start(f32[6,3,128]{2,1,0:T(4,128)} %param.18) | copy-start | bytes 27652
  7.2 87.3 %all-gather.9.cloned.1.call-start = ((), (), s32[]{:S(2)}) async-start(), calls=%async_computation.9 | async-start | bytes 2088960 | tf_op jit(solution)/shard_map/all_gather | solution.py:84
  10.3 2.8 %copy-start.12 = (f32[6,3,128,128]{3,2,1,0:T(8,128)S(1)}, f32[6,3,128,128]{3,2,1,0:T(8,128)}, u32[]{:S(2)}) copy-start(f32[6,3,128,128]{3,2,1,0:T(8,128)} %param.12) | copy-start | bytes 3538948
  27.3 5.7 %copy-start.3 = (f32[12,136,128]{2,1,0:T(8,128)}, f32[12,136,128]{2,1,0:T(8,128)S(1)}, u32[]{:S(2)}) copy-start(f32[12,136,128]{2,1,0:T(8,128)S(1)} %all-gather) | copy-start | bytes 2506756
  30.9 14.6 %copy-start.53 = (s32[6]{0:T(128)S(1)}, s32[6]{0:T(128)}, u32[]{:S(2)}) copy-start(s32[6]{0:T(128)} %param.16) | copy-start | bytes 76
  30.9 14.7 %copy-start.50 = (s32[6]{0:T(128)S(1)}, s32[6]{0:T(128)}, u32[]{:S(2)}) copy-start(s32[6]{0:T(128)} %param.17) | copy-start | bytes 76
  33.1 14.4 %copy-start.13 = (f32[6,128,128]{2,1,0:T(8,128)S(1)}, f32[6,128,128]{2,1,0:T(8,128)}, u32[]{:S(2)}) copy-start(f32[6,128,128]{2,1,0:T(8,128)} %param.13) | copy-start | bytes 1179652
  45.5 3.3 %copy-start.20 = (f32[3,1,128]{2,1,0:T(1,128)}, f32[3,1,128]{2,1,0:T(1,128)S(1)}, u32[]{:S(2)}) copy-start(f32[3,1,128]{2,1,0:T(1,128)S(1)} %fusion.32) | copy-start | bytes 4612
  45.6 0.6 copy-start.34
  45.6 1.0 copy-start.44
  45.6 1.8 copy-start.42
  45.6 8.3 %copy-start.36 = (f32[1,3,1,128]{3,2,1,0:T(1,128)}, f32[1,3,1,128]{3,2,1,0:T(1,128)S(1)}, u32[]{:S(2)}) copy-start(f32[1,3,1,128]{3,2,1,0:T(1,128)S(1)} %get-tuple-element.39) | copy-start | bytes 4612
  45.6 8.3 %copy-start.38 = (f32[1,3,1,128]{3,2,1,0:T(1,128)}, f32[1,3,1,128]{3,2,1,0:T(1,128)S(1)}, u32[]{:S(2)}) copy-start(f32[1,3,1,128]{3,2,1,0:T(1,128)S(1)} %get-tuple-element.43) | copy-start | bytes 4612
  45.6 8.3 %copy-start.40 = (f32[1,3,1,128]{3,2,1,0:T(1,128)}, f32[1,3,1,128]{3,2,1,0:T(1,128)S(1)}, u32[]{:S(2)}) copy-start(f32[1,3,1,128]{3,2,1,0:T(1,128)S(1)} %get-tuple-element.45) | copy-start | bytes 4612
  45.6 8.3 %copy-start.46 = (f32[1,3,1,128]{3,2,1,0:T(1,128)}, f32[1,3,1,128]{3,2,1,0:T(1,128)S(1)}, u32[]{:S(2)}) copy-start(f32[1,3,1,128]{3,2,1,0:T(1,128)S(1)} %get-tuple-element.44) | copy-start | bytes 4612
  46.5 1.4 copy-start.26
  47.0 7.0 %copy-start.28 = (f32[3,1,128]{2,1,0:T(1,128)}, f32[3,1,128]{2,1,0:T(1,128)S(1)}, u32[]{:S(2)}) copy-start(f32[3,1,128]{2,1,0:T(1,128)S(1)} %fusion.40) | copy-start | bytes 4612
  47.9 6.1 %copy-start.30 = (f32[3,1,128]{2,1,0:T(1,128)}, f32[3,1,128]{2,1,0:T(1,128)S(1)}, u32[]{:S(2)}) copy-start(f32[3,1,128]{2,1,0:T(1,128)S(1)} %fusion.36) | copy-start | bytes 4612
  48.2 29.4 %copy-start.22 = (f32[3,1,128]{2,1,0:T(1,128)}, f32[3,1,128]{2,1,0:T(1,128)S(1)}, u32[]{:S(2)}) copy-start(f32[3,1,128]{2,1,0:T(1,128)S(1)} %fusion.39) | copy-start | bytes 4612
  48.5 0.6 copy-start.24
  54.8 22.0 %all-to-all-start = ((f32[16,16,128]{2,1,0:T(8,128)}), f32[16,16,128]{2,1,0:T(8,128)S(1)}, u32[]{:S(2)}, u32[]{:S(2)}) async-start(f32[16,16,128]{2,1,0:T(8,128)} %broadcast_in_dim.48), calls=%async_computation | async-start | bytes 262144 | tf_op jit(solution)/shard_map/all_to_all | solution.py:28
  66.4 0.7 copy-start.8
  67.5 16.4 %copy-start.9 = (f32[3,128,128]{2,1,0:T(8,128)}, f32[3,128,128]{2,1,0:T(8,128)S(1)}, u32[]{:S(2)}) copy-start(f32[3,128,128]{2,1,0:T(8,128)S(1)} %fusion.38) | copy-start | bytes 589828
  77.6 11.1 %all-to-all-start.1 = ((f32[4,16,16,128]{3,2,1,0:T(8,128)}), f32[4,16,16,128]{3,2,1,0:T(8,128)}, u32[]{:S(2)}, u32[]{:S(2)}) async-start(f32[4,16,16,128]{3,2,1,0:T(8,128)} %broadcast_in_dim.49), calls=%async_computation.1 | async-start | bytes 1048576 | tf_op jit(solution)/shard_map/all_to_all | solution.py:28
  82.1 0.7 copy-start.10
  89.9 0.8 copy-start.6
  96.9 11.0 %all-to-all-start.2 = ((f32[4,2,3,40,128]{4,3,2,1,0:T(8,128)}), f32[4,2,3,40,128]{4,3,2,1,0:T(8,128)}, u32[]{:S(2)}, u32[]{:S(2)}) async-start(f32[4,2,3,40,128]{4,3,2,1,0:T(8,128)} %bitcast.578), calls=%async_computation.2 | async-start | bytes 983040 | tf_op jit(solution)/shard_map/all_to_all | solution.py:159
  101.2 4.2 %copy-start.54 = (s32[6]{0:T(128)S(1)}, s32[6]{0:T(128)}, u32[]{:S(2)}) copy-start(s32[6]{0:T(128)} %param.16) | copy-start | bytes 76
  101.2 5.4 %copy-start.51 = (s32[6]{0:T(128)S(1)}, s32[6]{0:T(128)}, u32[]{:S(2)}) copy-start(s32[6]{0:T(128)} %param.17) | copy-start | bytes 76
  108.9 10.2 %copy-start.11 = (f32[3,128,128]{2,1,0:T(8,128)S(1)}, f32[3,128,128]{2,1,0:T(8,128)}, u32[]{:S(2)}) copy-start(f32[3,128,128]{2,1,0:T(8,128)} %fusion.45) | copy-start | bytes 589828
  118.9 0.9 copy-start.31
  119.0 2.3 copy-start.33
  119.0 2.3 copy-start.47
  119.0 2.3 copy-start.58
  119.9 0.7 copy-start.7
  132.5 0.8 copy-start.1
  132.5 0.9 copy-start.2
  132.5 1.3 copy-start.57
  132.5 30.3 %copy-start.5 = (f32[6,128,128]{2,1,0:T(8,128)}, f32[6,128,128]{2,1,0:T(8,128)S(1)}, u32[]{:S(2)}) copy-start(f32[6,128,128]{2,1,0:T(8,128)S(1)} %fusion.6) | copy-start | bytes 1179652
  193.5 11.1 %all-to-all-start.6 = ((f32[4,16,16,128]{3,2,1,0:T(8,128)}), f32[4,16,16,128]{3,2,1,0:T(8,128)}, u32[]{:S(2)}, u32[]{:S(2)}) async-start(f32[4,16,16,128]{3,2,1,0:T(8,128)} %broadcast_in_dim.109), calls=%async_computation.6 | async-start | bytes 1048576 | tf_op jit(solution)/shard_map/all_to_all | solution.py:28
  216.2 17.3 %all-to-all-start.7 = ((f32[16,16,128]{2,1,0:T(8,128)}), f32[16,16,128]{2,1,0:T(8,128)S(1)}, u32[]{:S(2)}, u32[]{:S(2)}) async-start(f32[16,16,128]{2,1,0:T(8,128)} %broadcast_in_dim.110), calls=%async_computation.7 | async-start | bytes 262144 | tf_op jit(solution)/shard_map/all_to_all | solution.py:28
  224.2 13.6 %copy-start.52 = (s32[6]{0:T(128)S(1)}, s32[6]{0:T(128)}, u32[]{:S(2)}) copy-start(s32[6]{0:T(128)} %param.17) | copy-start | bytes 76
  224.2 13.6 %copy-start.55 = (s32[6]{0:T(128)S(1)}, s32[6]{0:T(128)}, u32[]{:S(2)}) copy-start(s32[6]{0:T(128)} %param.16) | copy-start | bytes 76
  234.3 10.4 %all-to-all-start.8 = ((f32[4,16,16,128]{3,2,1,0:T(8,128)}), f32[4,16,16,128]{3,2,1,0:T(8,128)S(1)}, u32[]{:S(2)}, u32[]{:S(2)}) async-start(f32[4,16,16,128]{3,2,1,0:T(8,128)} %broadcast_in_dim.111), calls=%async_computation.8 | async-start | bytes 1048576 | tf_op jit(solution)/shard_map/all_to_all | solution.py:28
  237.9 7.6 %copy-start.17 = (f32[1,1,3,1,128]{4,3,2,1,0:T(1,128)S(1)}, f32[1,1,3,1,128]{4,3,2,1,0:T(1,128)}, u32[]{:S(2)}) copy-start(f32[1,1,3,1,128]{4,3,2,1,0:T(1,128)} %copy-done.16) | copy-start | bytes 4612
  244.7 1.4 copy-start.18
  244.7 1.4 copy-start.59
  244.7 4.9 %copy-start.27 = (f32[3,1,128]{2,1,0:T(1,128)S(1)}, f32[3,1,128]{2,1,0:T(1,128)}, u32[]{:S(2)}) copy-start(f32[3,1,128]{2,1,0:T(1,128)} %copy-done.26) | copy-start | bytes 4612
  244.7 4.9 %copy-start.29 = (f32[3,1,128]{2,1,0:T(1,128)S(1)}, f32[3,1,128]{2,1,0:T(1,128)}, u32[]{:S(2)}) copy-start(f32[3,1,128]{2,1,0:T(1,128)} %copy-done.28) | copy-start | bytes 4612
  244.7 4.9 %copy-start.35 = (f32[1,3,1,128]{3,2,1,0:T(1,128)S(1)}, f32[1,3,1,128]{3,2,1,0:T(1,128)}, u32[]{:S(2)}) copy-start(f32[1,3,1,128]{3,2,1,0:T(1,128)} %copy-done.34) | copy-start | bytes 4612
  244.7 4.9 %copy-start.43 = (f32[1,3,1,128]{3,2,1,0:T(1,128)S(1)}, f32[1,3,1,128]{3,2,1,0:T(1,128)}, u32[]{:S(2)}) copy-start(f32[1,3,1,128]{3,2,1,0:T(1,128)} %copy-done.42) | copy-start | bytes 4612
  244.8 4.9 %copy-start.45 = (f32[1,3,1,128]{3,2,1,0:T(1,128)S(1)}, f32[1,3,1,128]{3,2,1,0:T(1,128)}, u32[]{:S(2)}) copy-start(f32[1,3,1,128]{3,2,1,0:T(1,128)} %copy-done.44) | copy-start | bytes 4612
  245.5 5.7 %copy-start.19 = (f32[6,128]{1,0:T(8,128)S(1)}, f32[6,128]{1,0:T(8,128)}, u32[]{:S(2)}) copy-start(f32[6,128]{1,0:T(8,128)} %param.19) | copy-start | bytes 9220
  245.5 6.6 %copy-start.15 = (f32[1,1,3,1,128]{4,3,2,1,0:T(1,128)S(1)}, f32[1,1,3,1,128]{4,3,2,1,0:T(1,128)}, u32[]{:S(2)}) copy-start(f32[1,1,3,1,128]{4,3,2,1,0:T(1,128)} %copy-done.14) | copy-start | bytes 4612
  246.4 8.4 %copy-start.21 = (f32[3,1,128]{2,1,0:T(1,128)S(1)}, f32[3,1,128]{2,1,0:T(1,128)}, u32[]{:S(2)}) copy-start(f32[3,1,128]{2,1,0:T(1,128)} %copy-done.20) | copy-start | bytes 4612
  246.4 8.4 %copy-start.23 = (f32[3,1,128]{2,1,0:T(1,128)S(1)}, f32[3,1,128]{2,1,0:T(1,128)}, u32[]{:S(2)}) copy-start(f32[3,1,128]{2,1,0:T(1,128)} %copy-done.22) | copy-start | bytes 4612
  246.4 8.4 %copy-start.25 = (f32[3,1,128]{2,1,0:T(1,128)S(1)}, f32[3,1,128]{2,1,0:T(1,128)}, u32[]{:S(2)}) copy-start(f32[3,1,128]{2,1,0:T(1,128)} %copy-done.24) | copy-start | bytes 4612
  246.4 8.4 %copy-start.37 = (f32[1,3,1,128]{3,2,1,0:T(1,128)S(1)}, f32[1,3,1,128]{3,2,1,0:T(1,128)}, u32[]{:S(2)}) copy-start(f32[1,3,1,128]{3,2,1,0:T(1,128)} %copy-done.36) | copy-start | bytes 4612
  246.4 8.4 %copy-start.39 = (f32[1,3,1,128]{3,2,1,0:T(1,128)S(1)}, f32[1,3,1,128]{3,2,1,0:T(1,128)}, u32[]{:S(2)}) copy-start(f32[1,3,1,128]{3,2,1,0:T(1,128)} %copy-done.38) | copy-start | bytes 4612
  246.4 8.4 %copy-start.41 = (f32[1,3,1,128]{3,2,1,0:T(1,128)S(1)}, f32[1,3,1,128]{3,2,1,0:T(1,128)}, u32[]{:S(2)}) copy-start(f32[1,3,1,128]{3,2,1,0:T(1,128)} %copy-done.40) | copy-start | bytes 4612
  246.4 15.9 %copy-start.4 = (f32[12,136,128]{2,1,0:T(8,128)S(1)}, f32[12,136,128]{2,1,0:T(8,128)}, u32[]{:S(2)}) copy-start(f32[12,136,128]{2,1,0:T(8,128)} %copy-done.3) | copy-start | bytes 2506756
  249.6 13.2 %copy-start.48 = (f32[1,6,1,128]{3,2,1,0:T(1,128)S(1)}, f32[1,6,1,128]{3,2,1,0:T(1,128)}, u32[]{:S(2)}) copy-start(f32[1,6,1,128]{3,2,1,0:T(1,128)} %get-tuple-element.32) | copy-start | bytes 9220
  253.5 11.6 %copy-start.49 = (f32[1,6,1,128]{3,2,1,0:T(1,128)S(1)}, f32[1,6,1,128]{3,2,1,0:T(1,128)}, u32[]{:S(2)}) copy-start(f32[1,6,1,128]{3,2,1,0:T(1,128)} %get-tuple-element.33) | copy-start | bytes 9220
  (3 other events, 1.7 us)
Sparse Core Ops, SparseCore 0:
  10.4 72.7 all-gather.8

commit v2 on v0

v2 whole, which is shorter than its diff:
```python
import jax
import jax.numpy as jnp
from jax import lax
from jax.experimental import pallas as pl
from jax.experimental.pallas import tpu as pltpu
from jax.sharding import Mesh, PartitionSpec as P

SWEEPS = 4
WIDTH = 128
PACK = WIDTH + 8
F32 = jnp.float32

smem = pl.BlockSpec(memory_space=pltpu.SMEM)
vmem = pl.BlockSpec(memory_space=pltpu.VMEM)


def run(kernel, outs, *args, scalars=0):
    single = not isinstance(outs, list)
    shapes = [jax.ShapeDtypeStruct(o, F32) if isinstance(o, tuple) else o for o in ([outs] if single else outs)]
    result = pl.pallas_call(
        kernel,
        out_shape=shapes,
        in_specs=[smem] * scalars + [vmem] * (len(args) - scalars),
        out_specs=[vmem] * len(shapes),
        compiler_params=pltpu.CompilerParams(vmem_limit_bytes=40 * 1024 * 1024),
    )(*args)
    return result[0] if single else result


def two_parts(a):
    high = a.astype(jnp.bfloat16)
    return high, (a - high.astype(F32)).astype(jnp.bfloat16)


def dot(a, b, transposed=False):
    dims = (((1,), (1 if transposed else 0,)), ((), ()))
    return lax.dot_general(a, b, dims, preferred_element_type=F32)


def product(a, b):
    (ah, al), (bh, bl) = two_parts(a), two_parts(b)
    return dot(ah, bh) + (dot(ah, bl) + dot(al, bh))


def along(vector, matrix, transposed):
    vh, vl = two_parts(vector)
    mh, ml = two_parts(matrix)
    return dot(vh, mh, transposed) + (dot(vl, mh, transposed) + dot(vh, ml, transposed))


def applied(matrix, row):
    return along(row, matrix, True)


def applied_transposed(matrix, row):
    return along(row, matrix, False)


def table_kernel(inv_ref, residual_ref, cotangent_ref, out_ref):
    piece = out_ref.shape[1] - 8
    start = pl.multiple_of(lax.axis_index("y") * piece, 8)
    for k in range(inv_ref.shape[0]):
        out_ref[k, :piece] = inv_ref[k, pl.ds(start, piece)]
        out_ref[k, piece : piece + 1] = residual_ref[k : k + 1]
        out_ref[k, piece + 1 : piece + 2] = cotangent_ref[k : k + 1]
        out_ref[k, piece + 2 :] = jnp.zeros((6, WIDTH), F32)


def local_kernel(inv_ref, link_ref, residual_ref, cotangent_ref, mult_ref, forced_ref, out_ref):
    members, blocks = inv_ref.shape[:2]
    for s in range(members):
        m = []
        for i in range(blocks):
            m.append(product(inv_ref[s, i], link_ref[s, i]))
            mult_ref[s, i] = m[i]
        f = [applied(inv_ref[s, i], residual_ref[s, i : i + 1]) for i in range(blocks)]
        total, vector = m[0], f[0]
        forced_ref[s, 0:1] = f[0]
        for i in range(1, blocks):
            forced_ref[s, i : i + 1] = f[i]
            total = product(m[i], total)
            vector = applied(m[i], vector) + f[i]
        back = cotangent_ref[s, blocks - 1 : blocks]
        for i in range(blocks - 2, -1, -1):
            back = cotangent_ref[s, i : i + 1] + applied_transposed(m[i + 1], back)
        out_ref[s, :WIDTH] = total
        out_ref[s, WIDTH : WIDTH + 1] = vector
        out_ref[s, WIDTH + 1 : WIDTH + 2] = applied_transposed(m[0], back)
        out_ref[s, WIDTH + 2 :] = jnp.zeros((6, WIDTH), F32)


def pair_kernel(pair_ref, out_ref):
    half = out_ref.shape[0]
    first_s = lax.axis_index("c") * half
    for k in range(half):
        first, second = pair_ref[0, first_s + k], pair_ref[1, first_s + k]
        one, two = first[:WIDTH], second[:WIDTH]
        out_ref[k, :WIDTH] = product(two, one)
        out_ref[k, WIDTH : WIDTH + 1] = (
            applied(two, first[WIDTH : WIDTH + 1]) + second[WIDTH : WIDTH + 1]
        )
        out_ref[k, WIDTH + 1 : WIDTH + 2] = (
            applied_transposed(one, second[WIDTH + 1 : WIDTH + 2]) + first[WIDTH + 1 : WIDTH + 2]
        )
        out_ref[k, WIDTH + 2 :] = jnp.zeros((6, WIDTH), F32)


def chain_kernel(lower_ref, upper_ref, chips_ref, outlet_ref, schur_ref, before_ref, after_ref, rows_ref, spread_ref):
    chips, half = chips_ref.shape[:2]
    first_s = lax.axis_index("c") * half
    y = lax.axis_index("y")
    row = lax.broadcasted_iota(jnp.int32, (8, WIDTH), 0)
    lane = lax.broadcasted_iota(jnp.int32, (8, WIDTH), 1)
    eye = (
        lax.broadcasted_iota(jnp.int32, (WIDTH, WIDTH), 0)
        == lax.broadcasted_iota(jnp.int32, (WIDTH, WIDTH), 1)
    ).astype(F32)
    nothing = jnp.zeros((1, WIDTH), F32)
    ids = jnp.zeros((8, WIDTH), jnp.int32)
    payload = [nothing] * 8
    for k in range(half):
        ids = jnp.where(lane == k, lower_ref[first_s + k], ids)
        ids = jnp.where(lane == half + k, upper_ref[first_s + k], ids)
        maps = [chips_ref[i, k, :WIDTH] for i in range(chips)]
        before, before_row = eye, nothing
        reached, reached_row = maps[0], chips_ref[0, k, WIDTH : WIDTH + 1]
        for i in range(1, chips):
            before = jnp.where(y == i, reached, before)
            before_row = jnp.where(y == i, reached_row, before_row)
            if i < chips - 1:
                reached = product(maps[i], reached)
            reached_row = applied(maps[i], reached_row) + chips_ref[i, k, WIDTH : WIDTH + 1]
        outlet = outlet_ref[first_s + k]
        schur, after = outlet, outlet
        upward, after_row = nothing, nothing
        for i in range(chips - 1, -1, -1):
            after = jnp.where(y == i, schur, after)
            after_row = jnp.where(y == i, upward, after_row)
            schur = product(schur, maps[i])
            upward = applied_transposed(maps[i], upward) + chips_ref[i, k, WIDTH + 1 : WIDTH + 2]
        schur_ref[k] = schur
        before_ref[k] = before
        after_ref[k] = after
        rows_ref[k : k + 1] = before_row
        rows_ref[half + k : half + k + 1] = after_row
        payload[k] = applied(outlet, reached_row)
        payload[half + k] = upward
    rows_ref[2 * half :] = jnp.zeros((2, WIDTH), F32)
    full = jnp.where(row == 2 * half, ids.astype(F32), jnp.concatenate(payload))
    for i in range(spread_ref.shape[0]):
        spread_ref[i] = full


def pick_kernel(ids_ref, table_ref, out_ref):
    dests, tiles = out_ref.shape[:2]
    half = tiles // 2
    owned = 2 * half
    x = lax.axis_index("x")
    for d in range(dests):
        for k in range(tiles):
            junction = ids_ref[d, (k + half) % tiles]
            basin = lax.div(junction, owned)
            line = lax.div(basin, dests)
            at = line * owned + (junction - basin * owned)
            here = basin - line * dests == x
            out_ref[d, k] = jnp.where(here, table_ref[at], 0.0)


def merge_kernel(picked_ref, out_ref):
    total = picked_ref[0]
    for d in range(1, picked_ref.shape[0]):
        total = total + picked_ref[d]
    for i in range(out_ref.shape[0]):
        out_ref[i] = total


def rule(above, below, half):
    row = lax.broadcasted_iota(jnp.int32, (8, WIDTH), 0)
    return jnp.where(row < half, above, jnp.where(row < 2 * half, below, -2))


def gathered(ids, values, pattern, half):
    total = jnp.sum(jnp.where(ids == pattern[None], values, 0.0), axis=0)
    inflow, outflow = total[0:1], total[half : half + 1]
    for k in range(1, half):
        inflow = inflow + total[k : k + 1]
        outflow = outflow + total[half + k : half + k + 1]
    return inflow, outflow


def step(lower_ref, upper_ref, ids, values, tiles, schur_ref, ends, base, spread_ref):
    half = schur_ref.shape[0]
    first_s = lax.axis_index("c") * half
    payload = [jnp.zeros((1, WIDTH), F32)] * 8
    for k in range(half):
        pattern = rule(upper_ref[first_s + k], lower_ref[first_s + k], half)
        inflow, outflow = gathered(ids, values, pattern, half)
        head = applied(tiles[k], ends[k : k + 1] + inflow)
        relief = applied_transposed(tiles[half + k], ends[half + k : half + k + 1] + outflow)
        schur = schur_ref[k]
        payload[k] = base[k : k + 1] + applied(schur, head)
        payload[half + k] = base[half + k : half + k + 1] + applied_transposed(schur, relief)
    full = jnp.concatenate(payload)
    for i in range(spread_ref.shape[0]):
        spread_ref[i] = full


def first_step_kernel(
    lower_ref, upper_ref, terms_ref, ends_ref, schur_ref, base_ref, tiles_ref, ids_ref, rows_ref, spread_ref
):
    half = schur_ref.shape[0]
    piece = ends_ref.shape[2] - 8
    row = lax.broadcasted_iota(jnp.int32, (8, WIDTH), 0)
    lane = lax.broadcasted_iota(jnp.int32, (8, WIDTH), 1)
    values = terms_ref[...].reshape(-1, 8, WIDTH)
    chosen = jnp.where((row == lane) & (row < 2 * half), values[:, 2 * half : 2 * half + 1], 0.0)
    ids = jnp.sum(chosen, axis=2, keepdims=True).astype(jnp.int32)
    ids = jnp.broadcast_to(ids, values.shape)
    ids_ref[...] = ids
    for k in range(2 * half):
        for i in range(ends_ref.shape[0]):
            tiles_ref[k, i * piece : (i + 1) * piece] = ends_ref[i, k, :piece]
    ends = [ends_ref[0, k, piece : piece + 1] for k in range(half)]
    ends += [ends_ref[0, half + k, piece + 1 : piece + 2] for k in range(half)]
    ends = jnp.concatenate(ends + [jnp.zeros((2, WIDTH), F32)])
    rows_ref[...] = ends
    tiles = [tiles_ref[k] for k in range(2 * half)]
    step(lower_ref, upper_ref, ids, values, tiles, schur_ref, ends, base_ref[0], spread_ref)


def step_kernel(
    lower_ref, upper_ref, terms_ref, ids_ref, tiles_ref, schur_ref, rows_ref, base_ref, spread_ref
):
    values = terms_ref[...].reshape(-1, 8, WIDTH)
    tiles = [tiles_ref[k] for k in range(tiles_ref.shape[0])]
    step(lower_ref, upper_ref, ids_ref[...], values, tiles, schur_ref, rows_ref[...], base_ref[0], spread_ref)


def last_kernel(
    lower_ref, upper_ref, terms_ref, ids_ref, tiles_ref, rows_ref, before_ref, after_ref, passing_ref,
    inv_ref, residual_ref, cotangent_ref, sections_ref, adjoint_ref, shared_ref,
):
    half = before_ref.shape[0]
    owned = inv_ref.shape[0]
    first_s = lax.axis_index("c") * half
    first_j = (lax.axis_index("z") * lax.axis_size("x") + lax.axis_index("x")) * owned
    values = terms_ref[...].reshape(-1, 8, WIDTH)
    ids = ids_ref[...]
    shared_ref[2 * half :] = jnp.zeros((2, WIDTH), F32)
    for k in range(half):
        pattern = rule(upper_ref[first_s + k], lower_ref[first_s + k], half)
        inflow, outflow = gathered(ids, values, pattern, half)
        head = applied(tiles_ref[k], rows_ref[k : k + 1] + inflow)
        relief = applied_transposed(
            tiles_ref[half + k], rows_ref[half + k : half + k + 1] + outflow
        )
        shared_ref[k : k + 1] = applied(before_ref[k], head) + passing_ref[k : k + 1]
        shared_ref[half + k : half + k + 1] = (
            applied_transposed(after_ref[k], relief) + passing_ref[half + k : half + k + 1]
        )
    for k in range(owned):
        inflow, outflow = gathered(ids, values, rule(first_j + k, first_j + k, half), half)
        sections_ref[k : k + 1] = applied(inv_ref[k], residual_ref[k : k + 1] + inflow)
        adjoint_ref[k : k + 1] = cotangent_ref[k : k + 1] + outflow


def cells_kernel(shared_ref, pair_ref, mult_ref, forced_ref, cotangent_ref, update_ref, adjoint_ref):
    members, blocks = mult_ref.shape[:2]
    half = members // 2
    c = lax.axis_index("c")
    for s in range(members):
        core, k = s // half, s % half
        enter = shared_ref[core, k : k + 1]
        leave = shared_ref[core, half + k : half + k + 1]
        other = pair_ref[1 - c, s]
        matrix = other[:WIDTH]
        further = applied(matrix, enter) + other[WIDTH : WIDTH + 1]
        nearer = applied_transposed(matrix, leave) + other[WIDTH + 1 : WIDTH + 2]
        enter = jnp.where(c == 1, further, enter)
        leave = jnp.where(c == 0, nearer, leave)
        for i in range(blocks):
            enter = applied(mult_ref[s, i], enter) + forced_ref[s, i : i + 1]
            update_ref[s, i : i + 1] = enter
        carried = cotangent_ref[s, blocks - 1 : blocks] + leave
        adjoint_ref[s, blocks - 1 : blocks] = carried
        for i in range(blocks - 2, -1, -1):
            carried = cotangent_ref[s, i : i + 1] + applied_transposed(mult_ref[s, i + 1], carried)
            adjoint_ref[s, i : i + 1] = carried


def swap(spread, axis):
    return lax.all_to_all(spread, axis, 0, 0, tiled=False)


def exchanged(spread):
    along_z = swap(spread, "z")
    sides = ("x", "c")
    return swap(jnp.broadcast_to(along_z[None], (lax.axis_size(sides),) + along_z.shape), sides)


def shards(
    reach_residual,
    chain_inv,
    chain_link,
    outlet_link,
    junction_inv,
    junction_residual,
    upper_junction,
    lower_junction,
    cell_cotangent,
    junction_cotangent,
):
    members, blocks, width = reach_residual.shape
    owned = junction_inv.shape[0]
    zs, xs, ys = lax.axis_size("z"), lax.axis_size("x"), lax.axis_size("y")
    half = members // 2
    piece = width // ys
    square = (width, width)
    lower, upper = lower_junction, upper_junction

    part = run(table_kernel, (owned, piece + 8, width), junction_inv, junction_residual, junction_cotangent)
    table = lax.all_gather(part, "z").reshape(zs * owned, piece + 8, width)

    multiplier, forced, local = run(
        local_kernel,
        [(members, blocks) + square, (members, blocks, width), (members, PACK, width)],
        chain_inv, chain_link, reach_residual, cell_cotangent,
    )
    pair = lax.all_gather(local, "c")
    chips = lax.all_gather(run(pair_kernel, (half, PACK, width), pair), "y")
    schur, before, after, passing, spread = run(
        chain_kernel,
        [(half,) + square, (half,) + square, (half,) + square, (8, width), (zs, 8, width)],
        lower, upper, chips, outlet_link, scalars=2,
    )
    terms = exchanged(spread)

    plane = lax.dynamic_slice(
        terms.reshape(xs, 2, zs, 8, width),
        (0, lax.axis_index("c"), lax.axis_index("z"), 2 * half, 0),
        (xs, 1, 1, 1, 2 * half),
    ).reshape(xs, 2 * half).astype(jnp.int32)
    picked = run(pick_kernel, (xs, 2 * half, piece + 8, width), plane, table, scalars=1)
    merged = run(merge_kernel, (ys, 2 * half, piece + 8, width), swap(picked, "x"))
    ends = swap(merged, "y")
    first = spread
    tiles, ids, rows, spread = run(
        first_step_kernel,
        [(2 * half,) + square, jax.ShapeDtypeStruct((zs * xs * 2, 8, width), jnp.int32), (8, width), (zs, 8, width)],
        lower, upper, terms, ends, schur, first, scalars=2,
    )
    terms = exchanged(spread)
    for sweep in range(2, SWEEPS):
        spread = run(
            step_kernel, (zs, 8, width), lower, upper, terms, ids, tiles, schur, rows, first, scalars=2
        )
        terms = exchanged(spread)
    sections, adjoint, shared = run(
        last_kernel,
        [(owned, width), (owned, width), (8, width)],
        lower, upper, terms, ids, tiles, rows, before, after, passing,
        junction_inv, junction_residual, junction_cotangent, scalars=2,
    )
    cell_update, cell_adjoint = run(
        cells_kernel,
        [(members, blocks, width), (members, blocks, width)],
        lax.all_gather(shared, "c"), pair, multiplier, forced, cell_cotangent,
    )
    return (cell_update, sections, cell_adjoint, adjoint)


def solution(mesh):
    basins = mesh.shape["basin"]
    grid = Mesh(mesh.devices.reshape(basins // 4, 4, 4, 2), ("z", "x", "y", "c"))
    b, r = ("z", "x"), ("y", "c")
    return jax.shard_map(
        shards,
        mesh=grid,
        in_specs=(
            P(b, r, None),
            P(b, r, None, None),
            P(b, r, None, None),
            P(b, None, None),
            P(b, None, None),
            P(b, None),
            P(b),
            P(b),
            P(b, r, None),
            P(b, None),
        ),
        out_specs=(P(b, r, None), P(b, None), P(b, r, None), P(b, None)),
        check_vma=False,
    )
```

time: 1940 us -> 228 us (0.12)
  the two profiles are of different devices: /device:TPU:8 before, /device:TPU:1 now
where the time goes in v2:
time: 228 us; the launch traced here: 227 us
  blocking collectives  165 us (72%)
  Pallas kernels  22.5 us (10%)
  between operations  14.2 us (6%)
  waiting for transfers between devices  9.52 us (4%)
  local copies, waits for them, and re-layouts  8.85 us (4%)
  starting transfers between devices  7.37 us (3%)
    all_to_all x9, blocking collectives, swap(): return lax.all_to_all(spread, axis, 0, 0, tiled=False)  142 us
    pallas_call x11, Pallas kernels, run(): pl.pallas_call(kernel, out_shape=shapes, in_specs=[smem] * scalars + [vme...  22.5 us
    all_gather x1, blocking collectives, shards(): chips = lax.all_gather(run(pair_kernel, (half, PACK, width), pair), 'y')  11.1 us
    all_to_all x1, waiting for transfers between devices, swap(): return lax.all_to_all(spread, axis, 0, 0, tiled=False)  9.48 us
    all_gather x1, blocking collectives, shards(): pair = lax.all_gather(local, 'c')  8.91 us
    unnamed x30, local copies, waits for them, and re-layouts  7.88 us
    all_to_all x1, starting transfers between devices, swap(): return lax.all_to_all(spread, axis, 0, 0, tiled=False)  7.34 us
  transfers between devices with their start and end apart: 2, of which 1 were waited for; matrix products, arithmetic and copies ran while one was open for 0% of the time, Pallas kernels for 4%

profile of v2, /device:TPU:1, one launch (start us, length us, event | category | flops | bytes accessed | tf_op | source)
XLA Modules:
  0.0 227.0 jit_solution(6163325642315028057)
XLA Ops:
  7.2 0.0 all-gather.6.cloned.1.call-start
  7.2 0.0 copy-start.1
  7.2 1.0 copy-done.1
  8.2 0.0 copy-start.8
  8.2 0.7 copy-done.8
  8.9 0.0 copy-start.10
  8.9 0.7 copy-done.10
  9.6 0.7 shard_map.132
  10.2 0.0 all-gather.6.cloned.1.call-update
  10.3 0.0 copy-start.3
  10.3 1.3 copy-done.3
  11.5 0.0 copy-start.4
  11.5 1.3 copy-done.4
  12.8 0.0 copy-start.6
  12.8 0.7 copy-done.6
  13.5 0.0 copy-start.14
  13.5 0.7 copy-done.14
  14.2 4.9 %shard_map.129 = (f32[6,3,128,128]{3,2,1,0:T(8,128)S(1)}, f32[6,3,128]{2,1,0:T(4,128)S(1)}, f32[6,136,128]{2,1,0:T(8,128)S(1)}) custom-call(f32[6,3,128,128]{3,2,1,0:T(8,128)S(1)} %copy-done.3, f32[6,3,128,128]{3,2,1,0:T(8,128)S(1)} %copy-done.4, f32[6,3,128]{2,1,0:T(4,128)S(1)} %copy-done.14, f32[6,3,128]{2,1,0:T(4,128)S(1)} %copy-done.6), custom_call_target="tpu_custom_call" | custom-call | tf_op jit(solution)/shard_map/pallas_call | solution.py:20
  19.1 8.9 %all-gather = f32[12,136,128]{2,1,0:T(8,128)S(1)} all-gather(f32[6,136,128]{2,1,0:T(8,128)S(1)} %get-tuple-element.21), channel_id=2, replica_groups=mesh['z'=16,'x'=4,'y'=4,'c'=2] {'c'}, dimensions={0}, use_global_device_ids=true | all-gather | bytes 1253376 | tf_op jit(solution)/shard_map/all_gather | solution.py:329
  28.0 0.0 copy-start.5
  28.0 0.0 copy-start.12
  28.0 0.0 copy-start.13
  28.0 0.4 shard_map.130
  28.4 11.1 %all-gather.1 = f32[12,136,128]{2,1,0:T(8,128)S(1)} all-gather(f32[3,136,128]{2,1,0:T(8,128)S(1)} %shard_map.130), channel_id=3, replica_groups=mesh['z'=16,'x'=4,'y'=4,'c'=2] {'y'}, dimensions={0}, use_global_device_ids=true | all-gather | bytes 1044480 | tf_op jit(solution)/shard_map/all_gather | solution.py:330
  39.5 0.0 copy-done.5
  39.5 0.0 copy-done.12
  39.5 0.0 copy-done.13
  39.6 3.6 %shard_map.131 = (f32[3,128,128]{2,1,0:T(8,128)S(1)}, f32[3,128,128]{2,1,0:T(8,128)S(1)}, f32[3,128,128]{2,1,0:T(8,128)S(1)}, f32[8,128]{1,0:T(8,128)S(1)}, f32[16,8,128]{2,1,0:T(8,128)S(1)}) custom-call(s32[6]{0:T(128)S(1)} %copy-done.12, s32[6]{0:T(128)S(1)} %copy-done.13, f32[4,3,136,128]{3,2,1,0:T(8,128)S(1)} %bitcast.9, f32[6,128,128]{2,1,0:T(8,128)S(1)} %copy-done.5), custom_call_target="tpu_custom_call" | custom-call | tf_op jit(solution)/shard_map/pallas_call | solution.py:20
  43.2 23.3 %all_to_all.50 = f32[16,8,128]{2,1,0:T(8,128)S(1)} all-to-all(f32[16,8,128]{2,1,0:T(8,128)S(1)} %get-tuple-element.22.base_ref), channel_id=1, replica_groups=mesh['z'=16,'x'=4,'y'=4,'c'=2] {'z'}, dimensions={0} | all-to-all | bytes 131072 | tf_op jit(solution)/shard_map/all_to_all | solution.py:292
  66.5 0.9 broadcast_in_dim.8
  67.4 7.3 %all-to-all-start.1 = ((f32[8,16,8,128]{3,2,1,0:T(8,128)}), f32[8,16,8,128]{3,2,1,0:T(8,128)S(1)}, u32[]{:S(2)}, u32[]{:S(2)}) async-start(f32[8,16,8,128]{3,2,1,0:T(8,128)} %broadcast_in_dim.8), calls=%async_computation.1 | async-start | bytes 1048576 | tf_op jit(solution)/shard_map/all_to_all | solution.py:292
  74.7 9.5 %all-to-all-done.1.terms_ref = f32[8,16,8,128]{3,2,1,0:T(8,128)S(1)} async-done(((f32[8,16,8,128]{3,2,1,0:T(8,128)}), f32[8,16,8,128]{3,2,1,0:T(8,128)S(1)}, u32[]{:S(2)}, u32[]{:S(2)}) %all-to-all-start.1) | async-done | bytes 524320 | tf_op jit(solution)/shard_map/all_to_all | solution.py:292
  84.2 0.0 all-gather.6.cloned.1.call-done.table_ref
  84.2 0.0 copy-start
  84.2 1.5 copy-done
  85.8 0.7 shard_map.133
  86.5 9.1 %all_to_all.51.picked_ref = f32[4,6,40,128]{3,2,1,0:T(8,128)S(1)} all-to-all(f32[4,6,40,128]{3,2,1,0:T(8,128)S(1)} %shard_map.133), channel_id=1, replica_groups=mesh['z'=16,'x'=4,'y'=4,'c'=2] {'x'}, dimensions={0} | all-to-all | bytes 983040 | tf_op jit(solution)/shard_map/all_to_all | solution.py:292
  95.7 11.1 %all_to_all.52.ends_ref = f32[4,6,40,128]{3,2,1,0:T(8,128)S(1)} all-to-all(f32[4,6,40,128]{3,2,1,0:T(8,128)S(1)} %shard_map.134), channel_id=1, replica_groups=mesh['z'=16,'x'=4,'y'=4,'c'=2] {'y'}, dimensions={0} | all-to-all | bytes 983040 | tf_op jit(solution)/shard_map/all_to_all | solution.py:292
  106.8 1.7 shard_map.135
  108.5 16.2 %all_to_all.53 = f32[16,8,128]{2,1,0:T(8,128)S(1)} all-to-all(f32[16,8,128]{2,1,0:T(8,128)S(1)} %get-tuple-element.24), channel_id=1, replica_groups=mesh['z'=16,'x'=4,'y'=4,'c'=2] {'z'}, dimensions={0} | all-to-all | bytes 131072 | tf_op jit(solution)/shard_map/all_to_all | solution.py:292
  124.8 25.6 %all_to_all.54.terms_ref = f32[8,16,8,128]{3,2,1,0:T(8,128)S(1)} all-to-all(f32[8,16,8,128]{3,2,1,0:T(8,128)S(1)} %broadcast_in_dim.9), channel_id=1, replica_groups=mesh['z'=16,'x'=4,'y'=4,'c'=2] {'x','c'}, dimensions={0} | all-to-all | bytes 1048576 | tf_op jit(solution)/shard_map/all_to_all | solution.py:292
  150.3 1.6 shard_map.136
  151.9 14.2 %all_to_all.55 = f32[16,8,128]{2,1,0:T(8,128)S(1)} all-to-all(f32[16,8,128]{2,1,0:T(8,128)S(1)} %shard_map.136), channel_id=1, replica_groups=mesh['z'=16,'x'=4,'y'=4,'c'=2] {'z'}, dimensions={0} | all-to-all | bytes 131072 | tf_op jit(solution)/shard_map/all_to_all | solution.py:292
  166.2 14.0 %all_to_all.56.terms_ref = f32[8,16,8,128]{3,2,1,0:T(8,128)S(1)} all-to-all(f32[8,16,8,128]{3,2,1,0:T(8,128)S(1)} %broadcast_in_dim.10), channel_id=1, replica_groups=mesh['z'=16,'x'=4,'y'=4,'c'=2] {'x','c'}, dimensions={0} | all-to-all | bytes 1048576 | tf_op jit(solution)/shard_map/all_to_all | solution.py:292
  180.2 1.6 shard_map.137
  181.8 0.0 copy-start.2
  181.8 0.0 copy-start.9
  181.8 0.0 copy-start.11
  181.9 14.3 %all_to_all.57 = f32[16,8,128]{2,1,0:T(8,128)S(1)} all-to-all(f32[16,8,128]{2,1,0:T(8,128)S(1)} %shard_map.137), channel_id=1, replica_groups=mesh['z'=16,'x'=4,'y'=4,'c'=2] {'z'}, dimensions={0} | all-to-all | bytes 131072 | tf_op jit(solution)/shard_map/all_to_all | solution.py:292
  196.2 14.1 %all_to_all.58.terms_ref = f32[8,16,8,128]{3,2,1,0:T(8,128)S(1)} all-to-all(f32[8,16,8,128]{3,2,1,0:T(8,128)S(1)} %broadcast_in_dim.11), channel_id=1, replica_groups=mesh['z'=16,'x'=4,'y'=4,'c'=2] {'x','c'}, dimensions={0} | all-to-all | bytes 1048576 | tf_op jit(solution)/shard_map/all_to_all | solution.py:292
  210.4 0.0 copy-start.7
  210.4 0.0 copy-done.2
  210.4 0.0 copy-done.9
  210.4 0.0 copy-done.11
  210.4 2.6 %shard_map.138 = (f32[6,128]{1,0:T(8,128)}, f32[6,128]{1,0:T(8,128)}, f32[8,128]{1,0:T(8,128)S(1)}) custom-call(s32[6]{0:T(128)S(1)} %copy-done.12, s32[6]{0:T(128)S(1)} %copy-done.13, f32[8,16,8,128]{3,2,1,0:T(8,128)S(1)} %all_to_all.58.terms_ref, s32[128,8,128]{2,1,0:T(8,128)S(1)} %get-tuple-element.25.ids_ref, ...), custom_call_target="tpu_custom_call" | custom-call | tf_op jit(solution)/shard_map/pallas_call | solution.py:20
  213.0 2.5 %all-gather.3 = f32[16,128]{1,0:T(8,128)S(1)} all-gather(f32[8,128]{1,0:T(8,128)S(1)} %get-tuple-element.31), channel_id=5, replica_groups=mesh['z'=16,'x'=4,'y'=4,'c'=2] {'c'}, dimensions={0}, use_global_device_ids=true | all-gather | bytes 12288 | tf_op jit(solution)/shard_map/all_gather | solution.py:367
  215.5 0.0 copy-done.7
  215.5 4.7 %shard_map.139 = (f32[6,3,128]{2,1,0:T(4,128)}, f32[6,3,128]{2,1,0:T(4,128)}) custom-call(f32[2,8,128]{2,1,0:T(8,128)S(1)} %bitcast.11, f32[2,6,136,128]{3,2,1,0:T(8,128)S(1)} %bitcast.8, f32[6,3,128,128]{3,2,1,0:T(8,128)S(1)} %get-tuple-element.32.mult_ref, f32[6,3,128]{2,1,0:T(4,128)S(1)} %get-tuple-element.33.forced_ref, f32[6,3,128]{2,1,0:T(4,128)S(1)} %copy-done.7), custom_call_target="tpu_custom_call" | custom-call | tf_op jit(solution)/shard_map/pallas_call | solution.py:20
  (6 shorter events, 0.2 us)
Async XLA Ops:
  7.2 77.0 %all-gather.6.cloned.1.call-start = ((), (), s32[]{:S(2)}) async-start(), calls=%async_computation.10 | async-start | bytes 2088960 | tf_op jit(solution)/shard_map/all_gather | solution.py:322
  7.2 1.0 copy-start.1
  8.2 0.7 copy-start.8
  8.9 0.7 copy-start.10
  10.3 1.3 copy-start.3
  11.5 1.3 copy-start.4
  12.8 0.7 copy-start.6
  13.5 0.7 copy-start.14
  28.0 11.6 %copy-start.5 = (f32[6,128,128]{2,1,0:T(8,128)S(1)}, f32[6,128,128]{2,1,0:T(8,128)}, u32[]{:S(2)}) copy-start(f32[6,128,128]{2,1,0:T(8,128)} %outlet_ref.1) | copy-start | bytes 1179652
  28.0 11.6 %copy-start.12 = (s32[6]{0:T(128)S(1)}, s32[6]{0:T(128)}, u32[]{:S(2)}) copy-start(s32[6]{0:T(128)} %lower_ref.9) | copy-start | bytes 76
  28.0 11.6 %copy-start.13 = (s32[6]{0:T(128)S(1)}, s32[6]{0:T(128)}, u32[]{:S(2)}) copy-start(s32[6]{0:T(128)} %upper_ref.9) | copy-start | bytes 76
  67.4 16.8 %all-to-all-start.1 = ((f32[8,16,8,128]{3,2,1,0:T(8,128)}), f32[8,16,8,128]{3,2,1,0:T(8,128)S(1)}, u32[]{:S(2)}, u32[]{:S(2)}) async-start(f32[8,16,8,128]{3,2,1,0:T(8,128)} %broadcast_in_dim.8), calls=%async_computation.1 | async-start | bytes 1048576 | tf_op jit(solution)/shard_map/all_to_all | solution.py:292
  84.2 1.5 copy-start
  181.8 28.5 %copy-start.2 = (f32[6,128,128]{2,1,0:T(8,128)S(1)}, f32[6,128,128]{2,1,0:T(8,128)}, u32[]{:S(2)}) copy-start(f32[6,128,128]{2,1,0:T(8,128)} %inv_ref.5) | copy-start | bytes 1179652
  181.8 28.5 %copy-start.9 = (f32[6,128]{1,0:T(8,128)S(1)}, f32[6,128]{1,0:T(8,128)}, u32[]{:S(2)}) copy-start(f32[6,128]{1,0:T(8,128)} %residual_ref.5) | copy-start | bytes 9220
  181.8 28.5 %copy-start.11 = (f32[6,128]{1,0:T(8,128)S(1)}, f32[6,128]{1,0:T(8,128)}, u32[]{:S(2)}) copy-start(f32[6,128]{1,0:T(8,128)} %cotangent_ref.6) | copy-start | bytes 9220
  210.4 5.1 %copy-start.7 = (f32[6,3,128]{2,1,0:T(4,128)S(1)}, f32[6,3,128]{2,1,0:T(4,128)}, u32[]{:S(2)}) copy-start(f32[6,3,128]{2,1,0:T(4,128)} %cotangent_ref.7) | copy-start | bytes 27652
Sparse Core Ops, SparseCore 0:
  10.4 70.5 all-gather.5

commit v3 on v2

v3 whole, which is shorter than its diff:
```python
import jax
import jax.numpy as jnp
from jax import lax
from jax.experimental import pallas as pl
from jax.experimental.pallas import tpu as pltpu
from jax.sharding import Mesh, PartitionSpec as P

SWEEPS = 4
WIDTH = 128
PACK = WIDTH + 8
F32 = jnp.float32

smem = pl.BlockSpec(memory_space=pltpu.SMEM)
vmem = pl.BlockSpec(memory_space=pltpu.VMEM)
hbm = pl.BlockSpec(memory_space=pltpu.HBM)


def array(*shape, dtype=F32):
    return jax.ShapeDtypeStruct(shape, dtype)


def run(kernel, outs, *args, scalars=0, where=vmem, scratch=(), limit=40, flops=0):
    single = not isinstance(outs, list)
    shapes = [outs] if single else outs
    result = pl.pallas_call(
        kernel,
        out_shape=shapes,
        in_specs=[smem] * scalars + [where] * (len(args) - scalars),
        out_specs=[vmem] * len(shapes),
        scratch_shapes=scratch,
        compiler_params=pltpu.CompilerParams(vmem_limit_bytes=limit * 1024 * 1024),
        cost_estimate=pl.CostEstimate(flops=flops, bytes_accessed=flops // 100, transcendentals=0) if flops else None,
    )(*args)
    return result[0] if single else result


def two_parts(a):
    high = a.astype(jnp.bfloat16)
    return high, (a - high.astype(F32)).astype(jnp.bfloat16)


def dot(a, b, transposed=False):
    dims = (((1,), (1 if transposed else 0,)), ((), ()))
    return lax.dot_general(a, b, dims, preferred_element_type=F32)


def parts_of(a):
    return a if isinstance(a, tuple) else two_parts(a)


def product(a, b):
    (ah, al), (bh, bl) = parts_of(a), parts_of(b)
    return dot(ah, bh) + (dot(ah, bl) + dot(al, bh))


def along(vector, matrix, transposed):
    vh, vl = two_parts(vector)
    mh, ml = parts_of(matrix)
    return dot(vh, mh, transposed) + (dot(vl, mh, transposed) + dot(vh, ml, transposed))


def applied(matrix, row):
    return along(row, matrix, True)


def applied_transposed(matrix, row):
    return along(row, matrix, False)


def fetch(pairs, sems):
    copies = [pltpu.make_async_copy(src, dst, sems.at[i]) for i, (src, dst) in enumerate(pairs)]
    for copy in copies:
        copy.start()
    return copies


def table_kernel(inv_ref, residual_ref, cotangent_ref, out_ref, inv, residual, cotangent, sems):
    piece = inv.shape[1]
    start = (lax.axis_index("y") * lax.axis_size("c") + lax.axis_index("c")) * piece
    start = pl.multiple_of(start, 8)
    copies = fetch(
        [
            (inv_ref.at[:, pl.ds(start, piece)], inv),
            (residual_ref, residual),
            (cotangent_ref, cotangent),
        ],
        sems,
    )
    for copy in copies:
        copy.wait()
    out_ref[:, :piece] = inv[...]
    for k in range(out_ref.shape[0]):
        out_ref[k, piece:] = jnp.concatenate(
            [residual[k : k + 1], cotangent[k : k + 1], jnp.zeros((6, WIDTH), F32)]
        )


def local_kernel(
    inv_hbm, link_hbm, residual_hbm, cotangent_hbm, high_ref, low_ref, forced_ref, out_ref,
    inv_ref, link_ref, residual_ref, cotangent_ref, sems,
):
    members, blocks = inv_ref.shape[:2]
    pairs = [(residual_hbm, residual_ref), (cotangent_hbm, cotangent_ref)]
    for s in range(members):
        pairs += [(inv_hbm.at[s], inv_ref.at[s]), (link_hbm.at[s], link_ref.at[s])]
    copies = fetch(pairs, sems)
    copies[0].wait()
    copies[1].wait()
    for s in range(members):
        copies[2 + 2 * s].wait()
        copies[3 + 2 * s].wait()
        m, f = [], []
        for i in range(blocks):
            inverse = two_parts(inv_ref[s, i])
            m.append(two_parts(product(inverse, two_parts(link_ref[s, i]))))
            high_ref[s, i], low_ref[s, i] = m[i]
            f.append(applied(inverse, residual_ref[s, i : i + 1]))
            forced_ref[s, i : i + 1] = f[i]
        total, vector = m[0], f[0]
        for i in range(1, blocks):
            total = product(m[i], total if i == 1 else two_parts(total))
            vector = applied(m[i], vector) + f[i]
        back = cotangent_ref[s, blocks - 1 : blocks]
        for i in range(blocks - 2, -1, -1):
            back = cotangent_ref[s, i : i + 1] + applied_transposed(m[i + 1], back)
        out_ref[s, :WIDTH] = total
        out_ref[s, WIDTH:] = jnp.concatenate(
            [vector, applied_transposed(m[0], back), jnp.zeros((6, WIDTH), F32)]
        )


def pair_kernel(pair_ref, out_ref):
    half = out_ref.shape[0]
    first_s = lax.axis_index("c") * half
    for k in range(half):
        first, second = pair_ref[0, first_s + k], pair_ref[1, first_s + k]
        one, two = two_parts(first[:WIDTH]), two_parts(second[:WIDTH])
        out_ref[k, :WIDTH] = product(two, one)
        out_ref[k, WIDTH : WIDTH + 1] = (
            applied(two, first[WIDTH : WIDTH + 1]) + second[WIDTH : WIDTH + 1]
        )
        out_ref[k, WIDTH + 1 : WIDTH + 2] = (
            applied_transposed(one, second[WIDTH + 1 : WIDTH + 2]) + first[WIDTH + 1 : WIDTH + 2]
        )
        out_ref[k, WIDTH + 2 :] = jnp.zeros((6, WIDTH), F32)


def keep(ref, k, matrix):
    ref[0, k], ref[1, k] = two_parts(matrix)


def kept(ref, k):
    return ref[0, k], ref[1, k]


def chain_kernel(lower_ref, upper_ref, chips_ref, outlet_ref, schur_ref, before_ref, after_ref, rows_ref, spread_ref):
    chips, half = chips_ref.shape[:2]
    first_s = lax.axis_index("c") * half
    y = lax.axis_index("y")
    row = lax.broadcasted_iota(jnp.int32, (8, WIDTH), 0)
    lane = lax.broadcasted_iota(jnp.int32, (8, WIDTH), 1)
    eye = (
        lax.broadcasted_iota(jnp.int32, (WIDTH, WIDTH), 0)
        == lax.broadcasted_iota(jnp.int32, (WIDTH, WIDTH), 1)
    ).astype(F32)
    nothing = jnp.zeros((1, WIDTH), F32)
    ids = jnp.zeros((8, WIDTH), jnp.int32)
    payload = [nothing] * 8
    for k in range(half):
        ids = jnp.where(lane == k, lower_ref[first_s + k], ids)
        ids = jnp.where(lane == half + k, upper_ref[first_s + k], ids)
        maps = [two_parts(chips_ref[i, k, :WIDTH]) for i in range(chips)]
        before, before_row = eye, nothing
        reached, reached_row = chips_ref[0, k, :WIDTH], chips_ref[0, k, WIDTH : WIDTH + 1]
        for i in range(1, chips):
            before = jnp.where(y == i, reached, before)
            before_row = jnp.where(y == i, reached_row, before_row)
            if i < chips - 1:
                reached = product(maps[i], reached)
            reached_row = applied(maps[i], reached_row) + chips_ref[i, k, WIDTH : WIDTH + 1]
        schur = outlet_ref[first_s + k]
        payload[k] = applied(schur, reached_row)
        after = schur
        upward, after_row = nothing, nothing
        for i in range(chips - 1, -1, -1):
            after = jnp.where(y == i, schur, after)
            after_row = jnp.where(y == i, upward, after_row)
            schur = product(schur, maps[i])
            upward = applied_transposed(maps[i], upward) + chips_ref[i, k, WIDTH + 1 : WIDTH + 2]
        payload[half + k] = upward
        keep(schur_ref, k, schur)
        keep(before_ref, k, before)
        keep(after_ref, k, after)
        rows_ref[k : k + 1] = before_row
        rows_ref[half + k : half + k + 1] = after_row
    rows_ref[2 * half :] = jnp.zeros((2, WIDTH), F32)
    full = jnp.where(row == 2 * half, ids.astype(F32), jnp.concatenate(payload))
    for i in range(spread_ref.shape[0]):
        spread_ref[i] = full


def build_kernel(ids_ref, table_ref, terms_ref, out_ref):
    dests = out_ref.shape[0]
    owned, rows = ids_ref.shape[0] // (2 * dests), table_ref.shape[1]
    half = owned // 2
    count = terms_ref.shape[0] * terms_ref.shape[1]
    x = lax.axis_index("x")
    terms = terms_ref[...].reshape(count, WIDTH)
    for step in range(dests):
        d = lax.rem(x + step, dests)
        out_ref[d, :count] = terms
        for tile in range(2 * owned):
            core, t = tile // owned, tile % owned
            side, k = (1, t) if t < half else (0, t - half)
            junction = ids_ref[(2 * step + side) * owned + core * half + k]
            basin = lax.div(junction, owned)
            line = lax.div(basin, dests)
            at = line * owned + (junction - basin * owned)
            here = basin - line * dests == x
            start = count + tile * rows
            out_ref[d, start : start + rows] = jnp.where(here, table_ref[at], 0.0)


def merge_kernel(picked_ref, out_ref):
    sides, rows = picked_ref.shape[:2]
    count = (out_ref.shape[0] - rows) // (sides - 1)
    for d in range(sides):
        out_ref[d * count : (d + 1) * count] = picked_ref[d, :count]
    total = picked_ref[0, count:]
    for d in range(1, sides):
        total = total + picked_ref[d, count:]
    out_ref[sides * count :] = total


def ends_kernel(both_ref, out_ref):
    tiles, rows = out_ref.shape[1:3]
    piece = (rows - 8) // 2
    first = both_ref.shape[1] - 2 * tiles * (piece + 8)
    c = lax.axis_index("c")
    for t in range(tiles):
        start = pl.multiple_of(first + (c * tiles + t) * (piece + 8), 8)
        full = jnp.concatenate(
            [both_ref[0, pl.ds(start, piece)], both_ref[1, pl.ds(start, piece)], both_ref[0, pl.ds(start + piece, 8)]]
        )
        for i in range(out_ref.shape[0]):
            out_ref[i, t] = full


def rule(above, below, half):
    row = lax.broadcasted_iota(jnp.int32, (8, WIDTH), 0)
    return jnp.where(row < half, above, jnp.where(row < 2 * half, below, -2))


def gathered(ids, values, pattern, half):
    total = jnp.sum(jnp.where(ids == pattern[None], values, 0.0), axis=0)
    inflow, outflow = total[0:1], total[half : half + 1]
    for k in range(1, half):
        inflow = inflow + total[k : k + 1]
        outflow = outflow + total[half + k : half + k + 1]
    return inflow, outflow


def step(lower_ref, upper_ref, ids, values, tiles, schur_ref, ends, base, spread_ref):
    half = schur_ref.shape[1]
    first_s = lax.axis_index("c") * half
    payload = [jnp.zeros((1, WIDTH), F32)] * 8
    for k in range(half):
        pattern = rule(upper_ref[first_s + k], lower_ref[first_s + k], half)
        inflow, outflow = gathered(ids, values, pattern, half)
        head = applied(kept(tiles, k), ends[k : k + 1] + inflow)
        relief = applied_transposed(
            kept(tiles, half + k), ends[half + k : half + k + 1] + outflow
        )
        schur = kept(schur_ref, k)
        payload[k] = base[k : k + 1] + applied(schur, head)
        payload[half + k] = base[half + k : half + k + 1] + applied_transposed(schur, relief)
    full = jnp.concatenate(payload)
    for i in range(spread_ref.shape[0]):
        spread_ref[i] = full


def first_step_kernel(
    lower_ref, upper_ref, terms_ref, ends_ref, schur_ref, base_ref, tiles_ref, ids_ref, rows_ref, spread_ref
):
    half = schur_ref.shape[1]
    piece = ends_ref.shape[2] - 8
    row = lax.broadcasted_iota(jnp.int32, (8, WIDTH), 0)
    lane = lax.broadcasted_iota(jnp.int32, (8, WIDTH), 1)
    values = terms_ref[:, : ids_ref.shape[0] * 4].reshape(-1, 8, WIDTH)
    chosen = jnp.where((row == lane) & (row < 2 * half), values[:, 2 * half : 2 * half + 1], 0.0)
    ids = jnp.sum(chosen, axis=2, keepdims=True).astype(jnp.int32)
    ids = jnp.broadcast_to(ids, values.shape)
    ids_ref[...] = ids
    for k in range(2 * half):
        keep(tiles_ref, k, jnp.concatenate([ends_ref[i, k, :piece] for i in range(ends_ref.shape[0])]))
    ends = [ends_ref[0, k, piece : piece + 1] for k in range(half)]
    ends += [ends_ref[0, half + k, piece + 1 : piece + 2] for k in range(half)]
    ends = jnp.concatenate(ends + [jnp.zeros((2, WIDTH), F32)])
    rows_ref[...] = ends
    step(lower_ref, upper_ref, ids, values, tiles_ref, schur_ref, ends, base_ref[0], spread_ref)


def step_kernel(
    lower_ref, upper_ref, terms_ref, ids_ref, tiles_ref, schur_ref, rows_ref, base_ref, spread_ref
):
    values = terms_ref[...].reshape(-1, 8, WIDTH)
    step(lower_ref, upper_ref, ids_ref[...], values, tiles_ref, schur_ref, rows_ref[...], base_ref[0], spread_ref)


def last_kernel(
    lower_ref, upper_ref, terms_ref, ids_ref, tiles_ref, rows_ref, before_ref, after_ref, passing_ref,
    inv_ref, residual_ref, cotangent_ref, sections_ref, adjoint_ref, shared_ref,
):
    half = before_ref.shape[1]
    owned = inv_ref.shape[0]
    first_s = lax.axis_index("c") * half
    first_j = (lax.axis_index("z") * lax.axis_size("x") + lax.axis_index("x")) * owned
    values = terms_ref[...].reshape(-1, 8, WIDTH)
    ids = ids_ref[...]
    shared_ref[2 * half :] = jnp.zeros((2, WIDTH), F32)
    for k in range(half):
        pattern = rule(upper_ref[first_s + k], lower_ref[first_s + k], half)
        inflow, outflow = gathered(ids, values, pattern, half)
        head = applied(kept(tiles_ref, k), rows_ref[k : k + 1] + inflow)
        relief = applied_transposed(
            kept(tiles_ref, half + k), rows_ref[half + k : half + k + 1] + outflow
        )
        shared_ref[k : k + 1] = applied(kept(before_ref, k), head) + passing_ref[k : k + 1]
        shared_ref[half + k : half + k + 1] = (
            applied_transposed(kept(after_ref, k), relief) + passing_ref[half + k : half + k + 1]
        )
    for k in range(owned):
        inflow, outflow = gathered(ids, values, rule(first_j + k, first_j + k, half), half)
        sections_ref[k : k + 1] = applied(inv_ref[k], residual_ref[k : k + 1] + inflow)
        adjoint_ref[k : k + 1] = cotangent_ref[k : k + 1] + outflow


def cells_kernel(shared_ref, pair_ref, high_ref, low_ref, forced_ref, cotangent_ref, update_ref, adjoint_ref):
    members, blocks = high_ref.shape[:2]
    half = members // 2
    c = lax.axis_index("c")
    for s in range(members):
        core, k = s // half, s % half
        enter = shared_ref[core, k : k + 1]
        leave = shared_ref[core, half + k : half + k + 1]
        other = pair_ref[1 - c, s]
        matrix = two_parts(other[:WIDTH])
        further = applied(matrix, enter) + other[WIDTH : WIDTH + 1]
        nearer = applied_transposed(matrix, leave) + other[WIDTH + 1 : WIDTH + 2]
        enter = jnp.where(c == 1, further, enter)
        leave = jnp.where(c == 0, nearer, leave)
        for i in range(blocks):
            enter = applied((high_ref[s, i], low_ref[s, i]), enter) + forced_ref[s, i : i + 1]
            update_ref[s, i : i + 1] = enter
        carried = cotangent_ref[s, blocks - 1 : blocks] + leave
        adjoint_ref[s, blocks - 1 : blocks] = carried
        for i in range(blocks - 2, -1, -1):
            carried = cotangent_ref[s, i : i + 1] + applied_transposed(
                (high_ref[s, i + 1], low_ref[s, i + 1]), carried
            )
            adjoint_ref[s, i : i + 1] = carried


def swap(spread, axis):
    return lax.all_to_all(spread, axis, 0, 0, tiled=False)


def over_x(values):
    return swap(jnp.broadcast_to(values[None], (lax.axis_size("x"),) + values.shape), "x")


def exchanged(spread):
    along_x = over_x(swap(spread, "z"))
    return lax.all_gather(along_x.reshape(-1, WIDTH), "c")


def shifted(values, places):
    n = lax.axis_size("x")
    return lax.ppermute(values, "x", [((i + places) % n, i) for i in range(n)])


def shards(
    reach_residual,
    chain_inv,
    chain_link,
    outlet_link,
    junction_inv,
    junction_residual,
    upper_junction,
    lower_junction,
    cell_cotangent,
    junction_cotangent,
):
    members, blocks, width = reach_residual.shape
    owned = junction_inv.shape[0]
    zs, xs, ys, cs = (lax.axis_size(a) for a in ("z", "x", "y", "c"))
    half = members // cs
    piece = width // (ys * cs)
    bf16 = jnp.bfloat16
    lower, upper = lower_junction, upper_junction

    own = jnp.stack([lower, upper])[None]
    beside = shifted(own, 1)

    part = run(
        table_kernel,
        array(owned, piece + 8, width),
        junction_inv, junction_residual, junction_cotangent,
        where=hbm, limit=60,
        scratch=[
            pltpu.VMEM((owned, piece, width), F32),
            pltpu.VMEM((owned, width), F32),
            pltpu.VMEM((owned, width), F32),
            pltpu.SemaphoreType.DMA((3,)),
        ],
    )
    table = lax.all_gather(part, "z").reshape(zs * owned, piece + 8, width)

    chain = (members, blocks, width, width)
    high, low, forced, local = run(
        local_kernel,
        [
            array(*chain, dtype=bf16),
            array(*chain, dtype=bf16),
            array(members, blocks, width),
            array(members, PACK, width),
        ],
        chain_inv, chain_link, reach_residual, cell_cotangent,
        where=hbm, limit=60, flops=2_000_000_000,
        scratch=[
            pltpu.VMEM(chain, F32),
            pltpu.VMEM(chain, F32),
            pltpu.VMEM((members, blocks, width), F32),
            pltpu.VMEM((members, blocks, width), F32),
            pltpu.SemaphoreType.DMA((2 + 2 * members,)),
        ],
    )
    local, beside = lax.optimization_barrier((local, beside))
    two = jnp.concatenate([own, beside])
    plane = jnp.concatenate([two, shifted(two, 2)]).reshape(-1)
    pair = lax.all_gather(local, "c")
    chips = lax.all_gather(run(pair_kernel, array(half, PACK, width), pair), "y")
    matrices = array(2, half, width, width, dtype=bf16)
    schur, before, after, passing, first = run(
        chain_kernel,
        [matrices, matrices, matrices, array(8, width), array(zs, 8, width)],
        lower, upper, chips, outlet_link, scalars=2,
    )

    count = zs * 8
    fetched = 2 * owned * (piece + 8)
    built = run(
        build_kernel, array(xs, count + fetched, width), plane, table, swap(first, "z"), scalars=1
    )
    merged = run(merge_kernel, array(xs * count + fetched, width), swap(built, "x"))
    both = lax.all_gather(merged, "c")
    ends = swap(run(ends_kernel, array(ys, owned, 2 * piece + 8, width), both), "y")
    tiles, ids, rows, spread = run(
        first_step_kernel,
        [
            array(2, 2 * half, width, width, dtype=bf16),
            array(cs * xs * zs, 8, width, dtype=jnp.int32),
            array(8, width),
            array(zs, 8, width),
        ],
        lower, upper, both, ends, schur, first, scalars=2,
    )
    terms = exchanged(spread)
    for sweep in range(2, SWEEPS):
        spread = run(
            step_kernel, array(zs, 8, width), lower, upper, terms, ids, tiles, schur, rows, first, scalars=2
        )
        terms = exchanged(spread)
    sections, adjoint, shared = run(
        last_kernel,
        [array(owned, width), array(owned, width), array(8, width)],
        lower, upper, terms, ids, tiles, rows, before, after, passing,
        junction_inv, junction_residual, junction_cotangent, scalars=2,
    )
    cell_update, cell_adjoint = run(
        cells_kernel,
        [array(members, blocks, width), array(members, blocks, width)],
        lax.all_gather(shared, "c"), pair, high, low, forced, cell_cotangent,
    )
    return (cell_update, sections, cell_adjoint, adjoint)


def solution(mesh):
    basins = mesh.shape["basin"]
    grid = Mesh(mesh.devices.reshape(basins // 4, 4, 4, 2), ("z", "x", "y", "c"))
    b, r = ("z", "x"), ("y", "c")
    return jax.shard_map(
        shards,
        mesh=grid,
        in_specs=(
            P(b, r, None),
            P(b, r, None, None),
            P(b, r, None, None),
            P(b, None, None),
            P(b, None, None),
            P(b, None),
            P(b),
            P(b),
            P(b, r, None),
            P(b, None),
        ),
        out_specs=(P(b, r, None), P(b, None), P(b, r, None), P(b, None)),
        check_vma=False,
    )
```

time: 228 us -> 228 us (level)
  blocking collectives: 165 us -> 144 us
  starting transfers between devices: 7.37 us -> 21.3 us
  waiting for transfers between devices: 9.52 us -> 18.1 us
  local copies, waits for them, and re-layouts: 8.85 us -> 1.45 us
  Pallas kernels: 22.5 us -> 27.9 us
    all_to_all x9 -> x8, blocking collectives: 142 us -> 95.4 us  [swap(): return lax.all_to_all(spread, axis, 0, 0, tiled=False)]
    all_gather x1 -> x5, blocking collectives: 11.1 us -> 40.5 us  [the longest x3 16 us: exchanged(): return lax.all_gather(along_x.reshape(-1, WIDTH), 'c')]
    all_gather x1, waiting for transfers between devices: 0.02 us -> 8.57 us  [shards(): table = lax.all_gather(part, 'z').reshape(zs * owned, piece + 8, width)]
    ppermute x0 -> x2, starting transfers between devices: none -> 7.51 us  [shifted(): return lax.ppermute(values, 'x', [((i + places) % n, i) for i in range(n)])]
    unnamed x30 -> x22, local copies, waits for them, and re-layouts: 7.88 us -> 1.31 us
    all_to_all x1, starting transfers between devices: 7.34 us -> 13.8 us  [swap(): return lax.all_to_all(spread, axis, 0, 0, tiled=False)]
    pallas_call x11 -> x12, Pallas kernels: 22.5 us -> 27.9 us  [run(): pl.pallas_call(kernel, out_shape=shapes, in_specs=[smem] * scalars + [whe...]
    ppermute x0 -> x2, waiting for transfers between devices: none -> 3.52 us  [shifted(): return lax.ppermute(values, 'x', [((i + places) % n, i) for i in range(n)])]
  transfers between devices with their start and end apart: 2 -> 4, of which waited for: 1 -> 3; matrix products, arithmetic and copies ran while one was open for 0% -> 0% of each run, Pallas kernels for 4% -> 5%
where the time goes in v3:
time: 228 us; the launch traced here: 227 us
  blocking collectives  144 us (63%)
  Pallas kernels  27.9 us (12%)
  starting transfers between devices  21.3 us (9%)
  waiting for transfers between devices  18.1 us (8%)
  between operations  14.2 us (6%)
    all_to_all x8, blocking collectives, swap(): return lax.all_to_all(spread, axis, 0, 0, tiled=False)  95.4 us
    pallas_call x12, Pallas kernels, run(): pl.pallas_call(kernel, out_shape=shapes, in_specs=[smem] * scalars + [whe...  27.9 us
    all_gather x3, blocking collectives, exchanged(): return lax.all_gather(along_x.reshape(-1, WIDTH), 'c')  16 us
    all_to_all x1, starting transfers between devices, swap(): return lax.all_to_all(spread, axis, 0, 0, tiled=False)  13.8 us
    all_gather x1, blocking collectives, shards(): both = lax.all_gather(merged, 'c')  13.4 us
    all_gather x1, blocking collectives, shards(): lax.all_gather(run(pair_kernel, array(half, PACK, width), pair), 'y')  11.1 us
    all_gather x1, waiting for transfers between devices, shards(): table = lax.all_gather(part, 'z').reshape(zs * owned, piece + 8, width)  8.57 us
    ppermute x2, starting transfers between devices, shifted(): return lax.ppermute(values, 'x', [((i + places) % n, i) for i in range(n)])  7.51 us
  transfers between devices with their start and end apart: 4, of which 3 were waited for; matrix products, arithmetic and copies ran while one was open for 0% of the time, Pallas kernels for 5%

profile of v3, /device:TPU:1, one launch (start us, length us, event | category | flops | bytes accessed | tf_op | source)
XLA Modules:
  0.0 227.2 jit_solution(5231230334318268873)
XLA Ops:
  7.2 0.0 all-gather.7.cloned.1.call-start
  7.2 1.5 shard_map.130
  8.7 0.0 all-gather.7.cloned.1.call-update
  8.7 0.7 add_bitcast_fusion
  9.4 5.2 %collective-permute-start = (s32[1,2,6]{2,1,0:T(2,128)S(1)}, s32[1,2,6]{2,1,0:T(2,128)S(1)}, u32[]{:S(2)}, u32[]{:S(2)}) collective-permute-start(s32[1,2,6]{2,1,0:T(2,128)S(1)} %add_bitcast_fusion), channel_id=1, source_target_pairs={{8,0},{16,8},{24,16},{0,24},{9,1},{17,9},{25,17},{1,25},{10,2},{18... | collective-permute-start | bytes 152 | tf_op jit(solution)/shard_map/ppermute | solution.py:379
  14.6 7.5 %shard_map.129 = (bf16[6,3,128,128]{3,2,1,0:T(8,128)(2,1)}, bf16[6,3,128,128]{3,2,1,0:T(8,128)(2,1)}, f32[6,3,128]{2,1,0:T(4,128)}, f32[6,136,128]{2,1,0:T(8,128)}) custom-call(f32[6,3,128,128]{3,2,1,0:T(8,128)} %inv_hbm.1, f32[6,3,128,128]{3,2,1,0:T(8,128)} %link_hbm.1, f32[6,3,128]{2,1,0:T(4,128)} %residual_hbm.1, f32[6,3,128]{2,1,0:T(4,128)} %cotangent_ref.5), custom_call_target="tpu_custom_call" | custom-call | flops 2000000000 | bytes 20000000 | tf_op jit(solution)/shard_map/pallas_call | solution.py:25
  22.1 0.0 collective-permute-done
  22.2 5.8 %all-gather.1 = f32[12,136,128]{2,1,0:T(8,128)S(1)} all-gather(f32[6,136,128]{2,1,0:T(8,128)} %get-tuple-element.26), channel_id=3, replica_groups=mesh['z'=16,'x'=4,'y'=4,'c'=2] {'c'}, dimensions={0}, use_global_device_ids=true | all-gather | bytes 1253376 | tf_op jit(solution)/shard_map/all_gather | solution.py:441
  28.0 0.0 copy-start.4
  28.0 0.0 copy-start.5
  28.0 0.0 copy-start.6
  28.0 0.4 shard_map.131
  28.4 11.1 %all-gather.2 = f32[12,136,128]{2,1,0:T(8,128)S(1)} all-gather(f32[3,136,128]{2,1,0:T(8,128)S(1)} %shard_map.131), channel_id=4, replica_groups=mesh['z'=16,'x'=4,'y'=4,'c'=2] {'y'}, dimensions={0}, use_global_device_ids=true | all-gather | bytes 1044480 | tf_op jit(solution)/shard_map/all_gather | solution.py:442
  39.5 0.0 copy-done.4
  39.5 0.0 copy-done.5
  39.6 0.0 copy-done.6
  39.6 4.4 %shard_map.132 = (bf16[2,3,128,128]{3,2,1,0:T(8,128)(2,1)S(1)}, bf16[2,3,128,128]{3,2,1,0:T(8,128)(2,1)S(1)}, bf16[2,3,128,128]{3,2,1,0:T(8,128)(2,1)S(1)}, f32[8,128]{1,0:T(8,128)S(1)}, f32[16,8,128]{2,1,0:T(8,128)}) custom-call(s32[6]{0:T(128)S(1)} %copy-done.5, s32[6]{0:T(128)S(1)} %copy-done.6, f32[4,3,136,128]{3,2,1,0:T(8,128)S(1)} %bitcast.15, ...), custom_call_target="tpu_custom_call" | custom-call | tf_op jit(solution)/shard_map/pallas_call | solution.py:25
  44.0 13.8 %all-to-all-start = ((f32[16,8,128]{2,1,0:T(8,128)}), f32[16,8,128]{2,1,0:T(8,128)S(1)}, u32[]{:S(2)}, u32[]{:S(2)}) async-start(f32[16,8,128]{2,1,0:T(8,128)} %get-tuple-element.27.base_ref), calls=%async_computation | async-start | bytes 131072 | tf_op jit(solution)/shard_map/all_to_all | solution.py:365
  57.8 2.3 %collective-permute-start.1 = (s32[2,2,6]{2,1,0:T(2,128)S(1)}, s32[2,2,6]{2,1,0:T(2,128)S(1)}, u32[]{:S(2)}, u32[]{:S(2)}) collective-permute-start(s32[2,2,6]{2,1,0:T(2,128)S(1)} %pad_add_fusion.1), channel_id=1, source_target_pairs={{16,0},{24,8},{0,16},{8,24},{17,1},{25,9},{1,17},{9,25},{18,2},{26... | collective-permute-start | bytes 296 | tf_op jit(solution)/shard_map/ppermute | solution.py:379
  60.1 3.5 %collective-permute-done.1 = s32[2,2,6]{2,1,0:T(2,128)S(1)} collective-permute-done((s32[2,2,6]{2,1,0:T(2,128)S(1)}, s32[2,2,6]{2,1,0:T(2,128)S(1)}, u32[]{:S(2)}, u32[]{:S(2)}) %collective-permute-start.1) | collective-permute-done | bytes 128 | tf_op jit(solution)/shard_map/ppermute | solution.py:379
  63.6 0.1 reshape.17.ids_ref
  63.7 6.0 %all-to-all-done.terms_ref = f32[16,8,128]{2,1,0:T(8,128)S(1)} async-done(((f32[16,8,128]{2,1,0:T(8,128)}), f32[16,8,128]{2,1,0:T(8,128)S(1)}, u32[]{:S(2)}, u32[]{:S(2)}) %all-to-all-start) | async-done | bytes 65568 | tf_op jit(solution)/shard_map/all_to_all | solution.py:365
  69.7 8.6 %all-gather.7.cloned.1.call-done.table_ref = f32[96,24,128]{2,1,0:T(8,128)} async-done(((f32[6,24,128]{2,1,0:T(8,128)}), f32[96,24,128]{2,1,0:T(8,128)}) %all-gather.7.cloned.1.call-update) | async-done | bytes 1179664 | tf_op jit(solution)/shard_map/all_gather | solution.py:417
  78.3 0.0 copy-start.1
  78.3 1.3 copy-done.1
  79.6 0.9 shard_map.133
  80.5 12.4 %all_to_all.45.picked_ref = f32[4,416,128]{2,1,0:T(8,128)S(1)} all-to-all(f32[4,416,128]{2,1,0:T(8,128)S(1)} %shard_map.133), channel_id=1, replica_groups=mesh['z'=16,'x'=4,'y'=4,'c'=2] {'x'}, dimensions={0} | all-to-all | bytes 1703936 | tf_op jit(solution)/shard_map/all_to_all | solution.py:365
  92.9 13.4 %all-gather.3 = f32[1600,128]{1,0:T(8,128)S(1)} all-gather(f32[800,128]{1,0:T(8,128)S(1)} %shard_map.134), channel_id=5, replica_groups=mesh['z'=16,'x'=4,'y'=4,'c'=2] {'c'}, dimensions={0}, use_global_device_ids=true | all-gather | bytes 1228800 | tf_op jit(solution)/shard_map/all_gather | solution.py:456
  106.3 12.4 %all_to_all.46.ends_ref = f32[4,6,40,128]{3,2,1,0:T(8,128)S(1)} all-to-all(f32[4,6,40,128]{3,2,1,0:T(8,128)S(1)} %shard_map.135), channel_id=1, replica_groups=mesh['z'=16,'x'=4,'y'=4,'c'=2] {'y'}, dimensions={0} | all-to-all | bytes 983040 | tf_op jit(solution)/shard_map/all_to_all | solution.py:365
  118.7 2.0 shard_map.136
  120.8 18.1 %all_to_all.47 = f32[16,8,128]{2,1,0:T(8,128)S(1)} all-to-all(f32[16,8,128]{2,1,0:T(8,128)S(1)} %get-tuple-element.29), channel_id=1, replica_groups=mesh['z'=16,'x'=4,'y'=4,'c'=2] {'z'}, dimensions={0} | all-to-all | bytes 131072 | tf_op jit(solution)/shard_map/all_to_all | solution.py:365
  138.8 7.9 %all_to_all.48 = f32[4,16,8,128]{3,2,1,0:T(8,128)S(1)} all-to-all(f32[4,16,8,128]{3,2,1,0:T(8,128)S(1)} %broadcast_in_dim.9), channel_id=1, replica_groups=mesh['z'=16,'x'=4,'y'=4,'c'=2] {'x'}, dimensions={0} | all-to-all | bytes 524288 | tf_op jit(solution)/shard_map/all_to_all | solution.py:365
  146.8 6.2 %all_gather.47.terms_ref = f32[2,512,128]{2,1,0:T(8,128)S(1)} all-gather(f32[1,512,128]{2,1,0:T(8,128)S(1)} %bitcast.19), channel_id=1, replica_groups=mesh['z'=16,'x'=4,'y'=4,'c'=2] {'c'}, dimensions={0}, use_global_device_ids=true | all-gather | bytes 786432 | tf_op jit(solution)/shard_map/all_gather | solution.py:374
  153.0 1.9 shard_map.137
  154.9 14.3 %all_to_all.49 = f32[16,8,128]{2,1,0:T(8,128)S(1)} all-to-all(f32[16,8,128]{2,1,0:T(8,128)S(1)} %shard_map.137), channel_id=1, replica_groups=mesh['z'=16,'x'=4,'y'=4,'c'=2] {'z'}, dimensions={0} | all-to-all | bytes 131072 | tf_op jit(solution)/shard_map/all_to_all | solution.py:365
  169.2 7.9 %all_to_all.50 = f32[4,16,8,128]{3,2,1,0:T(8,128)S(1)} all-to-all(f32[4,16,8,128]{3,2,1,0:T(8,128)S(1)} %broadcast_in_dim.10), channel_id=1, replica_groups=mesh['z'=16,'x'=4,'y'=4,'c'=2] {'x'}, dimensions={0} | all-to-all | bytes 524288 | tf_op jit(solution)/shard_map/all_to_all | solution.py:365
  177.1 4.9 %all_gather.48.terms_ref = f32[2,512,128]{2,1,0:T(8,128)S(1)} all-gather(f32[1,512,128]{2,1,0:T(8,128)S(1)} %bitcast.20), channel_id=1, replica_groups=mesh['z'=16,'x'=4,'y'=4,'c'=2] {'c'}, dimensions={0}, use_global_device_ids=true | all-gather | bytes 786432 | tf_op jit(solution)/shard_map/all_gather | solution.py:374
  181.9 1.9 shard_map.138
  183.8 0.0 copy-start
  183.9 0.0 copy-start.7
  183.9 0.0 copy-start.8
  183.9 14.5 %all_to_all.51 = f32[16,8,128]{2,1,0:T(8,128)S(1)} all-to-all(f32[16,8,128]{2,1,0:T(8,128)S(1)} %shard_map.138), channel_id=1, replica_groups=mesh['z'=16,'x'=4,'y'=4,'c'=2] {'z'}, dimensions={0} | all-to-all | bytes 131072 | tf_op jit(solution)/shard_map/all_to_all | solution.py:365
  198.4 7.9 %all_to_all.52 = f32[4,16,8,128]{3,2,1,0:T(8,128)S(1)} all-to-all(f32[4,16,8,128]{3,2,1,0:T(8,128)S(1)} %broadcast_in_dim.11), channel_id=1, replica_groups=mesh['z'=16,'x'=4,'y'=4,'c'=2] {'x'}, dimensions={0} | all-to-all | bytes 524288 | tf_op jit(solution)/shard_map/all_to_all | solution.py:365
  206.3 4.9 %all_gather.49.terms_ref = f32[2,512,128]{2,1,0:T(8,128)S(1)} all-gather(f32[1,512,128]{2,1,0:T(8,128)S(1)} %bitcast.21), channel_id=1, replica_groups=mesh['z'=16,'x'=4,'y'=4,'c'=2] {'c'}, dimensions={0}, use_global_device_ids=true | all-gather | bytes 786432 | tf_op jit(solution)/shard_map/all_gather | solution.py:374
  211.2 0.0 copy-start.2
  211.2 0.0 copy-start.3
  211.2 0.0 copy-start.9
  211.2 0.0 copy-start.10
  211.2 0.0 copy-done
  211.2 0.0 copy-done.7
  211.3 0.0 copy-done.8
  211.3 2.6 %shard_map.139 = (f32[6,128]{1,0:T(8,128)}, f32[6,128]{1,0:T(8,128)}, f32[8,128]{1,0:T(8,128)S(1)}) custom-call(s32[6]{0:T(128)S(1)} %copy-done.5, s32[6]{0:T(128)S(1)} %copy-done.6, f32[2,512,128]{2,1,0:T(8,128)S(1)} %all_gather.49.terms_ref, s32[128,8,128]{2,1,0:T(8,128)S(1)} %get-tuple-element.30.ids_ref, ...), custom_call_target="tpu_custom_call" | custom-call | tf_op jit(solution)/shard_map/pallas_call | solution.py:25
  213.9 1.9 all-gather.4
  215.7 0.0 copy-done.2
  215.7 0.0 copy-done.3
  215.7 0.0 copy-done.9
  215.7 0.0 copy-done.10
  215.7 4.7 %shard_map.140 = (f32[6,3,128]{2,1,0:T(4,128)}, f32[6,3,128]{2,1,0:T(4,128)}) custom-call(f32[2,8,128]{2,1,0:T(8,128)S(1)} %bitcast.16, f32[2,6,136,128]{3,2,1,0:T(8,128)S(1)} %bitcast.12, bf16[6,3,128,128]{3,2,1,0:T(8,128)(2,1)S(1)} %copy-done.2, bf16[6,3,128,128]{3,2,1,0:T(8,128)(2,1)S(1)} %copy-done.3, f32[6,3,128]{2,1,0:T(4,128)S(1)} %copy-done.10, ...), custom_call_target="tpu_custom_call" | custom-call | tf_op jit(solution)/shard_map/pallas_call | solution.py:25
  (7 shorter events, 0.1 us)
Async XLA Ops:
  7.2 71.1 %all-gather.7.cloned.1.call-start = ((), (), s32[]{:S(2)}) async-start(), calls=%async_computation.9 | async-start | bytes 1253376 | tf_op jit(solution)/shard_map/all_gather | solution.py:417
  9.4 12.8 %collective-permute-start = (s32[1,2,6]{2,1,0:T(2,128)S(1)}, s32[1,2,6]{2,1,0:T(2,128)S(1)}, u32[]{:S(2)}, u32[]{:S(2)}) collective-permute-start(s32[1,2,6]{2,1,0:T(2,128)S(1)} %add_bitcast_fusion), channel_id=1, source_target_pairs={{8,0},{16,8},{24,16},{0,24},{9,1},{17,9},{25,17},{1,25},{10,2},{18... | collective-permute-start | bytes 152 | tf_op jit(solution)/shard_map/ppermute | solution.py:379
  28.0 11.6 %copy-start.4 = (f32[6,128,128]{2,1,0:T(8,128)S(1)}, f32[6,128,128]{2,1,0:T(8,128)}, u32[]{:S(2)}) copy-start(f32[6,128,128]{2,1,0:T(8,128)} %outlet_ref.1) | copy-start | bytes 1179652
  28.0 11.6 %copy-start.5 = (s32[6]{0:T(128)S(1)}, s32[6]{0:T(128)}, u32[]{:S(2)}) copy-start(s32[6]{0:T(128)} %lower_ref.9) | copy-start | bytes 76
  28.0 11.6 %copy-start.6 = (s32[6]{0:T(128)S(1)}, s32[6]{0:T(128)}, u32[]{:S(2)}) copy-start(s32[6]{0:T(128)} %upper_ref.9) | copy-start | bytes 76
  44.0 25.7 %all-to-all-start = ((f32[16,8,128]{2,1,0:T(8,128)}), f32[16,8,128]{2,1,0:T(8,128)S(1)}, u32[]{:S(2)}, u32[]{:S(2)}) async-start(f32[16,8,128]{2,1,0:T(8,128)} %get-tuple-element.27.base_ref), calls=%async_computation | async-start | bytes 131072 | tf_op jit(solution)/shard_map/all_to_all | solution.py:365
  57.8 5.8 %collective-permute-start.1 = (s32[2,2,6]{2,1,0:T(2,128)S(1)}, s32[2,2,6]{2,1,0:T(2,128)S(1)}, u32[]{:S(2)}, u32[]{:S(2)}) collective-permute-start(s32[2,2,6]{2,1,0:T(2,128)S(1)} %pad_add_fusion.1), channel_id=1, source_target_pairs={{16,0},{24,8},{0,16},{8,24},{17,1},{25,9},{1,17},{9,25},{18,2},{26... | collective-permute-start | bytes 296 | tf_op jit(solution)/shard_map/ppermute | solution.py:379
  78.3 1.3 copy-start.1
  183.8 27.4 %copy-start = (f32[6,128,128]{2,1,0:T(8,128)S(1)}, f32[6,128,128]{2,1,0:T(8,128)}, u32[]{:S(2)}) copy-start(f32[6,128,128]{2,1,0:T(8,128)} %inv_ref.3) | copy-start | bytes 1179652
  183.9 27.4 %copy-start.7 = (f32[6,128]{1,0:T(8,128)S(1)}, f32[6,128]{1,0:T(8,128)}, u32[]{:S(2)}) copy-start(f32[6,128]{1,0:T(8,128)} %residual_ref.3) | copy-start | bytes 9220
  183.9 27.4 %copy-start.8 = (f32[6,128]{1,0:T(8,128)S(1)}, f32[6,128]{1,0:T(8,128)}, u32[]{:S(2)}) copy-start(f32[6,128]{1,0:T(8,128)} %cotangent_ref.4) | copy-start | bytes 9220
  211.2 4.5 %copy-start.2 = (bf16[6,3,128,128]{3,2,1,0:T(8,128)(2,1)S(1)}, bf16[6,3,128,128]{3,2,1,0:T(8,128)(2,1)}, u32[]{:S(2)}) copy-start(bf16[6,3,128,128]{3,2,1,0:T(8,128)(2,1)} %get-tuple-element.37.high_ref) | copy-start | bytes 1769476
  211.2 4.5 %copy-start.3 = (bf16[6,3,128,128]{3,2,1,0:T(8,128)(2,1)S(1)}, bf16[6,3,128,128]{3,2,1,0:T(8,128)(2,1)}, u32[]{:S(2)}) copy-start(bf16[6,3,128,128]{3,2,1,0:T(8,128)(2,1)} %get-tuple-element.38.low_ref) | copy-start | bytes 1769476
  211.2 4.5 %copy-start.9 = (f32[6,3,128]{2,1,0:T(4,128)S(1)}, f32[6,3,128]{2,1,0:T(4,128)}, u32[]{:S(2)}) copy-start(f32[6,3,128]{2,1,0:T(4,128)} %cotangent_ref.5) | copy-start | bytes 27652
  211.2 4.5 %copy-start.10 = (f32[6,3,128]{2,1,0:T(4,128)S(1)}, f32[6,3,128]{2,1,0:T(4,128)}, u32[]{:S(2)}) copy-start(f32[6,3,128]{2,1,0:T(4,128)} %get-tuple-element.39.forced_ref) | copy-start | bytes 27652
Sparse Core Ops, SparseCore 0:
  10.1 68.1 all-gather.6

commit v4 on v3

--- a/solution.py
+++ b/solution.py
@@ -1,3 +1,5 @@
+import math
+
 import jax
 import jax.numpy as jnp
 from jax import lax
@@ -74,25 +76,36 @@
     return copies
 
 
-def table_kernel(inv_ref, residual_ref, cotangent_ref, out_ref, inv, residual, cotangent, sems):
-    piece = inv.shape[1]
-    start = (lax.axis_index("y") * lax.axis_size("c") + lax.axis_index("c")) * piece
-    start = pl.multiple_of(start, 8)
+def table_kernel(inv_ref, residual_ref, cotangent_ref, out_ref, residual, cotangent, sems):
     copies = fetch(
         [
-            (inv_ref.at[:, pl.ds(start, piece)], inv),
+            (inv_ref, out_ref.at[:, :WIDTH]),
             (residual_ref, residual),
             (cotangent_ref, cotangent),
         ],
         sems,
     )
+    copies[1].wait()
+    copies[2].wait()
+    for k in range(out_ref.shape[0]):
+        out_ref[k, WIDTH:] = jnp.concatenate(
+            [residual[k : k + 1], cotangent[k : k + 1], jnp.zeros((6, WIDTH), F32)]
+        )
+    copies[0].wait()
+
+
+def slice_kernel(near_ref, out_ref, sems):
+    piece = out_ref.shape[1] - 8
+    start = pl.multiple_of(lax.axis_index("y") * piece, 8)
+    copies = fetch(
+        [
+            (near_ref.at[:, pl.ds(start, piece)], out_ref.at[:, :piece]),
+            (near_ref.at[:, WIDTH:], out_ref.at[:, piece:]),
+        ],
+        sems,
+    )
     for copy in copies:
         copy.wait()
-    out_ref[:, :piece] = inv[...]
-    for k in range(out_ref.shape[0]):
-        out_ref[k, piece:] = jnp.concatenate(
-            [residual[k : k + 1], cotangent[k : k + 1], jnp.zeros((6, WIDTH), F32)]
-        )
 
 
 def local_kernel(
@@ -199,51 +212,29 @@
         spread_ref[i] = full
 
 
-def build_kernel(ids_ref, table_ref, terms_ref, out_ref):
-    dests = out_ref.shape[0]
-    owned, rows = ids_ref.shape[0] // (2 * dests), table_ref.shape[1]
+def pick_kernel(ids_ref, table_ref, out_ref):
+    dests, owned = out_ref.shape[:2]
     half = owned // 2
-    count = terms_ref.shape[0] * terms_ref.shape[1]
     x = lax.axis_index("x")
-    terms = terms_ref[...].reshape(count, WIDTH)
-    for step in range(dests):
-        d = lax.rem(x + step, dests)
-        out_ref[d, :count] = terms
-        for tile in range(2 * owned):
-            core, t = tile // owned, tile % owned
+    first_s = lax.axis_index("c") * half
+    for d in range(dests):
+        for t in range(owned):
             side, k = (1, t) if t < half else (0, t - half)
-            junction = ids_ref[(2 * step + side) * owned + core * half + k]
+            junction = ids_ref[(2 * d + side) * owned + first_s + k]
             basin = lax.div(junction, owned)
             line = lax.div(basin, dests)
             at = line * owned + (junction - basin * owned)
             here = basin - line * dests == x
-            start = count + tile * rows
-            out_ref[d, start : start + rows] = jnp.where(here, table_ref[at], 0.0)
+            out_ref[d, t] = jnp.where(here, table_ref[at], 0.0)
 
 
 def merge_kernel(picked_ref, out_ref):
-    sides, rows = picked_ref.shape[:2]
-    count = (out_ref.shape[0] - rows) // (sides - 1)
-    for d in range(sides):
-        out_ref[d * count : (d + 1) * count] = picked_ref[d, :count]
-    total = picked_ref[0, count:]
-    for d in range(1, sides):
-        total = total + picked_ref[d, count:]
-    out_ref[sides * count :] = total
-
-
-def ends_kernel(both_ref, out_ref):
-    tiles, rows = out_ref.shape[1:3]
-    piece = (rows - 8) // 2
-    first = both_ref.shape[1] - 2 * tiles * (piece + 8)
-    c = lax.axis_index("c")
-    for t in range(tiles):
-        start = pl.multiple_of(first + (c * tiles + t) * (piece + 8), 8)
-        full = jnp.concatenate(
-            [both_ref[0, pl.ds(start, piece)], both_ref[1, pl.ds(start, piece)], both_ref[0, pl.ds(start + piece, 8)]]
-        )
-        for i in range(out_ref.shape[0]):
-            out_ref[i, t] = full
+    total = picked_ref[0]
+    for d in range(1, picked_ref.shape[0]):
+        total = total + picked_ref[d]
+    rows = picked_ref.shape[2]
+    out_ref[:, :rows] = total
+    out_ref[:, rows:] = jnp.zeros((out_ref.shape[0], out_ref.shape[1] - rows, WIDTH), F32)
 
 
 def rule(above, below, half):
@@ -283,10 +274,10 @@
     lower_ref, upper_ref, terms_ref, ends_ref, schur_ref, base_ref, tiles_ref, ids_ref, rows_ref, spread_ref
 ):
     half = schur_ref.shape[1]
-    piece = ends_ref.shape[2] - 8
+    piece = WIDTH // ends_ref.shape[0]
     row = lax.broadcasted_iota(jnp.int32, (8, WIDTH), 0)
     lane = lax.broadcasted_iota(jnp.int32, (8, WIDTH), 1)
-    values = terms_ref[:, : ids_ref.shape[0] * 4].reshape(-1, 8, WIDTH)
+    values = terms_ref[...].reshape(-1, 8, WIDTH)
     chosen = jnp.where((row == lane) & (row < 2 * half), values[:, 2 * half : 2 * half + 1], 0.0)
     ids = jnp.sum(chosen, axis=2, keepdims=True).astype(jnp.int32)
     ids = jnp.broadcast_to(ids, values.shape)
@@ -314,7 +305,7 @@
     half = before_ref.shape[1]
     owned = inv_ref.shape[0]
     first_s = lax.axis_index("c") * half
-    first_j = (lax.axis_index("z") * lax.axis_size("x") + lax.axis_index("x")) * owned
+    first_j = (lax.axis_index(("zh", "zl")) * lax.axis_size("x") + lax.axis_index("x")) * owned
     values = terms_ref[...].reshape(-1, 8, WIDTH)
     ids = ids_ref[...]
     shared_ref[2 * half :] = jnp.zeros((2, WIDTH), F32)
@@ -370,13 +361,8 @@
 
 
 def exchanged(spread):
-    along_x = over_x(swap(spread, "z"))
+    along_x = over_x(swap(spread, ("zh", "zl")))
     return lax.all_gather(along_x.reshape(-1, WIDTH), "c")
-
-
-def shifted(values, places):
-    n = lax.axis_size("x")
-    return lax.ppermute(values, "x", [((i + places) % n, i) for i in range(n)])
 
 
 def shards(
@@ -393,28 +379,26 @@
 ):
     members, blocks, width = reach_residual.shape
     owned = junction_inv.shape[0]
-    zs, xs, ys, cs = (lax.axis_size(a) for a in ("z", "x", "y", "c"))
+    zs, xs, ys, cs = (lax.axis_size(a) for a in (("zh", "zl"), "x", "y", "c"))
     half = members // cs
-    piece = width // (ys * cs)
+    piece = width // ys
     bf16 = jnp.bfloat16
     lower, upper = lower_junction, upper_junction
 
-    own = jnp.stack([lower, upper])[None]
-    beside = shifted(own, 1)
+    plane = over_x(jnp.stack([lower, upper])).reshape(-1)
 
     part = run(
         table_kernel,
-        array(owned, piece + 8, width),
+        array(owned, PACK, width),
         junction_inv, junction_residual, junction_cotangent,
         where=hbm, limit=60,
         scratch=[
-            pltpu.VMEM((owned, piece, width), F32),
             pltpu.VMEM((owned, width), F32),
             pltpu.VMEM((owned, width), F32),
             pltpu.SemaphoreType.DMA((3,)),
         ],
     )
-    table = lax.all_gather(part, "z").reshape(zs * owned, piece + 8, width)
+    near = lax.all_gather(part, "zl").reshape(-1, PACK, width)
 
     chain = (members, blocks, width, width)
     high, low, forced, local = run(
@@ -435,11 +419,15 @@
             pltpu.SemaphoreType.DMA((2 + 2 * members,)),
         ],
     )
-    local, beside = lax.optimization_barrier((local, beside))
-    two = jnp.concatenate([own, beside])
-    plane = jnp.concatenate([two, shifted(two, 2)]).reshape(-1)
     pair = lax.all_gather(local, "c")
-    chips = lax.all_gather(run(pair_kernel, array(half, PACK, width), pair), "y")
+    chip = run(pair_kernel, array(half, PACK, width), pair)
+    sliced = run(
+        slice_kernel, array(near.shape[0], piece + 8, width), near,
+        where=hbm, limit=60, scratch=[pltpu.SemaphoreType.DMA((2,))],
+    )
+    chip, sliced = lax.optimization_barrier((chip, sliced))
+    table = lax.all_gather(sliced, "zh").reshape(zs * owned, piece + 8, width)
+    chips, plane = lax.optimization_barrier((lax.all_gather(chip, "y"), plane))
     matrices = array(2, half, width, width, dtype=bf16)
     schur, before, after, passing, first = run(
         chain_kernel,
@@ -447,14 +435,11 @@
         lower, upper, chips, outlet_link, scalars=2,
     )
 
-    count = zs * 8
-    fetched = 2 * owned * (piece + 8)
-    built = run(
-        build_kernel, array(xs, count + fetched, width), plane, table, swap(first, "z"), scalars=1
-    )
-    merged = run(merge_kernel, array(xs * count + fetched, width), swap(built, "x"))
-    both = lax.all_gather(merged, "c")
-    ends = swap(run(ends_kernel, array(ys, owned, 2 * piece + 8, width), both), "y")
+    picked = run(pick_kernel, array(xs, owned, piece + 8, width), plane, table, scalars=1)
+    merged = run(merge_kernel, array(owned, 3 * piece, width), swap(picked, "x"))
+    first, merged = lax.optimization_barrier((first, merged))
+    ends = lax.all_gather(merged, "y")
+    terms = exchanged(first)
     tiles, ids, rows, spread = run(
         first_step_kernel,
         [
@@ -463,7 +448,7 @@
             array(8, width),
             array(zs, 8, width),
         ],
-        lower, upper, both, ends, schur, first, scalars=2,
+        lower, upper, terms, ends, schur, first, scalars=2,
     )
     terms = exchanged(spread)
     for sweep in range(2, SWEEPS):
@@ -486,9 +471,11 @@
 
 
 def solution(mesh):
-    basins = mesh.shape["basin"]
-    grid = Mesh(mesh.devices.reshape(basins // 4, 4, 4, 2), ("z", "x", "y", "c"))
-    b, r = ("z", "x"), ("y", "c")
+    line = mesh.shape["basin"] // 4
+    near = math.gcd(line, 4)
+    shape = (line // near, near, 4, 4, 2)
+    grid = Mesh(mesh.devices.reshape(shape), ("zh", "zl", "x", "y", "c"))
+    b, r = ("zh", "zl", "x"), ("y", "c")
     return jax.shard_map(
         shards,
         mesh=grid,

time: 228 us -> 314 us (1.38)
  waiting for transfers between devices: 18.1 us -> 115 us
  starting transfers between devices: 21.3 us -> 3.67 us
  blocking collectives: 144 us -> 148 us
    all_gather x1 -> x3, waiting for transfers between devices: 8.57 us -> 110 us  [the longest x1 72.4 us: shards(): table = lax.all_gather(sliced, 'zh').reshape(zs * owned, piece + 8, width)]
    all_gather x2 -> x1, blocking collectives: 24.5 us -> 11.3 us  [shards(): chips, plane = lax.optimization_barrier((lax.all_gather(chip, 'y'), plane))]
    all_to_all x1, starting transfers between devices: 13.8 us -> 3.59 us  [swap(): return lax.all_to_all(spread, axis, 0, 0, tiled=False)]
    all_to_all x8 -> x9, blocking collectives: 95.4 us -> 104 us  [swap(): return lax.all_to_all(spread, axis, 0, 0, tiled=False)]
    ppermute x2 -> x0, starting transfers between devices: 7.51 us -> none  [shifted(): return lax.ppermute(values, 'x', [((i + places) % n, i) for i in range(n)])]
    all_gather x3 -> x4, blocking collectives: 16 us -> 22.2 us  [exchanged(): return lax.all_gather(along_x.reshape(-1, WIDTH), 'c')]
    ppermute x2 -> x0, waiting for transfers between devices: 3.52 us -> none  [shifted(): return lax.ppermute(values, 'x', [((i + places) % n, i) for i in range(n)])]
    all_gather x1, blocking collectives: 5.83 us -> 9.12 us  [shards(): pair = lax.all_gather(local, 'c')]
  transfers between devices with their start and end apart: 4 -> 4, of which waited for: 3 -> 3; matrix products, arithmetic and copies ran while one was open for 0% -> 0% of each run, Pallas kernels for 5% -> 4%
where the time goes in v4:
time: 314 us; the launch traced here: 313 us
  blocking collectives  148 us (47%)
  waiting for transfers between devices  115 us (37%)
  Pallas kernels  29.8 us (9%)
  between operations  13.9 us (4%)
  starting transfers between devices  3.67 us (1%)
    all_to_all x9, blocking collectives, swap(): return lax.all_to_all(spread, axis, 0, 0, tiled=False)  104 us
    all_gather x1, waiting for transfers between devices, shards(): table = lax.all_gather(sliced, 'zh').reshape(zs * owned, piece + 8, width)  72.4 us
    all_gather x1, waiting for transfers between devices, shards(): near = lax.all_gather(part, 'zl').reshape(-1, PACK, width)  37.5 us
    pallas_call x12, Pallas kernels, run(): pl.pallas_call(kernel, out_shape=shapes, in_specs=[smem] * scalars + [whe...  29.8 us
    all_gather x4, blocking collectives, exchanged(): return lax.all_gather(along_x.reshape(-1, WIDTH), 'c')  22.2 us
    all_gather x1, blocking collectives, shards(): chips, plane = lax.optimization_barrier((lax.all_gather(chip, 'y'), plane))  11.3 us
    all_gather x1, blocking collectives, shards(): pair = lax.all_gather(local, 'c')  9.12 us
  transfers between devices with their start and end apart: 4, of which 3 were waited for; matrix products, arithmetic and copies ran while one was open for 0% of the time, Pallas kernels for 4%

profile of v4, /device:TPU:1, one launch (start us, length us, event | category | flops | bytes accessed | tf_op | source)
XLA Modules:
  0.0 313.2 jit_solution(7759564349636949574)
XLA Ops:
  7.2 0.0 all-gather.10.cloned.1.call-start
  7.2 1.8 shard_map.131
  9.0 0.0 all-gather.10.cloned.1.call-update
  9.0 0.0 all-gather.12.cloned.1.call-start
  9.1 7.5 %shard_map.129 = (bf16[6,3,128,128]{3,2,1,0:T(8,128)(2,1)}, bf16[6,3,128,128]{3,2,1,0:T(8,128)(2,1)}, f32[6,3,128]{2,1,0:T(4,128)}, f32[6,136,128]{2,1,0:T(8,128)}) custom-call(f32[6,3,128,128]{3,2,1,0:T(8,128)} %inv_hbm.1, f32[6,3,128,128]{3,2,1,0:T(8,128)} %link_hbm.1, f32[6,3,128]{2,1,0:T(4,128)} %residual_hbm.1, f32[6,3,128]{2,1,0:T(4,128)} %cotangent_ref.5), custom_call_target="tpu_custom_call" | custom-call | flops 2000000000 | bytes 20000000 | tf_op jit(solution)/shard_map/pallas_call | solution.py:27
  16.6 9.1 %all-gather = f32[12,136,128]{2,1,0:T(8,128)S(1)} all-gather(f32[6,136,128]{2,1,0:T(8,128)} %get-tuple-element.28), channel_id=2, replica_groups=mesh['zh'=4,'zl'=4,'x'=4,'y'=4,'c'=2] {'c'}, dimensions={0}, use_global_device_ids=true | all-gather | bytes 1253376 | tf_op jit(solution)/shard_map/all_gather | solution.py:422
  25.7 0.4 shard_map.130
  26.1 0.0 copy-start.6
  26.1 0.0 copy-start.7
  26.1 37.5 %all-gather.10.cloned.1.call-done.near_ref = f32[24,136,128]{2,1,0:T(8,128)} async-done(((f32[6,136,128]{2,1,0:T(8,128)}), f32[24,136,128]{2,1,0:T(8,128)}) %all-gather.10.cloned.1.call-update) | async-done | bytes 1671184 | tf_op jit(solution)/shard_map/all_gather | solution.py:401
  63.6 1.8 shard_map.132
  65.4 0.0 all-gather.12.cloned.1.call-update
  65.5 0.0 copy-done.6
  65.5 0.0 copy-done.7
  65.5 7.9 %all_to_all.50 = s32[4,2,6]{2,1,0:T(2,128)S(1)} all-to-all(s32[4,2,6]{2,1,0:T(2,128)S(1)} %broadcast_in_dim.10), channel_id=1, replica_groups=mesh['zh'=4,'zl'=4,'x'=4,'y'=4,'c'=2] {'x'}, dimensions={0} | all-to-all | bytes 384 | tf_op jit(solution)/shard_map/all_to_all | solution.py:356
  73.4 0.1 reshape.23.ids_ref
  73.5 11.3 %all-gather.2 = f32[12,136,128]{2,1,0:T(8,128)S(1)} all-gather(f32[3,136,128]{2,1,0:T(8,128)S(1)} %shard_map.130), channel_id=4, replica_groups=mesh['zh'=4,'zl'=4,'x'=4,'y'=4,'c'=2] {'y'}, dimensions={0}, use_global_device_ids=true | all-gather | bytes 1044480 | tf_op jit(solution)/shard_map/all_gather | solution.py:430
  84.8 72.4 %all-gather.12.cloned.1.call-done.table_ref = f32[96,40,128]{2,1,0:T(8,128)} async-done(((f32[24,40,128]{2,1,0:T(8,128)}), f32[96,40,128]{2,1,0:T(8,128)}) %all-gather.12.cloned.1.call-update) | async-done | bytes 1966096 | tf_op jit(solution)/shard_map/all_gather | solution.py:429
  157.2 0.0 copy-start
  157.2 1.5 copy-done
  158.8 0.0 copy-start.5
  158.8 1.5 shard_map.134
  160.3 3.6 %all-to-all-start.1 = ((f32[4,6,40,128]{3,2,1,0:T(8,128)}), f32[4,6,40,128]{3,2,1,0:T(8,128)S(1)}, u32[]{:S(2)}, u32[]{:S(2)}) async-start(f32[4,6,40,128]{3,2,1,0:T(8,128)} %shard_map.134), calls=%async_computation.1 | async-start | bytes 983040 | tf_op jit(solution)/shard_map/all_to_all | solution.py:356
  163.9 0.0 all-gather.14.cloned.1.call-start
  163.9 0.0 copy-done.5
  163.9 3.8 %shard_map.133 = (bf16[2,3,128,128]{3,2,1,0:T(8,128)(2,1)S(1)}, bf16[2,3,128,128]{3,2,1,0:T(8,128)(2,1)S(1)}, bf16[2,3,128,128]{3,2,1,0:T(8,128)(2,1)S(1)}, f32[8,128]{1,0:T(8,128)S(1)}, f32[16,8,128]{2,1,0:T(8,128)S(1)}) custom-call(s32[6]{0:T(128)S(1)} %copy-done.6, s32[6]{0:T(128)S(1)} %copy-done.7, f32[4,3,136,128]{3,2,1,0:T(8,128)S(1)} %bitcast.12, ...), custom_call_target="tpu_custom_call" | custom-call | tf_op jit(solution)/shard_map/pallas_call | solution.py:27
  167.7 4.7 %all-to-all-done.1.picked_ref = f32[4,6,40,128]{3,2,1,0:T(8,128)S(1)} async-done(((f32[4,6,40,128]{3,2,1,0:T(8,128)}), f32[4,6,40,128]{3,2,1,0:T(8,128)S(1)}, u32[]{:S(2)}, u32[]{:S(2)}) %all-to-all-start.1) | async-done | bytes 491552 | tf_op jit(solution)/shard_map/all_to_all | solution.py:356
  172.3 0.7 shard_map.135
  173.1 0.0 all-gather.14.cloned.1.call-update
  173.1 16.3 %all_to_all.51 = f32[16,8,128]{2,1,0:T(8,128)S(1)} all-to-all(f32[16,8,128]{2,1,0:T(8,128)S(1)} %get-tuple-element.34.base_ref), channel_id=1, replica_groups=mesh['zh'=4,'zl'=4,'x'=4,'y'=4,'c'=2] {'zh','zl'}, dimensions={0} | all-to-all | bytes 131072 | tf_op jit(solution)/shard_map/all_to_all | solution.py:356
  189.4 8.0 %all_to_all.52 = f32[4,16,8,128]{3,2,1,0:T(8,128)S(1)} all-to-all(f32[4,16,8,128]{3,2,1,0:T(8,128)S(1)} %broadcast_in_dim.11), channel_id=1, replica_groups=mesh['zh'=4,'zl'=4,'x'=4,'y'=4,'c'=2] {'x'}, dimensions={0} | all-to-all | bytes 524288 | tf_op jit(solution)/shard_map/all_to_all | solution.py:356
  197.4 6.1 %all_gather.56.terms_ref = f32[2,512,128]{2,1,0:T(8,128)S(1)} all-gather(f32[1,512,128]{2,1,0:T(8,128)S(1)} %bitcast.17), channel_id=1, replica_groups=mesh['zh'=4,'zl'=4,'x'=4,'y'=4,'c'=2] {'c'}, dimensions={0}, use_global_device_ids=true | all-gather | bytes 786432 | tf_op jit(solution)/shard_map/all_gather | solution.py:365
  203.4 0.0 all-gather.14.cloned.1.call-done
  203.4 0.0 copy-start.2
  203.4 1.3 copy-done.2
  204.7 1.7 shard_map.136
  206.4 17.6 %all_to_all.53 = f32[16,8,128]{2,1,0:T(8,128)S(1)} all-to-all(f32[16,8,128]{2,1,0:T(8,128)S(1)} %get-tuple-element.37), channel_id=1, replica_groups=mesh['zh'=4,'zl'=4,'x'=4,'y'=4,'c'=2] {'zh','zl'}, dimensions={0} | all-to-all | bytes 131072 | tf_op jit(solution)/shard_map/all_to_all | solution.py:356
  224.0 9.3 %all_to_all.54 = f32[4,16,8,128]{3,2,1,0:T(8,128)S(1)} all-to-all(f32[4,16,8,128]{3,2,1,0:T(8,128)S(1)} %broadcast_in_dim.12), channel_id=1, replica_groups=mesh['zh'=4,'zl'=4,'x'=4,'y'=4,'c'=2] {'x'}, dimensions={0} | all-to-all | bytes 524288 | tf_op jit(solution)/shard_map/all_to_all | solution.py:356
  233.3 6.4 %all_gather.59.terms_ref = f32[2,512,128]{2,1,0:T(8,128)S(1)} all-gather(f32[1,512,128]{2,1,0:T(8,128)S(1)} %bitcast.18), channel_id=1, replica_groups=mesh['zh'=4,'zl'=4,'x'=4,'y'=4,'c'=2] {'c'}, dimensions={0}, use_global_device_ids=true | all-gather | bytes 786432 | tf_op jit(solution)/shard_map/all_gather | solution.py:365
  239.7 1.7 shard_map.137
  241.4 14.3 %all_to_all.55 = f32[16,8,128]{2,1,0:T(8,128)S(1)} all-to-all(f32[16,8,128]{2,1,0:T(8,128)S(1)} %shard_map.137), channel_id=1, replica_groups=mesh['zh'=4,'zl'=4,'x'=4,'y'=4,'c'=2] {'zh','zl'}, dimensions={0} | all-to-all | bytes 131072 | tf_op jit(solution)/shard_map/all_to_all | solution.py:356
  255.7 7.9 %all_to_all.56 = f32[4,16,8,128]{3,2,1,0:T(8,128)S(1)} all-to-all(f32[4,16,8,128]{3,2,1,0:T(8,128)S(1)} %broadcast_in_dim.13), channel_id=1, replica_groups=mesh['zh'=4,'zl'=4,'x'=4,'y'=4,'c'=2] {'x'}, dimensions={0} | all-to-all | bytes 524288 | tf_op jit(solution)/shard_map/all_to_all | solution.py:356
  263.6 4.9 %all_gather.60.terms_ref = f32[2,512,128]{2,1,0:T(8,128)S(1)} all-gather(f32[1,512,128]{2,1,0:T(8,128)S(1)} %bitcast.19), channel_id=1, replica_groups=mesh['zh'=4,'zl'=4,'x'=4,'y'=4,'c'=2] {'c'}, dimensions={0}, use_global_device_ids=true | all-gather | bytes 786432 | tf_op jit(solution)/shard_map/all_gather | solution.py:365
  268.5 1.7 shard_map.138
  270.1 0.0 copy-start.1
  270.1 0.0 copy-start.8
  270.2 0.0 copy-start.9
  270.2 14.5 %all_to_all.57 = f32[16,8,128]{2,1,0:T(8,128)S(1)} all-to-all(f32[16,8,128]{2,1,0:T(8,128)S(1)} %shard_map.138), channel_id=1, replica_groups=mesh['zh'=4,'zl'=4,'x'=4,'y'=4,'c'=2] {'zh','zl'}, dimensions={0} | all-to-all | bytes 131072 | tf_op jit(solution)/shard_map/all_to_all | solution.py:356
  284.7 7.9 %all_to_all.58 = f32[4,16,8,128]{3,2,1,0:T(8,128)S(1)} all-to-all(f32[4,16,8,128]{3,2,1,0:T(8,128)S(1)} %broadcast_in_dim.14), channel_id=1, replica_groups=mesh['zh'=4,'zl'=4,'x'=4,'y'=4,'c'=2] {'x'}, dimensions={0} | all-to-all | bytes 524288 | tf_op jit(solution)/shard_map/all_to_all | solution.py:356
  292.6 4.9 %all_gather.61.terms_ref = f32[2,512,128]{2,1,0:T(8,128)S(1)} all-gather(f32[1,512,128]{2,1,0:T(8,128)S(1)} %bitcast.20), channel_id=1, replica_groups=mesh['zh'=4,'zl'=4,'x'=4,'y'=4,'c'=2] {'c'}, dimensions={0}, use_global_device_ids=true | all-gather | bytes 786432 | tf_op jit(solution)/shard_map/all_gather | solution.py:365
  297.5 0.0 copy-start.3
  297.5 0.0 copy-start.4
  297.5 0.0 copy-start.10
  297.5 0.0 copy-start.11
  297.5 0.0 copy-done.1
  297.6 0.0 copy-done.8
  297.6 0.0 copy-done.9
  297.6 2.6 shard_map.139
  300.1 1.9 all-gather.5
  302.0 0.0 copy-done.3
  302.0 0.0 copy-done.4
  302.0 0.0 copy-done.10
  302.0 0.0 copy-done.11
  302.0 4.7 %shard_map.140 = (f32[6,3,128]{2,1,0:T(4,128)}, f32[6,3,128]{2,1,0:T(4,128)}) custom-call(f32[2,8,128]{2,1,0:T(8,128)S(1)} %bitcast.14, f32[2,6,136,128]{3,2,1,0:T(8,128)S(1)} %bitcast.11, bf16[6,3,128,128]{3,2,1,0:T(8,128)(2,1)S(1)} %copy-done.3, bf16[6,3,128,128]{3,2,1,0:T(8,128)(2,1)S(1)} %copy-done.4, f32[6,3,128]{2,1,0:T(4,128)S(1)} %copy-done.11, ...), custom_call_target="tpu_custom_call" | custom-call | tf_op jit(solution)/shard_map/pallas_call | solution.py:27
  (6 shorter events, 0.1 us)
Async XLA Ops:
  7.2 56.5 %all-gather.10.cloned.1.call-start = ((), (), s32[]{:S(2)}) async-start(), calls=%async_computation.10 | async-start | bytes 2088960 | tf_op jit(solution)/shard_map/all_gather | solution.py:401
  9.0 148.2 %all-gather.12.cloned.1.call-start = ((), (), s32[]{:S(2)}) async-start(), calls=%async_computation.11 | async-start | bytes 2457600 | tf_op jit(solution)/shard_map/all_gather | solution.py:429
  26.1 39.3 %copy-start.6 = (s32[6]{0:T(128)S(1)}, s32[6]{0:T(128)}, u32[]{:S(2)}) copy-start(s32[6]{0:T(128)} %lower_ref.9) | copy-start | bytes 76
  26.1 39.3 %copy-start.7 = (s32[6]{0:T(128)S(1)}, s32[6]{0:T(128)}, u32[]{:S(2)}) copy-start(s32[6]{0:T(128)} %upper_ref.9) | copy-start | bytes 76
  157.2 1.5 copy-start
  158.8 5.1 %copy-start.5 = (f32[6,128,128]{2,1,0:T(8,128)S(1)}, f32[6,128,128]{2,1,0:T(8,128)}, u32[]{:S(2)}) copy-start(f32[6,128,128]{2,1,0:T(8,128)} %outlet_ref.1) | copy-start | bytes 1179652
  160.3 12.1 %all-to-all-start.1 = ((f32[4,6,40,128]{3,2,1,0:T(8,128)}), f32[4,6,40,128]{3,2,1,0:T(8,128)S(1)}, u32[]{:S(2)}, u32[]{:S(2)}) async-start(f32[4,6,40,128]{3,2,1,0:T(8,128)} %shard_map.134), calls=%async_computation.1 | async-start | bytes 983040 | tf_op jit(solution)/shard_map/all_to_all | solution.py:356
  163.9 39.6 %all-gather.14.cloned.1.call-start = ((), (), s32[]{:S(2)}) async-start(), calls=%async_computation.12 | async-start | bytes 1474560 | tf_op jit(solution)/shard_map/all_gather | solution.py:441
  203.4 1.3 copy-start.2
  270.1 27.4 %copy-start.1 = (f32[6,128,128]{2,1,0:T(8,128)S(1)}, f32[6,128,128]{2,1,0:T(8,128)}, u32[]{:S(2)}) copy-start(f32[6,128,128]{2,1,0:T(8,128)} %inv_ref.3) | copy-start | bytes 1179652
  270.1 27.4 %copy-start.8 = (f32[6,128]{1,0:T(8,128)S(1)}, f32[6,128]{1,0:T(8,128)}, u32[]{:S(2)}) copy-start(f32[6,128]{1,0:T(8,128)} %residual_ref.3) | copy-start | bytes 9220
  270.2 27.4 %copy-start.9 = (f32[6,128]{1,0:T(8,128)S(1)}, f32[6,128]{1,0:T(8,128)}, u32[]{:S(2)}) copy-start(f32[6,128]{1,0:T(8,128)} %cotangent_ref.4) | copy-start | bytes 9220
  297.5 4.5 %copy-start.3 = (bf16[6,3,128,128]{3,2,1,0:T(8,128)(2,1)S(1)}, bf16[6,3,128,128]{3,2,1,0:T(8,128)(2,1)}, u32[]{:S(2)}) copy-start(bf16[6,3,128,128]{3,2,1,0:T(8,128)(2,1)} %get-tuple-element.45.high_ref) | copy-start | bytes 1769476
  297.5 4.5 %copy-start.4 = (bf16[6,3,128,128]{3,2,1,0:T(8,128)(2,1)S(1)}, bf16[6,3,128,128]{3,2,1,0:T(8,128)(2,1)}, u32[]{:S(2)}) copy-start(bf16[6,3,128,128]{3,2,1,0:T(8,128)(2,1)} %get-tuple-element.46.low_ref) | copy-start | bytes 1769476
  297.5 4.5 %copy-start.10 = (f32[6,3,128]{2,1,0:T(4,128)S(1)}, f32[6,3,128]{2,1,0:T(4,128)}, u32[]{:S(2)}) copy-start(f32[6,3,128]{2,1,0:T(4,128)} %cotangent_ref.5) | copy-start | bytes 27652
  297.5 4.5 %copy-start.11 = (f32[6,3,128]{2,1,0:T(4,128)S(1)}, f32[6,3,128]{2,1,0:T(4,128)}, u32[]{:S(2)}) copy-start(f32[6,3,128]{2,1,0:T(4,128)} %get-tuple-element.47.forced_ref) | copy-start | bytes 27652
Sparse Core Ops, SparseCore 0:
  10.1 53.4 all-gather.9
  65.7 91.4 all-gather.11
  173.2 24.3 all-gather.13

commit v5 on v4

--- a/solution.py
+++ b/solution.py
@@ -1,5 +1,3 @@
-import math
-
 import jax
 import jax.numpy as jnp
 from jax import lax
@@ -58,7 +56,8 @@
 def along(vector, matrix, transposed):
     vh, vl = two_parts(vector)
     mh, ml = parts_of(matrix)
-    return dot(vh, mh, transposed) + (dot(vl, mh, transposed) + dot(vh, ml, transposed))
+    both = dot(jnp.concatenate([vh, vl]), mh, transposed)
+    return both[0:1] + (both[1:2] + dot(vh, ml, transposed))
 
 
 def applied(matrix, row):
@@ -77,35 +76,23 @@
 
 
 def table_kernel(inv_ref, residual_ref, cotangent_ref, out_ref, residual, cotangent, sems):
+    piece = out_ref.shape[1] - 8
+    start = pl.multiple_of(lax.axis_index("y") * piece, 8)
     copies = fetch(
         [
-            (inv_ref, out_ref.at[:, :WIDTH]),
+            (inv_ref.at[:, pl.ds(start, piece)], out_ref.at[:, :piece]),
             (residual_ref, residual),
             (cotangent_ref, cotangent),
         ],
         sems,
     )
-    copies[1].wait()
-    copies[2].wait()
+    for copy in copies[1:]:
+        copy.wait()
     for k in range(out_ref.shape[0]):
-        out_ref[k, WIDTH:] = jnp.concatenate(
+        out_ref[k, piece:] = jnp.concatenate(
             [residual[k : k + 1], cotangent[k : k + 1], jnp.zeros((6, WIDTH), F32)]
         )
     copies[0].wait()
-
-
-def slice_kernel(near_ref, out_ref, sems):
-    piece = out_ref.shape[1] - 8
-    start = pl.multiple_of(lax.axis_index("y") * piece, 8)
-    copies = fetch(
-        [
-            (near_ref.at[:, pl.ds(start, piece)], out_ref.at[:, :piece]),
-            (near_ref.at[:, WIDTH:], out_ref.at[:, piece:]),
-        ],
-        sems,
-    )
-    for copy in copies:
-        copy.wait()
 
 
 def local_kernel(
@@ -142,20 +129,25 @@
         )
 
 
-def pair_kernel(pair_ref, out_ref):
+def pair_kernel(pair_ref, out_ref, other_ref, rows_ref):
     half = out_ref.shape[0]
-    first_s = lax.axis_index("c") * half
+    c = lax.axis_index("c")
+    first_s = c * half
     for k in range(half):
         first, second = pair_ref[0, first_s + k], pair_ref[1, first_s + k]
         one, two = two_parts(first[:WIDTH]), two_parts(second[:WIDTH])
         out_ref[k, :WIDTH] = product(two, one)
-        out_ref[k, WIDTH : WIDTH + 1] = (
-            applied(two, first[WIDTH : WIDTH + 1]) + second[WIDTH : WIDTH + 1]
-        )
-        out_ref[k, WIDTH + 1 : WIDTH + 2] = (
-            applied_transposed(one, second[WIDTH + 1 : WIDTH + 2]) + first[WIDTH + 1 : WIDTH + 2]
-        )
-        out_ref[k, WIDTH + 2 :] = jnp.zeros((6, WIDTH), F32)
+        out_ref[k, WIDTH:] = jnp.concatenate(
+            [
+                applied(two, first[WIDTH : WIDTH + 1]) + second[WIDTH : WIDTH + 1],
+                applied_transposed(one, second[WIDTH + 1 : WIDTH + 2])
+                + first[WIDTH + 1 : WIDTH + 2],
+                jnp.zeros((6, WIDTH), F32),
+            ]
+        )
+    for s in range(other_ref.shape[1]):
+        keep(other_ref, s, pair_ref[1 - c, s, :WIDTH])
+        rows_ref[s] = pair_ref[1 - c, s, WIDTH:]
 
 
 def keep(ref, k, matrix):
@@ -212,29 +204,25 @@
         spread_ref[i] = full
 
 
-def pick_kernel(ids_ref, table_ref, out_ref):
+def pick_kernel(ids_ref, table_ref, out_ref, sems):
     dests, owned = out_ref.shape[:2]
     half = owned // 2
     x = lax.axis_index("x")
-    first_s = lax.axis_index("c") * half
+    pairs, here = [], []
     for d in range(dests):
         for t in range(owned):
-            side, k = (1, t) if t < half else (0, t - half)
-            junction = ids_ref[(2 * d + side) * owned + first_s + k]
+            junction = ids_ref[d * owned + (t + half) % owned]
             basin = lax.div(junction, owned)
             line = lax.div(basin, dests)
             at = line * owned + (junction - basin * owned)
-            here = basin - line * dests == x
-            out_ref[d, t] = jnp.where(here, table_ref[at], 0.0)
-
-
-def merge_kernel(picked_ref, out_ref):
-    total = picked_ref[0]
-    for d in range(1, picked_ref.shape[0]):
-        total = total + picked_ref[d]
-    rows = picked_ref.shape[2]
-    out_ref[:, :rows] = total
-    out_ref[:, rows:] = jnp.zeros((out_ref.shape[0], out_ref.shape[1] - rows, WIDTH), F32)
+            here.append(basin - line * dests == x)
+            pairs.append((table_ref.at[at], out_ref.at[d, t]))
+    copies = fetch(pairs, sems)
+    for copy in copies:
+        copy.wait()
+    for d in range(dests):
+        for t in range(owned):
+            out_ref[d, t] = jnp.where(here[d * owned + t], out_ref[d, t], 0.0)
 
 
 def rule(above, below, half):
@@ -249,6 +237,12 @@
         inflow = inflow + total[k : k + 1]
         outflow = outflow + total[half + k : half + k + 1]
     return inflow, outflow
+
+
+def spread_rows(payload, spread_ref):
+    full = jnp.concatenate(payload)
+    for i in range(spread_ref.shape[0]):
+        spread_ref[i] = full
 
 
 def step(lower_ref, upper_ref, ids, values, tiles, schur_ref, ends, base, spread_ref):
@@ -265,16 +259,14 @@
         schur = kept(schur_ref, k)
         payload[k] = base[k : k + 1] + applied(schur, head)
         payload[half + k] = base[half + k : half + k + 1] + applied_transposed(schur, relief)
-    full = jnp.concatenate(payload)
-    for i in range(spread_ref.shape[0]):
-        spread_ref[i] = full
-
-
-def first_step_kernel(
-    lower_ref, upper_ref, terms_ref, ends_ref, schur_ref, base_ref, tiles_ref, ids_ref, rows_ref, spread_ref
-):
-    half = schur_ref.shape[1]
-    piece = WIDTH // ends_ref.shape[0]
+    spread_rows(payload, spread_ref)
+
+
+def partial_kernel(lower_ref, upper_ref, terms_ref, picked_ref, ids_ref, rows_ref, merged_ref, spread_ref, tile_ref):
+    half = picked_ref.shape[1] // 2
+    piece = WIDTH // spread_ref.shape[0]
+    first_s = lax.axis_index("c") * half
+    start = pl.multiple_of(lax.axis_index("y") * piece, 8)
     row = lax.broadcasted_iota(jnp.int32, (8, WIDTH), 0)
     lane = lax.broadcasted_iota(jnp.int32, (8, WIDTH), 1)
     values = terms_ref[...].reshape(-1, 8, WIDTH)
@@ -282,13 +274,53 @@
     ids = jnp.sum(chosen, axis=2, keepdims=True).astype(jnp.int32)
     ids = jnp.broadcast_to(ids, values.shape)
     ids_ref[...] = ids
-    for k in range(2 * half):
+    merged = picked_ref[0]
+    for d in range(1, picked_ref.shape[0]):
+        merged = merged + picked_ref[d]
+    merged_ref[:, : piece + 8] = merged
+    merged_ref[:, piece + 8 :] = jnp.zeros(
+        (2 * half, merged_ref.shape[1] - piece - 8, WIDTH), F32
+    )
+    tile_ref[...] = jnp.zeros(tile_ref.shape, F32)
+    payload = [jnp.zeros((1, WIDTH), F32)] * 8
+    ends = [jnp.zeros((1, WIDTH), F32)] * 8
+    for k in range(half):
+        pattern = rule(upper_ref[first_s + k], lower_ref[first_s + k], half)
+        inflow, outflow = gathered(ids, values, pattern, half)
+        ends[k] = merged[k, piece : piece + 1]
+        ends[half + k] = merged[half + k, piece + 1 : piece + 2]
+        tile_ref[k, pl.ds(start, piece)] = merged[k, :piece]
+        tile_ref[half + k, pl.ds(start, piece)] = merged[half + k, :piece]
+        payload[k] = applied(tile_ref[k], ends[k] + inflow)
+        payload[half + k] = applied_transposed(tile_ref[half + k], ends[half + k] + outflow)
+    rows_ref[...] = jnp.concatenate(ends)
+    spread_rows(payload, spread_ref)
+
+
+def second_kernel(parts_ref, schur_ref, base_ref, spread_ref):
+    half = schur_ref.shape[1]
+    total = parts_ref[0]
+    for i in range(1, parts_ref.shape[0]):
+        total = total + parts_ref[i]
+    base = base_ref[0]
+    payload = [jnp.zeros((1, WIDTH), F32)] * 8
+    for k in range(half):
+        schur = kept(schur_ref, k)
+        payload[k] = base[k : k + 1] + applied(schur, total[k : k + 1])
+        payload[half + k] = base[half + k : half + k + 1] + applied_transposed(
+            schur, total[half + k : half + k + 1]
+        )
+    spread_rows(payload, spread_ref)
+
+
+def third_kernel(
+    lower_ref, upper_ref, terms_ref, ids_ref, ends_ref, schur_ref, rows_ref, base_ref, tiles_ref, spread_ref
+):
+    piece = WIDTH // ends_ref.shape[0]
+    for k in range(tiles_ref.shape[1]):
         keep(tiles_ref, k, jnp.concatenate([ends_ref[i, k, :piece] for i in range(ends_ref.shape[0])]))
-    ends = [ends_ref[0, k, piece : piece + 1] for k in range(half)]
-    ends += [ends_ref[0, half + k, piece + 1 : piece + 2] for k in range(half)]
-    ends = jnp.concatenate(ends + [jnp.zeros((2, WIDTH), F32)])
-    rows_ref[...] = ends
-    step(lower_ref, upper_ref, ids, values, tiles_ref, schur_ref, ends, base_ref[0], spread_ref)
+    values = terms_ref[...].reshape(-1, 8, WIDTH)
+    step(lower_ref, upper_ref, ids_ref[...], values, tiles_ref, schur_ref, rows_ref[...], base_ref[0], spread_ref)
 
 
 def step_kernel(
@@ -305,7 +337,7 @@
     half = before_ref.shape[1]
     owned = inv_ref.shape[0]
     first_s = lax.axis_index("c") * half
-    first_j = (lax.axis_index(("zh", "zl")) * lax.axis_size("x") + lax.axis_index("x")) * owned
+    first_j = (lax.axis_index("z") * lax.axis_size("x") + lax.axis_index("x")) * owned
     values = terms_ref[...].reshape(-1, 8, WIDTH)
     ids = ids_ref[...]
     shared_ref[2 * half :] = jnp.zeros((2, WIDTH), F32)
@@ -326,7 +358,7 @@
         adjoint_ref[k : k + 1] = cotangent_ref[k : k + 1] + outflow
 
 
-def cells_kernel(shared_ref, pair_ref, high_ref, low_ref, forced_ref, cotangent_ref, update_ref, adjoint_ref):
+def cells_kernel(shared_ref, other_ref, passing_ref, high_ref, low_ref, forced_ref, cotangent_ref, update_ref, adjoint_ref):
     members, blocks = high_ref.shape[:2]
     half = members // 2
     c = lax.axis_index("c")
@@ -334,10 +366,9 @@
         core, k = s // half, s % half
         enter = shared_ref[core, k : k + 1]
         leave = shared_ref[core, half + k : half + k + 1]
-        other = pair_ref[1 - c, s]
-        matrix = two_parts(other[:WIDTH])
-        further = applied(matrix, enter) + other[WIDTH : WIDTH + 1]
-        nearer = applied_transposed(matrix, leave) + other[WIDTH + 1 : WIDTH + 2]
+        matrix = kept(other_ref, s)
+        further = applied(matrix, enter) + passing_ref[s, 0:1]
+        nearer = applied_transposed(matrix, leave) + passing_ref[s, 1:2]
         enter = jnp.where(c == 1, further, enter)
         leave = jnp.where(c == 0, nearer, leave)
         for i in range(blocks):
@@ -361,7 +392,7 @@
 
 
 def exchanged(spread):
-    along_x = over_x(swap(spread, ("zh", "zl")))
+    along_x = over_x(swap(spread, "z"))
     return lax.all_gather(along_x.reshape(-1, WIDTH), "c")
 
 
@@ -379,17 +410,15 @@
 ):
     members, blocks, width = reach_residual.shape
     owned = junction_inv.shape[0]
-    zs, xs, ys, cs = (lax.axis_size(a) for a in (("zh", "zl"), "x", "y", "c"))
+    zs, xs, ys, cs = (lax.axis_size(a) for a in ("z", "x", "y", "c"))
     half = members // cs
     piece = width // ys
     bf16 = jnp.bfloat16
     lower, upper = lower_junction, upper_junction
 
-    plane = over_x(jnp.stack([lower, upper])).reshape(-1)
-
     part = run(
         table_kernel,
-        array(owned, PACK, width),
+        array(owned, piece + 8, width),
         junction_inv, junction_residual, junction_cotangent,
         where=hbm, limit=60,
         scratch=[
@@ -398,7 +427,7 @@
             pltpu.SemaphoreType.DMA((3,)),
         ],
     )
-    near = lax.all_gather(part, "zl").reshape(-1, PACK, width)
+    table = lax.all_gather(part, "z").reshape(zs * owned, piece + 8, width)
 
     chain = (members, blocks, width, width)
     high, low, forced, local = run(
@@ -420,14 +449,12 @@
         ],
     )
     pair = lax.all_gather(local, "c")
-    chip = run(pair_kernel, array(half, PACK, width), pair)
-    sliced = run(
-        slice_kernel, array(near.shape[0], piece + 8, width), near,
-        where=hbm, limit=60, scratch=[pltpu.SemaphoreType.DMA((2,))],
-    )
-    chip, sliced = lax.optimization_barrier((chip, sliced))
-    table = lax.all_gather(sliced, "zh").reshape(zs * owned, piece + 8, width)
-    chips, plane = lax.optimization_barrier((lax.all_gather(chip, "y"), plane))
+    chip, other, other_rows = run(
+        pair_kernel,
+        [array(half, PACK, width), array(2, members, width, width, dtype=bf16), array(members, 8, width)],
+        pair,
+    )
+    chips = lax.all_gather(chip, "y")
     matrices = array(2, half, width, width, dtype=bf16)
     schur, before, after, passing, first = run(
         chain_kernel,
@@ -435,23 +462,37 @@
         lower, upper, chips, outlet_link, scalars=2,
     )
 
-    picked = run(pick_kernel, array(xs, owned, piece + 8, width), plane, table, scalars=1)
-    merged = run(merge_kernel, array(owned, 3 * piece, width), swap(picked, "x"))
-    first, merged = lax.optimization_barrier((first, merged))
-    ends = lax.all_gather(merged, "y")
     terms = exchanged(first)
-    tiles, ids, rows, spread = run(
-        first_step_kernel,
+    plane = lax.dynamic_slice(
+        terms.reshape(cs, xs, zs, 8, width),
+        (lax.axis_index("c"), 0, lax.axis_index("z"), 2 * half, 0),
+        (1, xs, 1, 1, owned),
+    ).reshape(-1).astype(jnp.int32)
+    picked = run(
+        pick_kernel, array(xs, owned, piece + 8, width), plane, table,
+        scalars=1, where=hbm, limit=60, scratch=[pltpu.SemaphoreType.DMA((xs * owned,))],
+    )
+    ids, rows, merged, parts = run(
+        partial_kernel,
         [
-            array(2, 2 * half, width, width, dtype=bf16),
             array(cs * xs * zs, 8, width, dtype=jnp.int32),
             array(8, width),
-            array(zs, 8, width),
+            array(owned, 3 * piece, width),
+            array(ys, 8, width),
         ],
-        lower, upper, terms, ends, schur, first, scalars=2,
+        lower, upper, terms, swap(picked, "x"), scalars=2,
+        scratch=[pltpu.VMEM((owned, width, width), F32)],
+    )
+    parts, merged = lax.optimization_barrier((parts, merged))
+    ends = lax.all_gather(merged, "y")
+    terms = exchanged(run(second_kernel, array(zs, 8, width), swap(parts, "y"), schur, first))
+    tiles, spread = run(
+        third_kernel,
+        [array(2, 2 * half, width, width, dtype=bf16), array(zs, 8, width)],
+        lower, upper, terms, ids, ends, schur, rows, first, scalars=2,
     )
     terms = exchanged(spread)
-    for sweep in range(2, SWEEPS):
+    for sweep in range(3, SWEEPS):
         spread = run(
             step_kernel, array(zs, 8, width), lower, upper, terms, ids, tiles, schur, rows, first, scalars=2
         )
@@ -465,17 +506,15 @@
     cell_update, cell_adjoint = run(
         cells_kernel,
         [array(members, blocks, width), array(members, blocks, width)],
-        lax.all_gather(shared, "c"), pair, high, low, forced, cell_cotangent,
+        lax.all_gather(shared, "c"), other, other_rows, high, low, forced, cell_cotangent,
     )
     return (cell_update, sections, cell_adjoint, adjoint)
 
 
 def solution(mesh):
-    line = mesh.shape["basin"] // 4
-    near = math.gcd(line, 4)
-    shape = (line // near, near, 4, 4, 2)
-    grid = Mesh(mesh.devices.reshape(shape), ("zh", "zl", "x", "y", "c"))
-    b, r = ("zh", "zl", "x"), ("y", "c")
+    basins = mesh.shape["basin"]
+    grid = Mesh(mesh.devices.reshape(basins // 4, 4, 4, 2), ("z", "x", "y", "c"))
+    b, r = ("z", "x"), ("y", "c")
     return jax.shard_map(
         shards,
         mesh=grid,

time: 314 us -> 222 us (0.71)
  waiting for transfers between devices: 115 us -> 6.26 us
  blocking collectives: 148 us -> 168 us
  Pallas kernels: 29.8 us -> 26.1 us
    all_gather x2 -> x1, waiting for transfers between devices: 110 us -> 0.7 us  [shards(): table = lax.all_gather(part, 'z').reshape(zs * owned, piece + 8, width)]
    all_gather x4, blocking collectives: 22.2 us -> 34.8 us  [exchanged(): return lax.all_gather(along_x.reshape(-1, WIDTH), 'c')]
    all_to_all x9, blocking collectives: 104 us -> 111 us  [swap(): return lax.all_to_all(spread, axis, 0, 0, tiled=False)]
    pallas_call x12 -> x11, Pallas kernels: 29.8 us -> 26.1 us  [run(): pl.pallas_call(kernel, out_shape=shapes, in_specs=[smem] * scalars + [whe...]
  transfers between devices with their start and end apart: 4 -> 3, of which waited for: 3 -> 2; matrix products, arithmetic and copies ran while one was open for 0% -> 1% of each run, Pallas kernels for 4% -> 5%
where the time goes in v5:
time: 222 us; the launch traced here: 221 us
  blocking collectives  168 us (76%)
  Pallas kernels  26.1 us (12%)
  between operations  14.2 us (6%)
  waiting for transfers between devices  6.26 us (3%)
  starting transfers between devices  3.84 us (2%)
  local copies, waits for them, and re-layouts  2.68 us (1%)
    all_to_all x9, blocking collectives, swap(): return lax.all_to_all(spread, axis, 0, 0, tiled=False)  111 us
    all_gather x4, blocking collectives, exchanged(): return lax.all_gather(along_x.reshape(-1, WIDTH), 'c')  34.8 us
    pallas_call x11, Pallas kernels, run(): pl.pallas_call(kernel, out_shape=shapes, in_specs=[smem] * scalars + [whe...  26.1 us
    all_gather x1, blocking collectives, shards(): chips = lax.all_gather(chip, 'y')  11.1 us
    all_gather x1, blocking collectives, shards(): pair = lax.all_gather(local, 'c')  9.12 us
    all_to_all x1, waiting for transfers between devices, swap(): return lax.all_to_all(spread, axis, 0, 0, tiled=False)  5.53 us
  transfers between devices with their start and end apart: 3, of which 2 were waited for; matrix products, arithmetic and copies ran while one was open for 1% of the time, Pallas kernels for 5%

profile of v5, /device:TPU:1, one launch (start us, length us, event | category | flops | bytes accessed | tf_op | source)
XLA Modules:
  0.0 221.3 jit_solution(9207273057080845051)
XLA Ops:
  7.2 0.0 all-gather.8.cloned.1.call-start
  7.2 1.6 shard_map.132
  8.8 0.0 all-gather.8.cloned.1.call-update
  8.8 6.9 %shard_map.129 = (bf16[6,3,128,128]{3,2,1,0:T(8,128)(2,1)}, bf16[6,3,128,128]{3,2,1,0:T(8,128)(2,1)}, f32[6,3,128]{2,1,0:T(4,128)}, f32[6,136,128]{2,1,0:T(8,128)}) custom-call(f32[6,3,128,128]{3,2,1,0:T(8,128)} %inv_hbm.1, f32[6,3,128,128]{3,2,1,0:T(8,128)} %link_hbm.1, f32[6,3,128]{2,1,0:T(4,128)} %residual_hbm.1, f32[6,3,128]{2,1,0:T(4,128)} %cotangent_ref.5), custom_call_target="tpu_custom_call" | custom-call | flops 2000000000 | bytes 20000000 | tf_op jit(solution)/shard_map/pallas_call | solution.py:25
  15.8 9.1 %all-gather = f32[12,136,128]{2,1,0:T(8,128)S(1)} all-gather(f32[6,136,128]{2,1,0:T(8,128)} %get-tuple-element.29), channel_id=2, replica_groups=mesh['z'=16,'x'=4,'y'=4,'c'=2] {'c'}, dimensions={0}, use_global_device_ids=true | all-gather | bytes 1253376 | tf_op jit(solution)/shard_map/all_gather | solution.py:451
  24.9 0.0 copy-start.4
  24.9 0.0 copy-start.7
  24.9 0.0 copy-start.8
  24.9 0.4 shard_map.130
  25.3 11.1 %all-gather.1 = f32[12,136,128]{2,1,0:T(8,128)S(1)} all-gather(f32[3,136,128]{2,1,0:T(8,128)S(1)} %get-tuple-element.30), channel_id=3, replica_groups=mesh['z'=16,'x'=4,'y'=4,'c'=2] {'y'}, dimensions={0}, use_global_device_ids=true | all-gather | bytes 1044480 | tf_op jit(solution)/shard_map/all_gather | solution.py:457
  36.4 0.0 copy-done.4
  36.4 0.0 copy-done.7
  36.4 0.0 copy-done.8
  36.4 3.7 %shard_map.131 = (bf16[2,3,128,128]{3,2,1,0:T(8,128)(2,1)S(1)}, bf16[2,3,128,128]{3,2,1,0:T(8,128)(2,1)S(1)}, bf16[2,3,128,128]{3,2,1,0:T(8,128)(2,1)S(1)}, f32[8,128]{1,0:T(8,128)S(1)}, f32[16,8,128]{2,1,0:T(8,128)S(1)}) custom-call(s32[6]{0:T(128)S(1)} %copy-done.7, s32[6]{0:T(128)S(1)} %copy-done.8, f32[4,3,136,128]{3,2,1,0:T(8,128)S(1)} %bitcast.12, ...), custom_call_target="tpu_custom_call" | custom-call | tf_op jit(solution)/shard_map/pallas_call | solution.py:25
  40.1 22.5 %all_to_all.50 = f32[16,8,128]{2,1,0:T(8,128)S(1)} all-to-all(f32[16,8,128]{2,1,0:T(8,128)S(1)} %get-tuple-element.31.base_ref), channel_id=1, replica_groups=mesh['z'=16,'x'=4,'y'=4,'c'=2] {'z'}, dimensions={0} | all-to-all | bytes 131072 | tf_op jit(solution)/shard_map/all_to_all | solution.py:387
  62.6 0.7 broadcast_in_dim.8
  63.4 3.8 %all-to-all-start.1 = ((f32[4,16,8,128]{3,2,1,0:T(8,128)}), f32[4,16,8,128]{3,2,1,0:T(8,128)S(1)}, u32[]{:S(2)}, u32[]{:S(2)}) async-start(f32[4,16,8,128]{3,2,1,0:T(8,128)} %broadcast_in_dim.8), calls=%async_computation.1 | async-start | bytes 524288 | tf_op jit(solution)/shard_map/all_to_all | solution.py:387
  67.2 0.0 all-gather.10.cloned.1.call-start
  67.2 5.5 %all-to-all-done.1 = f32[4,16,8,128]{3,2,1,0:T(8,128)S(1)} async-done(((f32[4,16,8,128]{3,2,1,0:T(8,128)}), f32[4,16,8,128]{3,2,1,0:T(8,128)S(1)}, u32[]{:S(2)}, u32[]{:S(2)}) %all-to-all-start.1) | async-done | bytes 262176 | tf_op jit(solution)/shard_map/all_to_all | solution.py:387
  72.7 7.0 %all_gather.46.terms_ref = f32[2,512,128]{2,1,0:T(8,128)S(1)} all-gather(f32[1,512,128]{2,1,0:T(8,128)S(1)} %bitcast.17), channel_id=1, replica_groups=mesh['z'=16,'x'=4,'y'=4,'c'=2] {'c'}, dimensions={0}, use_global_device_ids=true | all-gather | bytes 786432 | tf_op jit(solution)/shard_map/all_gather | solution.py:396
  79.7 0.6 convert_element_type.6.ids_ref
  80.2 0.7 all-gather.8.cloned.1.call-done.table_ref
  81.0 2.7 %shard_map.133 = f32[4,6,40,128]{3,2,1,0:T(8,128)} custom-call(s32[24]{0:T(128)} %convert_element_type.6.ids_ref, f32[96,40,128]{2,1,0:T(8,128)} %all-gather.8.cloned.1.call-done.table_ref), custom_call_target="tpu_custom_call" | custom-call | tf_op jit(solution)/shard_map/pallas_call | solution.py:25
  83.7 10.4 %all_to_all.51.picked_ref = f32[4,6,40,128]{3,2,1,0:T(8,128)S(1)} all-to-all(f32[4,6,40,128]{3,2,1,0:T(8,128)} %shard_map.133), channel_id=1, replica_groups=mesh['z'=16,'x'=4,'y'=4,'c'=2] {'x'}, dimensions={0} | all-to-all | bytes 983040 | tf_op jit(solution)/shard_map/all_to_all | solution.py:387
  94.0 1.6 shard_map.134
  95.7 0.0 all-gather.10.cloned.1.call-update
  95.7 8.3 %all_to_all.52.parts_ref = f32[4,8,128]{2,1,0:T(8,128)S(1)} all-to-all(f32[4,8,128]{2,1,0:T(8,128)S(1)} %get-tuple-element.34), channel_id=1, replica_groups=mesh['z'=16,'x'=4,'y'=4,'c'=2] {'y'}, dimensions={0} | all-to-all | bytes 32768 | tf_op jit(solution)/shard_map/all_to_all | solution.py:387
  103.9 0.3 shard_map.135
  104.2 17.7 %all_to_all.53 = f32[16,8,128]{2,1,0:T(8,128)S(1)} all-to-all(f32[16,8,128]{2,1,0:T(8,128)S(1)} %shard_map.135), channel_id=1, replica_groups=mesh['z'=16,'x'=4,'y'=4,'c'=2] {'z'}, dimensions={0} | all-to-all | bytes 131072 | tf_op jit(solution)/shard_map/all_to_all | solution.py:387
  121.9 8.0 %all_to_all.54 = f32[4,16,8,128]{3,2,1,0:T(8,128)S(1)} all-to-all(f32[4,16,8,128]{3,2,1,0:T(8,128)S(1)} %broadcast_in_dim.9), channel_id=1, replica_groups=mesh['z'=16,'x'=4,'y'=4,'c'=2] {'x'}, dimensions={0} | all-to-all | bytes 524288 | tf_op jit(solution)/shard_map/all_to_all | solution.py:387
  129.9 18.0 %all_gather.49.terms_ref = f32[2,512,128]{2,1,0:T(8,128)S(1)} all-gather(f32[1,512,128]{2,1,0:T(8,128)S(1)} %bitcast.18), channel_id=1, replica_groups=mesh['z'=16,'x'=4,'y'=4,'c'=2] {'c'}, dimensions={0}, use_global_device_ids=true | all-gather | bytes 786432 | tf_op jit(solution)/shard_map/all_gather | solution.py:396
  147.9 0.0 all-gather.10.cloned.1.call-done
  147.9 0.0 copy-start.1
  147.9 1.3 copy-done.1
  149.1 1.3 shard_map.136
  150.5 14.2 %all_to_all.55 = f32[16,8,128]{2,1,0:T(8,128)S(1)} all-to-all(f32[16,8,128]{2,1,0:T(8,128)S(1)} %get-tuple-element.39), channel_id=1, replica_groups=mesh['z'=16,'x'=4,'y'=4,'c'=2] {'z'}, dimensions={0} | all-to-all | bytes 131072 | tf_op jit(solution)/shard_map/all_to_all | solution.py:387
  164.7 7.9 %all_to_all.56 = f32[4,16,8,128]{3,2,1,0:T(8,128)S(1)} all-to-all(f32[4,16,8,128]{3,2,1,0:T(8,128)S(1)} %broadcast_in_dim.10), channel_id=1, replica_groups=mesh['z'=16,'x'=4,'y'=4,'c'=2] {'x'}, dimensions={0} | all-to-all | bytes 524288 | tf_op jit(solution)/shard_map/all_to_all | solution.py:387
  172.7 4.9 %all_gather.52.terms_ref = f32[2,512,128]{2,1,0:T(8,128)S(1)} all-gather(f32[1,512,128]{2,1,0:T(8,128)S(1)} %bitcast.19), channel_id=1, replica_groups=mesh['z'=16,'x'=4,'y'=4,'c'=2] {'c'}, dimensions={0}, use_global_device_ids=true | all-gather | bytes 786432 | tf_op jit(solution)/shard_map/all_gather | solution.py:396
  177.6 1.3 shard_map.137
  178.9 0.0 copy-start
  178.9 0.0 copy-start.5
  178.9 0.0 copy-start.6
  178.9 14.5 %all_to_all.57 = f32[16,8,128]{2,1,0:T(8,128)S(1)} all-to-all(f32[16,8,128]{2,1,0:T(8,128)S(1)} %shard_map.137), channel_id=1, replica_groups=mesh['z'=16,'x'=4,'y'=4,'c'=2] {'z'}, dimensions={0} | all-to-all | bytes 131072 | tf_op jit(solution)/shard_map/all_to_all | solution.py:387
  193.4 7.9 %all_to_all.58 = f32[4,16,8,128]{3,2,1,0:T(8,128)S(1)} all-to-all(f32[4,16,8,128]{3,2,1,0:T(8,128)S(1)} %broadcast_in_dim.11), channel_id=1, replica_groups=mesh['z'=16,'x'=4,'y'=4,'c'=2] {'x'}, dimensions={0} | all-to-all | bytes 524288 | tf_op jit(solution)/shard_map/all_to_all | solution.py:387
  201.4 4.9 %all_gather.53.terms_ref = f32[2,512,128]{2,1,0:T(8,128)S(1)} all-gather(f32[1,512,128]{2,1,0:T(8,128)S(1)} %bitcast.20), channel_id=1, replica_groups=mesh['z'=16,'x'=4,'y'=4,'c'=2] {'c'}, dimensions={0}, use_global_device_ids=true | all-gather | bytes 786432 | tf_op jit(solution)/shard_map/all_gather | solution.py:396
  206.3 0.0 copy-start.2
  206.3 0.0 copy-start.3
  206.3 0.0 copy-start.9
  206.3 0.0 copy-start.10
  206.3 0.0 copy-done
  206.3 0.0 copy-done.5
  206.3 0.0 copy-done.6
  206.3 2.3 %shard_map.138 = (f32[6,128]{1,0:T(8,128)}, f32[6,128]{1,0:T(8,128)}, f32[8,128]{1,0:T(8,128)S(1)}) custom-call(s32[6]{0:T(128)S(1)} %copy-done.7, s32[6]{0:T(128)S(1)} %copy-done.8, f32[2,512,128]{2,1,0:T(8,128)S(1)} %all_gather.53.terms_ref, s32[128,8,128]{2,1,0:T(8,128)S(1)} %get-tuple-element.36.ids_ref, ...), custom_call_target="tpu_custom_call" | custom-call | tf_op jit(solution)/shard_map/pallas_call | solution.py:25
  208.6 1.9 all-gather.4
  210.5 0.0 copy-done.2
  210.5 0.0 copy-done.3
  210.5 0.0 copy-done.9
  210.5 0.0 copy-done.10
  210.5 4.0 %shard_map.139 = (f32[6,3,128]{2,1,0:T(4,128)}, f32[6,3,128]{2,1,0:T(4,128)}) custom-call(f32[2,8,128]{2,1,0:T(8,128)S(1)} %bitcast.16, bf16[2,6,128,128]{3,2,1,0:T(8,128)(2,1)S(1)} %get-tuple-element.45.other_ref, f32[6,8,128]{2,1,0:T(8,128)S(1)} %get-tuple-element.46.passing_ref, bf16[6,3,128,128]{3,2,1,0:T(8,128)(2,1)S(1)} %copy-done.2, ...), custom_call_target="tpu_custom_call" | custom-call | tf_op jit(solution)/shard_map/pallas_call | solution.py:25
  (5 shorter events, 0.1 us)
Async XLA Ops:
  7.2 73.8 %all-gather.8.cloned.1.call-start = ((), (), s32[]{:S(2)}) async-start(), calls=%async_computation.10 | async-start | bytes 2088960 | tf_op jit(solution)/shard_map/all_gather | solution.py:430
  24.9 11.5 %copy-start.4 = (f32[6,128,128]{2,1,0:T(8,128)S(1)}, f32[6,128,128]{2,1,0:T(8,128)}, u32[]{:S(2)}) copy-start(f32[6,128,128]{2,1,0:T(8,128)} %outlet_ref.1) | copy-start | bytes 1179652
  24.9 11.5 %copy-start.7 = (s32[6]{0:T(128)S(1)}, s32[6]{0:T(128)}, u32[]{:S(2)}) copy-start(s32[6]{0:T(128)} %lower_ref.9) | copy-start | bytes 76
  24.9 11.5 %copy-start.8 = (s32[6]{0:T(128)S(1)}, s32[6]{0:T(128)}, u32[]{:S(2)}) copy-start(s32[6]{0:T(128)} %upper_ref.9) | copy-start | bytes 76
  63.4 9.3 %all-to-all-start.1 = ((f32[4,16,8,128]{3,2,1,0:T(8,128)}), f32[4,16,8,128]{3,2,1,0:T(8,128)S(1)}, u32[]{:S(2)}, u32[]{:S(2)}) async-start(f32[4,16,8,128]{3,2,1,0:T(8,128)} %broadcast_in_dim.8), calls=%async_computation.1 | async-start | bytes 524288 | tf_op jit(solution)/shard_map/all_to_all | solution.py:387
  67.2 80.7 %all-gather.10.cloned.1.call-start = ((), (), s32[]{:S(2)}) async-start(), calls=%async_computation.11 | async-start | bytes 1474560 | tf_op jit(solution)/shard_map/all_gather | solution.py:487
  147.9 1.3 copy-start.1
  178.9 27.4 %copy-start = (f32[6,128,128]{2,1,0:T(8,128)S(1)}, f32[6,128,128]{2,1,0:T(8,128)}, u32[]{:S(2)}) copy-start(f32[6,128,128]{2,1,0:T(8,128)} %inv_ref.3) | copy-start | bytes 1179652
  178.9 27.4 %copy-start.5 = (f32[6,128]{1,0:T(8,128)S(1)}, f32[6,128]{1,0:T(8,128)}, u32[]{:S(2)}) copy-start(f32[6,128]{1,0:T(8,128)} %residual_ref.3) | copy-start | bytes 9220
  178.9 27.4 %copy-start.6 = (f32[6,128]{1,0:T(8,128)S(1)}, f32[6,128]{1,0:T(8,128)}, u32[]{:S(2)}) copy-start(f32[6,128]{1,0:T(8,128)} %cotangent_ref.4) | copy-start | bytes 9220
  206.3 4.2 %copy-start.2 = (bf16[6,3,128,128]{3,2,1,0:T(8,128)(2,1)S(1)}, bf16[6,3,128,128]{3,2,1,0:T(8,128)(2,1)}, u32[]{:S(2)}) copy-start(bf16[6,3,128,128]{3,2,1,0:T(8,128)(2,1)} %get-tuple-element.47.high_ref) | copy-start | bytes 1769476
  206.3 4.2 %copy-start.3 = (bf16[6,3,128,128]{3,2,1,0:T(8,128)(2,1)S(1)}, bf16[6,3,128,128]{3,2,1,0:T(8,128)(2,1)}, u32[]{:S(2)}) copy-start(bf16[6,3,128,128]{3,2,1,0:T(8,128)(2,1)} %get-tuple-element.48.low_ref) | copy-start | bytes 1769476
  206.3 4.2 %copy-start.9 = (f32[6,3,128]{2,1,0:T(4,128)S(1)}, f32[6,3,128]{2,1,0:T(4,128)}, u32[]{:S(2)}) copy-start(f32[6,3,128]{2,1,0:T(4,128)} %cotangent_ref.5) | copy-start | bytes 27652
  206.3 4.2 %copy-start.10 = (f32[6,3,128]{2,1,0:T(4,128)S(1)}, f32[6,3,128]{2,1,0:T(4,128)}, u32[]{:S(2)}) copy-start(f32[6,3,128]{2,1,0:T(4,128)} %get-tuple-element.49.forced_ref) | copy-start | bytes 27652
Sparse Core Ops, SparseCore 0:
  10.1 70.8 all-gather.7
  95.8 36.6 all-gather.9

commit v6 on v5

--- a/solution.py
+++ b/solution.py
@@ -1,3 +1,5 @@
+import functools
+
 import jax
 import jax.numpy as jnp
 from jax import lax
@@ -96,7 +98,7 @@
 
 
 def local_kernel(
-    inv_hbm, link_hbm, residual_hbm, cotangent_hbm, high_ref, low_ref, forced_ref, out_ref,
+    inv_hbm, link_hbm, residual_hbm, cotangent_hbm, maps_ref, vectors_ref, out_ref,
     inv_ref, link_ref, residual_ref, cotangent_ref, sems,
 ):
     members, blocks = inv_ref.shape[:2]
@@ -113,17 +115,26 @@
         for i in range(blocks):
             inverse = two_parts(inv_ref[s, i])
             m.append(two_parts(product(inverse, two_parts(link_ref[s, i]))))
-            high_ref[s, i], low_ref[s, i] = m[i]
             f.append(applied(inverse, residual_ref[s, i : i + 1]))
-            forced_ref[s, i : i + 1] = f[i]
+        rows = [jnp.zeros((1, WIDTH), F32)] * 8
         total, vector = m[0], f[0]
-        for i in range(1, blocks):
-            total = product(m[i], total if i == 1 else two_parts(total))
-            vector = applied(m[i], vector) + f[i]
+        for i in range(blocks):
+            if i:
+                result = product(m[i], total)
+                total = two_parts(result)
+                vector = applied(m[i], vector) + f[i]
+            maps_ref[0, s, i], maps_ref[1, s, i] = total
+            rows[i] = vector
         back = cotangent_ref[s, blocks - 1 : blocks]
+        rows[2 * blocks - 1] = back
+        suffix = None
         for i in range(blocks - 2, -1, -1):
             back = cotangent_ref[s, i : i + 1] + applied_transposed(m[i + 1], back)
-        out_ref[s, :WIDTH] = total
+            rows[blocks + i] = back
+            suffix = m[i + 1] if suffix is None else two_parts(product(suffix, m[i + 1]))
+            maps_ref[0, s, blocks + i], maps_ref[1, s, blocks + i] = suffix
+        vectors_ref[s] = jnp.concatenate(rows)
+        out_ref[s, :WIDTH] = result
         out_ref[s, WIDTH:] = jnp.concatenate(
             [vector, applied_transposed(m[0], back), jnp.zeros((6, WIDTH), F32)]
         )
@@ -207,11 +218,11 @@
 def pick_kernel(ids_ref, table_ref, out_ref, sems):
     dests, owned = out_ref.shape[:2]
     half = owned // 2
-    x = lax.axis_index("x")
+    x, c = lax.axis_index("x"), lax.axis_index("c")
     pairs, here = [], []
     for d in range(dests):
         for t in range(owned):
-            junction = ids_ref[d * owned + (t + half) % owned]
+            junction = ids_ref[(c * dests + d) * owned + (t + half) % owned]
             basin = lax.div(junction, owned)
             line = lax.div(basin, dests)
             at = line * owned + (junction - basin * owned)
@@ -239,26 +250,60 @@
     return inflow, outflow
 
 
+def source_ids(values, half):
+    row = lax.broadcasted_iota(jnp.int32, (8, WIDTH), 0)
+    lane = lax.broadcasted_iota(jnp.int32, (8, WIDTH), 1)
+    chosen = jnp.where((row == lane) & (row < 2 * half), values[:, 2 * half : 2 * half + 1], 0.0)
+    ids = jnp.sum(chosen, axis=2, keepdims=True).astype(jnp.int32)
+    return jnp.broadcast_to(ids, values.shape)
+
+
+def sums_kernel(plane_ref, ids_ref, terms_ref, out_ref, *, half, cores, own):
+    ids, values = ids_ref[...], terms_ref[...]
+    sides = out_ref.shape[0] // cores
+    owned = cores * half
+    line = lax.axis_index("z") * sides
+    nothing = jnp.zeros((1, WIDTH), F32)
+    for d in range(out_ref.shape[0]):
+        x, c = d // cores, d % cores
+        at = (c * sides + x) * owned
+        rows = [nothing] * out_ref.shape[1]
+        for k in range(half):
+            pattern = rule(plane_ref[at + half + k], plane_ref[at + k], half)
+            rows[k], rows[half + k] = gathered(ids, values, pattern, half)
+            if own:
+                junction = (line + x) * owned + c * half + k
+                pattern = rule(junction, junction, half)
+                rows[8 + k], rows[8 + half + k] = gathered(ids, values, pattern, half)
+        out_ref[d] = jnp.concatenate(rows)
+
+
+def summed(parts_ref):
+    total = parts_ref[0]
+    for i in range(1, parts_ref.shape[0]):
+        total = total + parts_ref[i]
+    return total
+
+
 def spread_rows(payload, spread_ref):
     full = jnp.concatenate(payload)
     for i in range(spread_ref.shape[0]):
         spread_ref[i] = full
 
 
-def step(lower_ref, upper_ref, ids, values, tiles, schur_ref, ends, base, spread_ref):
+def step(total, tiles_ref, schur_ref, ends, base, spread_ref):
     half = schur_ref.shape[1]
-    first_s = lax.axis_index("c") * half
     payload = [jnp.zeros((1, WIDTH), F32)] * 8
+    total = total + ends
     for k in range(half):
-        pattern = rule(upper_ref[first_s + k], lower_ref[first_s + k], half)
-        inflow, outflow = gathered(ids, values, pattern, half)
-        head = applied(kept(tiles, k), ends[k : k + 1] + inflow)
-        relief = applied_transposed(
-            kept(tiles, half + k), ends[half + k : half + k + 1] + outflow
-        )
+        other = half + k
+        head, relief = total[k : k + 1], total[other : other + 1]
+        if tiles_ref is not None:
+            head = applied(kept(tiles_ref, k), head)
+            relief = applied_transposed(kept(tiles_ref, other), relief)
         schur = kept(schur_ref, k)
         payload[k] = base[k : k + 1] + applied(schur, head)
-        payload[half + k] = base[half + k : half + k + 1] + applied_transposed(schur, relief)
+        payload[other] = base[other : other + 1] + applied_transposed(schur, relief)
     spread_rows(payload, spread_ref)
 
 
@@ -267,13 +312,13 @@
     piece = WIDTH // spread_ref.shape[0]
     first_s = lax.axis_index("c") * half
     start = pl.multiple_of(lax.axis_index("y") * piece, 8)
-    row = lax.broadcasted_iota(jnp.int32, (8, WIDTH), 0)
-    lane = lax.broadcasted_iota(jnp.int32, (8, WIDTH), 1)
     values = terms_ref[...].reshape(-1, 8, WIDTH)
-    chosen = jnp.where((row == lane) & (row < 2 * half), values[:, 2 * half : 2 * half + 1], 0.0)
-    ids = jnp.sum(chosen, axis=2, keepdims=True).astype(jnp.int32)
-    ids = jnp.broadcast_to(ids, values.shape)
-    ids_ref[...] = ids
+    ids = source_ids(values, half)
+    count = ids_ref.shape[0] * 8
+    column = pl.multiple_of(lax.axis_index("x") * count, 8)
+    ids_ref[...] = source_ids(
+        terms_ref[lax.axis_index("c"), pl.ds(column, count)].reshape(ids_ref.shape), half
+    )
     merged = picked_ref[0]
     for d in range(1, picked_ref.shape[0]):
         merged = merged + picked_ref[d]
@@ -298,72 +343,53 @@
 
 
 def second_kernel(parts_ref, schur_ref, base_ref, spread_ref):
-    half = schur_ref.shape[1]
-    total = parts_ref[0]
-    for i in range(1, parts_ref.shape[0]):
-        total = total + parts_ref[i]
-    base = base_ref[0]
-    payload = [jnp.zeros((1, WIDTH), F32)] * 8
-    for k in range(half):
-        schur = kept(schur_ref, k)
-        payload[k] = base[k : k + 1] + applied(schur, total[k : k + 1])
-        payload[half + k] = base[half + k : half + k + 1] + applied_transposed(
-            schur, total[half + k : half + k + 1]
-        )
-    spread_rows(payload, spread_ref)
-
-
-def third_kernel(
-    lower_ref, upper_ref, terms_ref, ids_ref, ends_ref, schur_ref, rows_ref, base_ref, tiles_ref, spread_ref
-):
+    step(summed(parts_ref), None, schur_ref, 0.0, base_ref[0], spread_ref)
+
+
+def third_kernel(parts_ref, ends_ref, schur_ref, rows_ref, base_ref, tiles_ref, spread_ref):
     piece = WIDTH // ends_ref.shape[0]
     for k in range(tiles_ref.shape[1]):
         keep(tiles_ref, k, jnp.concatenate([ends_ref[i, k, :piece] for i in range(ends_ref.shape[0])]))
-    values = terms_ref[...].reshape(-1, 8, WIDTH)
-    step(lower_ref, upper_ref, ids_ref[...], values, tiles_ref, schur_ref, rows_ref[...], base_ref[0], spread_ref)
-
-
-def step_kernel(
-    lower_ref, upper_ref, terms_ref, ids_ref, tiles_ref, schur_ref, rows_ref, base_ref, spread_ref
-):
-    values = terms_ref[...].reshape(-1, 8, WIDTH)
-    step(lower_ref, upper_ref, ids_ref[...], values, tiles_ref, schur_ref, rows_ref[...], base_ref[0], spread_ref)
+    step(summed(parts_ref), tiles_ref, schur_ref, rows_ref[...], base_ref[0], spread_ref)
+
+
+def step_kernel(parts_ref, tiles_ref, schur_ref, rows_ref, base_ref, spread_ref):
+    step(summed(parts_ref), tiles_ref, schur_ref, rows_ref[...], base_ref[0], spread_ref)
 
 
 def last_kernel(
-    lower_ref, upper_ref, terms_ref, ids_ref, tiles_ref, rows_ref, before_ref, after_ref, passing_ref,
-    inv_ref, residual_ref, cotangent_ref, sections_ref, adjoint_ref, shared_ref,
+    parts_ref, tiles_ref, rows_ref, before_ref, after_ref, passing_ref,
+    inv_ref, residual_ref, cotangent_ref, shared_ref,
 ):
     half = before_ref.shape[1]
-    owned = inv_ref.shape[0]
-    first_s = lax.axis_index("c") * half
-    first_j = (lax.axis_index("z") * lax.axis_size("x") + lax.axis_index("x")) * owned
-    values = terms_ref[...].reshape(-1, 8, WIDTH)
-    ids = ids_ref[...]
-    shared_ref[2 * half :] = jnp.zeros((2, WIDTH), F32)
+    c = lax.axis_index("c")
+    total = summed(parts_ref)
+    ends = total[:8] + rows_ref[...]
+    out = [jnp.zeros((1, WIDTH), F32)] * 16
     for k in range(half):
-        pattern = rule(upper_ref[first_s + k], lower_ref[first_s + k], half)
-        inflow, outflow = gathered(ids, values, pattern, half)
-        head = applied(kept(tiles_ref, k), rows_ref[k : k + 1] + inflow)
-        relief = applied_transposed(
-            kept(tiles_ref, half + k), rows_ref[half + k : half + k + 1] + outflow
-        )
-        shared_ref[k : k + 1] = applied(kept(before_ref, k), head) + passing_ref[k : k + 1]
-        shared_ref[half + k : half + k + 1] = (
-            applied_transposed(kept(after_ref, k), relief) + passing_ref[half + k : half + k + 1]
-        )
-    for k in range(owned):
-        inflow, outflow = gathered(ids, values, rule(first_j + k, first_j + k, half), half)
-        sections_ref[k : k + 1] = applied(inv_ref[k], residual_ref[k : k + 1] + inflow)
-        adjoint_ref[k : k + 1] = cotangent_ref[k : k + 1] + outflow
-
-
-def cells_kernel(shared_ref, other_ref, passing_ref, high_ref, low_ref, forced_ref, cotangent_ref, update_ref, adjoint_ref):
-    members, blocks = high_ref.shape[:2]
+        other = half + k
+        head = applied(kept(tiles_ref, k), ends[k : k + 1])
+        relief = applied_transposed(kept(tiles_ref, other), ends[other : other + 1])
+        out[k] = applied(kept(before_ref, k), head) + passing_ref[k : k + 1]
+        out[other] = applied_transposed(kept(after_ref, k), relief) + passing_ref[other : other + 1]
+        residual = jnp.where(c == 1, residual_ref[other : other + 1], residual_ref[k : k + 1])
+        cotangent = jnp.where(c == 1, cotangent_ref[other : other + 1], cotangent_ref[k : k + 1])
+        out[8 + k] = applied(inv_ref[c * half + k], residual + total[8 + k : 9 + k])
+        out[8 + other] = cotangent + total[8 + other : 9 + other]
+    shared_ref[...] = jnp.concatenate(out)
+
+
+def cells_kernel(
+    shared_ref, other_ref, passing_ref, maps_ref, vectors_ref,
+    update_ref, sections_ref, adjoint_ref, junction_ref,
+):
+    members, blocks = update_ref.shape[:2]
     half = members // 2
     c = lax.axis_index("c")
     for s in range(members):
         core, k = s // half, s % half
+        sections_ref[s : s + 1] = shared_ref[core, 8 + k : 9 + k]
+        junction_ref[s : s + 1] = shared_ref[core, 8 + half + k : 9 + half + k]
         enter = shared_ref[core, k : k + 1]
         leave = shared_ref[core, half + k : half + k + 1]
         matrix = kept(other_ref, s)
@@ -371,16 +397,19 @@
         nearer = applied_transposed(matrix, leave) + passing_ref[s, 1:2]
         enter = jnp.where(c == 1, further, enter)
         leave = jnp.where(c == 0, nearer, leave)
+        rows, back = [], []
         for i in range(blocks):
-            enter = applied((high_ref[s, i], low_ref[s, i]), enter) + forced_ref[s, i : i + 1]
-            update_ref[s, i : i + 1] = enter
-        carried = cotangent_ref[s, blocks - 1 : blocks] + leave
-        adjoint_ref[s, blocks - 1 : blocks] = carried
-        for i in range(blocks - 2, -1, -1):
-            carried = cotangent_ref[s, i : i + 1] + applied_transposed(
-                (high_ref[s, i + 1], low_ref[s, i + 1]), carried
+            rows.append(
+                applied((maps_ref[0, s, i], maps_ref[1, s, i]), enter) + vectors_ref[s, i : i + 1]
             )
-            adjoint_ref[s, i : i + 1] = carried
+            if i < blocks - 1:
+                suffix = (maps_ref[0, s, blocks + i], maps_ref[1, s, blocks + i])
+                change = applied_transposed(suffix, leave)
+            else:
+                change = leave
+            back.append(change + vectors_ref[s, blocks + i : blocks + i + 1])
+        update_ref[s] = jnp.concatenate(rows)
+        adjoint_ref[s] = jnp.concatenate(back)
 
 
 def swap(spread, axis):
@@ -430,12 +459,11 @@
     table = lax.all_gather(part, "z").reshape(zs * owned, piece + 8, width)
 
     chain = (members, blocks, width, width)
-    high, low, forced, local = run(
+    maps, vectors, local = run(
         local_kernel,
         [
-            array(*chain, dtype=bf16),
-            array(*chain, dtype=bf16),
-            array(members, blocks, width),
+            array(2, members, 2 * blocks - 1, width, width, dtype=bf16),
+            array(members, 8, width),
             array(members, PACK, width),
         ],
         chain_inv, chain_link, reach_residual, cell_cotangent,
@@ -465,8 +493,8 @@
     terms = exchanged(first)
     plane = lax.dynamic_slice(
         terms.reshape(cs, xs, zs, 8, width),
-        (lax.axis_index("c"), 0, lax.axis_index("z"), 2 * half, 0),
-        (1, xs, 1, 1, owned),
+        (0, 0, lax.axis_index("z"), 2 * half, 0),
+        (cs, xs, 1, 1, owned),
     ).reshape(-1).astype(jnp.int32)
     picked = run(
         pick_kernel, array(xs, owned, piece + 8, width), plane, table,
@@ -475,7 +503,7 @@
     ids, rows, merged, parts = run(
         partial_kernel,
         [
-            array(cs * xs * zs, 8, width, dtype=jnp.int32),
+            array(zs, 8, width, dtype=jnp.int32),
             array(8, width),
             array(owned, 3 * piece, width),
             array(ys, 8, width),
@@ -485,28 +513,34 @@
     )
     parts, merged = lax.optimization_barrier((parts, merged))
     ends = lax.all_gather(merged, "y")
-    terms = exchanged(run(second_kernel, array(zs, 8, width), swap(parts, "y"), schur, first))
+    sides = ("x", "c")
+
+    def sums(spread, own):
+        kernel = functools.partial(sums_kernel, half=half, cores=cs, own=own)
+        shape = array(xs * cs, 16 if own else 8, width)
+        return swap(run(kernel, shape, plane, ids, swap(spread, "z"), scalars=1), sides)
+
+    spread = run(second_kernel, array(zs, 8, width), swap(parts, "y"), schur, first)
     tiles, spread = run(
         third_kernel,
         [array(2, 2 * half, width, width, dtype=bf16), array(zs, 8, width)],
-        lower, upper, terms, ids, ends, schur, rows, first, scalars=2,
-    )
-    terms = exchanged(spread)
+        sums(spread, False), ends, schur, rows, first,
+    )
     for sweep in range(3, SWEEPS):
         spread = run(
-            step_kernel, array(zs, 8, width), lower, upper, terms, ids, tiles, schur, rows, first, scalars=2
+            step_kernel, array(zs, 8, width), sums(spread, False), tiles, schur, rows, first
         )
-        terms = exchanged(spread)
-    sections, adjoint, shared = run(
-        last_kernel,
-        [array(owned, width), array(owned, width), array(8, width)],
-        lower, upper, terms, ids, tiles, rows, before, after, passing,
-        junction_inv, junction_residual, junction_cotangent, scalars=2,
-    )
-    cell_update, cell_adjoint = run(
+    shared = run(
+        last_kernel, array(16, width), sums(spread, True), tiles, rows, before, after, passing,
+        junction_inv, junction_residual, junction_cotangent,
+    )
+    cell_update, sections, cell_adjoint, adjoint = run(
         cells_kernel,
-        [array(members, blocks, width), array(members, blocks, width)],
-        lax.all_gather(shared, "c"), other, other_rows, high, low, forced, cell_cotangent,
+        [
+            array(members, blocks, width), array(owned, width),
+            array(members, blocks, width), array(owned, width),
+        ],
+        lax.all_gather(shared, "c"), other, other_rows, maps, vectors,
     )
     return (cell_update, sections, cell_adjoint, adjoint)
 

time: 222 us -> 209 us (0.941)
  blocking collectives: 168 us -> 157 us
    all_gather x4 -> x1, blocking collectives: 34.8 us -> 6.46 us  [exchanged(): return lax.all_gather(along_x.reshape(-1, WIDTH), 'c')]
    all_to_all x9, blocking collectives: 111 us -> 128 us  [swap(): return lax.all_to_all(spread, axis, 0, 0, tiled=False)]
    pallas_call x11 -> x14, Pallas kernels: 26.1 us -> 24.8 us  [run(): pl.pallas_call(kernel, out_shape=shapes, in_specs=[smem] * scalars + [whe...]
  transfers between devices with their start and end apart: 3 -> 3, of which waited for: 2 -> 1; matrix products, arithmetic and copies ran while one was open for 1% -> 1% of each run, Pallas kernels for 5% -> 6%
where the time goes in v6:
time: 209 us
  blocking collectives  157 us (75%)
  Pallas kernels  24.8 us (12%)
  between operations  14.1 us (7%)
  waiting for transfers between devices  5.56 us (3%)
  starting transfers between devices  4.4 us (2%)
  local copies, waits for them, and re-layouts  2.64 us (1%)
    all_to_all x9, blocking collectives, swap(): return lax.all_to_all(spread, axis, 0, 0, tiled=False)  128 us
    pallas_call x14, Pallas kernels, run(): pl.pallas_call(kernel, out_shape=shapes, in_specs=[smem] * scalars + [whe...  24.8 us
    all_gather x1, blocking collectives, shards(): chips = lax.all_gather(chip, 'y')  11.5 us
    all_gather x1, blocking collectives, shards(): pair = lax.all_gather(local, 'c')  9.12 us
    all_gather x1, blocking collectives, exchanged(): return lax.all_gather(along_x.reshape(-1, WIDTH), 'c')  6.46 us
    all_to_all x1, waiting for transfers between devices, swap(): return lax.all_to_all(spread, axis, 0, 0, tiled=False)  5.53 us
    all_to_all x1, starting transfers between devices, swap(): return lax.all_to_all(spread, axis, 0, 0, tiled=False)  4.36 us
  transfers between devices with their start and end apart: 3, of which 1 were waited for; matrix products, arithmetic and copies ran while one was open for 1% of the time, Pallas kernels for 6%

profile of v6, /device:TPU:1, one launch (start us, length us, event | category | flops | bytes accessed | tf_op | source)
XLA Modules:
  0.0 208.8 jit_solution(13758753289513411452)
XLA Ops:
  7.2 0.0 all-gather.8.cloned.1.call-start
  7.2 1.6 shard_map.132
  8.8 0.0 all-gather.8.cloned.1.call-update
  8.8 7.7 %shard_map.129 = (bf16[2,6,5,128,128]{4,3,2,1,0:T(8,128)(2,1)}, f32[6,8,128]{2,1,0:T(8,128)}, f32[6,136,128]{2,1,0:T(8,128)}) custom-call(f32[6,3,128,128]{3,2,1,0:T(8,128)} %inv_hbm.1, f32[6,3,128,128]{3,2,1,0:T(8,128)} %link_hbm.1, f32[6,3,128]{2,1,0:T(4,128)} %residual_hbm.1, f32[6,3,128]{2,1,0:T(4,128)} %cotangent_hbm.1), custom_call_target="tpu_custom_call" | custom-call | flops 2000000000 | bytes 20000000 | tf_op jit(solution)/shard_map/pallas_call | solution.py:27
  16.5 9.1 %all-gather = f32[12,136,128]{2,1,0:T(8,128)S(1)} all-gather(f32[6,136,128]{2,1,0:T(8,128)} %get-tuple-element.23), channel_id=2, replica_groups=mesh['z'=16,'x'=4,'y'=4,'c'=2] {'c'}, dimensions={0}, use_global_device_ids=true | all-gather | bytes 1253376 | tf_op jit(solution)/shard_map/all_gather | solution.py:479
  25.6 0.0 copy-start.3
  25.6 0.0 copy-start.8
  25.6 0.0 copy-start.9
  25.6 0.4 shard_map.130
  26.0 11.5 %all-gather.1 = f32[12,136,128]{2,1,0:T(8,128)S(1)} all-gather(f32[3,136,128]{2,1,0:T(8,128)S(1)} %get-tuple-element.24), channel_id=3, replica_groups=mesh['z'=16,'x'=4,'y'=4,'c'=2] {'y'}, dimensions={0}, use_global_device_ids=true | all-gather | bytes 1044480 | tf_op jit(solution)/shard_map/all_gather | solution.py:485
  37.6 0.0 copy-done.3
  37.6 0.0 copy-done.8
  37.6 0.0 copy-done.9
  37.6 3.7 %shard_map.131 = (bf16[2,3,128,128]{3,2,1,0:T(8,128)(2,1)S(1)}, bf16[2,3,128,128]{3,2,1,0:T(8,128)(2,1)S(1)}, bf16[2,3,128,128]{3,2,1,0:T(8,128)(2,1)S(1)}, f32[8,128]{1,0:T(8,128)S(1)}, f32[16,8,128]{2,1,0:T(8,128)S(1)}) custom-call(s32[6]{0:T(128)S(1)} %copy-done.8, s32[6]{0:T(128)S(1)} %copy-done.9, f32[4,3,136,128]{3,2,1,0:T(8,128)S(1)} %bitcast.9, ...), custom_call_target="tpu_custom_call" | custom-call | tf_op jit(solution)/shard_map/pallas_call | solution.py:27
  41.2 22.1 %all_to_all.50 = f32[16,8,128]{2,1,0:T(8,128)S(1)} all-to-all(f32[16,8,128]{2,1,0:T(8,128)S(1)} %get-tuple-element.25.base_ref), channel_id=1, replica_groups=mesh['z'=16,'x'=4,'y'=4,'c'=2] {'z'}, dimensions={0} | all-to-all | bytes 131072 | tf_op jit(solution)/shard_map/all_to_all | solution.py:416
  63.3 0.7 broadcast_in_dim.2
  64.1 4.4 %all-to-all-start.1 = ((f32[4,16,8,128]{3,2,1,0:T(8,128)}), f32[4,16,8,128]{3,2,1,0:T(8,128)S(1)}, u32[]{:S(2)}, u32[]{:S(2)}) async-start(f32[4,16,8,128]{3,2,1,0:T(8,128)} %broadcast_in_dim.2), calls=%async_computation.1 | async-start | bytes 524288 | tf_op jit(solution)/shard_map/all_to_all | solution.py:416
  68.4 0.0 all-gather.10.cloned.1.call-start
  68.4 5.5 %all-to-all-done.1 = f32[4,16,8,128]{3,2,1,0:T(8,128)S(1)} async-done(((f32[4,16,8,128]{3,2,1,0:T(8,128)}), f32[4,16,8,128]{3,2,1,0:T(8,128)S(1)}, u32[]{:S(2)}, u32[]{:S(2)}) %all-to-all-start.1) | async-done | bytes 262176 | tf_op jit(solution)/shard_map/all_to_all | solution.py:416
  73.9 6.5 %all_gather.37.terms_ref = f32[2,512,128]{2,1,0:T(8,128)S(1)} all-gather(f32[1,512,128]{2,1,0:T(8,128)S(1)} %bitcast.14), channel_id=1, replica_groups=mesh['z'=16,'x'=4,'y'=4,'c'=2] {'c'}, dimensions={0}, use_global_device_ids=true | all-gather | bytes 786432 | tf_op jit(solution)/shard_map/all_gather | solution.py:425
  80.4 0.6 convert_element_type.6.ids_ref.plane_ref
  81.0 0.0 all-gather.8.cloned.1.call-done.table_ref
  81.0 2.7 %shard_map.133 = f32[4,6,40,128]{3,2,1,0:T(8,128)} custom-call(s32[48]{0:T(128)} %convert_element_type.6.ids_ref.plane_ref, f32[96,40,128]{2,1,0:T(8,128)} %all-gather.8.cloned.1.call-done.table_ref), custom_call_target="tpu_custom_call" | custom-call | tf_op jit(solution)/shard_map/pallas_call | solution.py:27
  83.8 0.0 copy-start.7
  83.8 10.2 %all_to_all.51.picked_ref = f32[4,6,40,128]{3,2,1,0:T(8,128)S(1)} all-to-all(f32[4,6,40,128]{3,2,1,0:T(8,128)} %shard_map.133), channel_id=1, replica_groups=mesh['z'=16,'x'=4,'y'=4,'c'=2] {'x'}, dimensions={0} | all-to-all | bytes 983040 | tf_op jit(solution)/shard_map/all_to_all | solution.py:416
  94.0 1.7 shard_map.134
  95.6 0.0 all-gather.10.cloned.1.call-update
  95.7 8.5 %all_to_all.52.parts_ref = f32[4,8,128]{2,1,0:T(8,128)S(1)} all-to-all(f32[4,8,128]{2,1,0:T(8,128)S(1)} %get-tuple-element.29), channel_id=1, replica_groups=mesh['z'=16,'x'=4,'y'=4,'c'=2] {'y'}, dimensions={0} | all-to-all | bytes 32768 | tf_op jit(solution)/shard_map/all_to_all | solution.py:416
  104.2 0.3 shard_map.135
  104.5 18.2 %all_to_all.53.terms_ref = f32[16,8,128]{2,1,0:T(8,128)S(1)} all-to-all(f32[16,8,128]{2,1,0:T(8,128)S(1)} %shard_map.135), channel_id=1, replica_groups=mesh['z'=16,'x'=4,'y'=4,'c'=2] {'z'}, dimensions={0} | all-to-all | bytes 131072 | tf_op jit(solution)/shard_map/all_to_all | solution.py:416
  122.7 0.0 copy-done.7
  122.7 0.7 shard_map.136
  123.5 22.0 %all_to_all.54.parts_ref = f32[8,8,128]{2,1,0:T(8,128)S(1)} all-to-all(f32[8,8,128]{2,1,0:T(8,128)S(1)} %shard_map.136), channel_id=1, replica_groups=mesh['z'=16,'x'=4,'y'=4,'c'=2] {'x','c'}, dimensions={0} | all-to-all | bytes 65536 | tf_op jit(solution)/shard_map/all_to_all | solution.py:416
  145.5 0.0 all-gather.10.cloned.1.call-done
  145.5 0.0 copy-start.2
  145.5 1.3 copy-done.2
  146.8 0.0 copy-start.1
  146.8 0.0 copy-start.5
  146.8 0.0 copy-start.6
  146.8 0.7 shard_map.137
  147.4 14.2 %all_to_all.55.terms_ref = f32[16,8,128]{2,1,0:T(8,128)S(1)} all-to-all(f32[16,8,128]{2,1,0:T(8,128)S(1)} %get-tuple-element.33), channel_id=1, replica_groups=mesh['z'=16,'x'=4,'y'=4,'c'=2] {'z'}, dimensions={0} | all-to-all | bytes 131072 | tf_op jit(solution)/shard_map/all_to_all | solution.py:416
  161.6 0.7 shard_map.138
  162.4 9.0 %all_to_all.56.parts_ref = f32[8,8,128]{2,1,0:T(8,128)S(1)} all-to-all(f32[8,8,128]{2,1,0:T(8,128)S(1)} %shard_map.138), channel_id=1, replica_groups=mesh['z'=16,'x'=4,'y'=4,'c'=2] {'x','c'}, dimensions={0} | all-to-all | bytes 65536 | tf_op jit(solution)/shard_map/all_to_all | solution.py:416
  171.4 0.0 copy-start
  171.4 0.0 copy-start.4
  171.4 0.6 shard_map.139
  172.1 14.2 %all_to_all.57.terms_ref = f32[16,8,128]{2,1,0:T(8,128)S(1)} all-to-all(f32[16,8,128]{2,1,0:T(8,128)S(1)} %shard_map.139), channel_id=1, replica_groups=mesh['z'=16,'x'=4,'y'=4,'c'=2] {'z'}, dimensions={0} | all-to-all | bytes 131072 | tf_op jit(solution)/shard_map/all_to_all | solution.py:416
  186.3 0.9 shard_map.140
  187.3 9.3 %all_to_all.58.parts_ref = f32[8,16,128]{2,1,0:T(8,128)S(1)} all-to-all(f32[8,16,128]{2,1,0:T(8,128)S(1)} %shard_map.140), channel_id=1, replica_groups=mesh['z'=16,'x'=4,'y'=4,'c'=2] {'x','c'}, dimensions={0} | all-to-all | bytes 131072 | tf_op jit(solution)/shard_map/all_to_all | solution.py:416
  196.6 0.0 copy-done.1
  196.6 0.0 copy-done.5
  196.6 0.0 copy-done.6
  196.6 0.7 shard_map.141
  197.3 2.3 %all-gather.4 = f32[32,128]{1,0:T(8,128)S(1)} all-gather(f32[16,128]{1,0:T(8,128)S(1)} %shard_map.141), channel_id=6, replica_groups=mesh['z'=16,'x'=4,'y'=4,'c'=2] {'c'}, dimensions={0}, use_global_device_ids=true | all-gather | bytes 24576 | tf_op jit(solution)/shard_map/all_gather | solution.py:543
  199.6 0.0 copy-done
  199.6 0.0 copy-done.4
  199.6 2.3 %shard_map.142 = (f32[6,3,128]{2,1,0:T(4,128)}, f32[6,128]{1,0:T(8,128)}, f32[6,3,128]{2,1,0:T(4,128)}, f32[6,128]{1,0:T(8,128)}) custom-call(f32[2,16,128]{2,1,0:T(8,128)S(1)} %bitcast.13, bf16[2,6,128,128]{3,2,1,0:T(8,128)(2,1)S(1)} %get-tuple-element.38.other_ref, f32[6,8,128]{2,1,0:T(8,128)S(1)} %get-tuple-element.39.passing_ref, ...), custom_call_target="tpu_custom_call" | custom-call | tf_op jit(solution)/shard_map/pallas_call | solution.py:27
  (2 shorter events, 0.0 us)
Async XLA Ops:
  7.2 73.9 %all-gather.8.cloned.1.call-start = ((), (), s32[]{:S(2)}) async-start(), calls=%async_computation.10 | async-start | bytes 2088960 | tf_op jit(solution)/shard_map/all_gather | solution.py:459
  25.6 11.9 %copy-start.3 = (f32[6,128,128]{2,1,0:T(8,128)S(1)}, f32[6,128,128]{2,1,0:T(8,128)}, u32[]{:S(2)}) copy-start(f32[6,128,128]{2,1,0:T(8,128)} %outlet_ref.1) | copy-start | bytes 1179652
  25.6 11.9 %copy-start.8 = (s32[6]{0:T(128)S(1)}, s32[6]{0:T(128)}, u32[]{:S(2)}) copy-start(s32[6]{0:T(128)} %lower_ref.3) | copy-start | bytes 76
  25.6 11.9 %copy-start.9 = (s32[6]{0:T(128)S(1)}, s32[6]{0:T(128)}, u32[]{:S(2)}) copy-start(s32[6]{0:T(128)} %upper_ref.3) | copy-start | bytes 76
  64.1 9.9 %all-to-all-start.1 = ((f32[4,16,8,128]{3,2,1,0:T(8,128)}), f32[4,16,8,128]{3,2,1,0:T(8,128)S(1)}, u32[]{:S(2)}, u32[]{:S(2)}) async-start(f32[4,16,8,128]{3,2,1,0:T(8,128)} %broadcast_in_dim.2), calls=%async_computation.1 | async-start | bytes 524288 | tf_op jit(solution)/shard_map/all_to_all | solution.py:416
  68.4 77.1 %all-gather.10.cloned.1.call-start = ((), (), s32[]{:S(2)}) async-start(), calls=%async_computation.11 | async-start | bytes 1474560 | tf_op jit(solution)/shard_map/all_gather | solution.py:515
  83.8 38.9 %copy-start.7 = (s32[48]{0:T(128)S(1)}, s32[48]{0:T(128)}, u32[]{:S(2)}) copy-start(s32[48]{0:T(128)} %convert_element_type.6.ids_ref.plane_ref) | copy-start | bytes 580
  145.5 1.3 copy-start.2
  146.8 49.8 %copy-start.1 = (f32[6,128,128]{2,1,0:T(8,128)S(1)}, f32[6,128,128]{2,1,0:T(8,128)}, u32[]{:S(2)}) copy-start(f32[6,128,128]{2,1,0:T(8,128)} %inv_ref.3) | copy-start | bytes 1179652
  146.8 49.8 %copy-start.5 = (f32[6,128]{1,0:T(8,128)S(1)}, f32[6,128]{1,0:T(8,128)}, u32[]{:S(2)}) copy-start(f32[6,128]{1,0:T(8,128)} %residual_ref.3) | copy-start | bytes 9220
  146.8 49.8 %copy-start.6 = (f32[6,128]{1,0:T(8,128)S(1)}, f32[6,128]{1,0:T(8,128)}, u32[]{:S(2)}) copy-start(f32[6,128]{1,0:T(8,128)} %cotangent_ref.3) | copy-start | bytes 9220
  171.4 28.2 %copy-start = (bf16[2,6,5,128,128]{4,3,2,1,0:T(8,128)(2,1)S(1)}, bf16[2,6,5,128,128]{4,3,2,1,0:T(8,128)(2,1)}, u32[]{:S(2)}) copy-start(bf16[2,6,5,128,128]{4,3,2,1,0:T(8,128)(2,1)} %get-tuple-element.40.maps_ref) | copy-start | bytes 5898244
  171.4 28.2 %copy-start.4 = (f32[6,8,128]{2,1,0:T(8,128)S(1)}, f32[6,8,128]{2,1,0:T(8,128)}, u32[]{:S(2)}) copy-start(f32[6,8,128]{2,1,0:T(8,128)} %get-tuple-element.41.vectors_ref) | copy-start | bytes 73732
Sparse Core Ops, SparseCore 0:
  10.1 70.3 all-gather.7
  95.8 37.3 all-gather.9

commit v7 on v6

--- a/solution.py
+++ b/solution.py
@@ -27,7 +27,8 @@
     result = pl.pallas_call(
         kernel,
         out_shape=shapes,
-        in_specs=[smem] * scalars + [where] * (len(args) - scalars),
+        in_specs=[smem] * scalars
+        + (where if isinstance(where, list) else [where] * (len(args) - scalars)),
         out_specs=[vmem] * len(shapes),
         scratch_shapes=scratch,
         compiler_params=pltpu.CompilerParams(vmem_limit_bytes=limit * 1024 * 1024),
@@ -169,7 +170,7 @@
     return ref[0, k], ref[1, k]
 
 
-def chain_kernel(lower_ref, upper_ref, chips_ref, outlet_ref, schur_ref, before_ref, after_ref, rows_ref, spread_ref):
+def chain_kernel(lower_ref, upper_ref, chips_ref, outlet_ref, schur_ref, ways_ref, spread_ref):
     chips, half = chips_ref.shape[:2]
     first_s = lax.axis_index("c") * half
     y = lax.axis_index("y")
@@ -205,14 +206,33 @@
             upward = applied_transposed(maps[i], upward) + chips_ref[i, k, WIDTH + 1 : WIDTH + 2]
         payload[half + k] = upward
         keep(schur_ref, k, schur)
-        keep(before_ref, k, before)
-        keep(after_ref, k, after)
-        rows_ref[k : k + 1] = before_row
-        rows_ref[half + k : half + k + 1] = after_row
-    rows_ref[2 * half :] = jnp.zeros((2, WIDTH), F32)
+        for side, matrix, vector in ((0, before, before_row), (1, after, after_row)):
+            ways_ref[side, k, :WIDTH] = matrix
+            ways_ref[side, k, WIDTH:] = jnp.broadcast_to(vector, (8, WIDTH))
     full = jnp.where(row == 2 * half, ids.astype(F32), jnp.concatenate(payload))
     for i in range(spread_ref.shape[0]):
         spread_ref[i] = full
+
+
+def join_kernel(ways_ref, other_ref, passing_ref, enter_ref, leave_ref, rows_ref):
+    half = ways_ref.shape[2]
+    c = lax.axis_index("c")
+    for s in range(other_ref.shape[1]):
+        core, k = s // half, s % half
+        before, after = ways_ref[core, 0, k, :WIDTH], ways_ref[core, 1, k, :WIDTH]
+        enter, leave = (ways_ref[core, side, k, WIDTH : WIDTH + 1] for side in (0, 1))
+        matrix = kept(other_ref, s)
+        further = applied(matrix, enter) + passing_ref[s, 0:1]
+        nearer = applied_transposed(matrix, leave) + passing_ref[s, 1:2]
+        keep(enter_ref, s, jnp.where(c == 1, product(matrix, before), before))
+        keep(leave_ref, s, jnp.where(c == 0, product(after, matrix), after))
+        rows_ref[s] = jnp.concatenate(
+            [
+                jnp.where(c == 1, further, enter),
+                jnp.where(c == 0, nearer, leave),
+                jnp.zeros((6, WIDTH), F32),
+            ]
+        )
 
 
 def pick_kernel(ids_ref, table_ref, out_ref, sems):
@@ -228,12 +248,19 @@
             at = line * owned + (junction - basin * owned)
             here.append(basin - line * dests == x)
             pairs.append((table_ref.at[at], out_ref.at[d, t]))
-    copies = fetch(pairs, sems)
-    for copy in copies:
-        copy.wait()
-    for d in range(dests):
-        for t in range(owned):
-            out_ref[d, t] = jnp.where(here[d * owned + t], out_ref[d, t], 0.0)
+    copies = [
+        pltpu.make_async_copy(source, target, sems.at[i])
+        for i, (source, target) in enumerate(pairs)
+    ]
+    for copy, found, (_, target) in zip(copies, here, pairs):
+        pl.when(found)(copy.start)
+
+        @pl.when(jnp.logical_not(found))
+        def _(target=target):
+            target[...] = jnp.zeros(target.shape, F32)
+
+    for copy, found in zip(copies, here):
+        pl.when(found)(copy.wait)
 
 
 def rule(above, below, half):
@@ -278,6 +305,17 @@
         out_ref[d] = jnp.concatenate(rows)
 
 
+def sums_tiles_kernel(
+    plane_ref, ids_ref, terms_ref, ends_hbm, out_ref, tiles_ref, ends_ref, sems, *, half, cores
+):
+    piece = ends_ref.shape[2]
+    (copy,) = fetch([(ends_hbm.at[:, :, :piece], ends_ref)], sems)
+    sums_kernel(plane_ref, ids_ref, terms_ref, out_ref, half=half, cores=cores, own=False)
+    copy.wait()
+    for k in range(tiles_ref.shape[1]):
+        keep(tiles_ref, k, jnp.concatenate([ends_ref[i, k] for i in range(ends_ref.shape[0])]))
+
+
 def summed(parts_ref):
     total = parts_ref[0]
     for i in range(1, parts_ref.shape[0]):
@@ -297,19 +335,24 @@
     total = total + ends
     for k in range(half):
         other = half + k
-        head, relief = total[k : k + 1], total[other : other + 1]
-        if tiles_ref is not None:
-            head = applied(kept(tiles_ref, k), head)
-            relief = applied_transposed(kept(tiles_ref, other), relief)
+        head = applied(kept(tiles_ref, k), total[k : k + 1])
+        relief = applied_transposed(kept(tiles_ref, other), total[other : other + 1])
         schur = kept(schur_ref, k)
         payload[k] = base[k : k + 1] + applied(schur, head)
         payload[other] = base[other : other + 1] + applied_transposed(schur, relief)
     spread_rows(payload, spread_ref)
 
 
-def partial_kernel(lower_ref, upper_ref, terms_ref, picked_ref, ids_ref, rows_ref, merged_ref, spread_ref, tile_ref):
+def at_root(values):
+    return jnp.where(lax.axis_index("y") == 0, values, 0.0)
+
+
+def partial_kernel(
+    lower_ref, upper_ref, terms_ref, picked_ref, schur_ref, first_ref,
+    ids_ref, rows_ref, base_ref, merged_ref, spread_ref, tile_ref,
+):
     half = picked_ref.shape[1] // 2
-    piece = WIDTH // spread_ref.shape[0]
+    piece = picked_ref.shape[2] - 8
     first_s = lax.axis_index("c") * half
     start = pl.multiple_of(lax.axis_index("y") * piece, 8)
     values = terms_ref[...].reshape(-1, 8, WIDTH)
@@ -327,6 +370,8 @@
         (2 * half, merged_ref.shape[1] - piece - 8, WIDTH), F32
     )
     tile_ref[...] = jnp.zeros(tile_ref.shape, F32)
+    base = at_root(first_ref[0])
+    base_ref[...] = base
     payload = [jnp.zeros((1, WIDTH), F32)] * 8
     ends = [jnp.zeros((1, WIDTH), F32)] * 8
     for k in range(half):
@@ -336,67 +381,60 @@
         ends[half + k] = merged[half + k, piece + 1 : piece + 2]
         tile_ref[k, pl.ds(start, piece)] = merged[k, :piece]
         tile_ref[half + k, pl.ds(start, piece)] = merged[half + k, :piece]
-        payload[k] = applied(tile_ref[k], ends[k] + inflow)
-        payload[half + k] = applied_transposed(tile_ref[half + k], ends[half + k] + outflow)
-    rows_ref[...] = jnp.concatenate(ends)
+        head = applied(tile_ref[k], ends[k] + inflow)
+        relief = applied_transposed(tile_ref[half + k], ends[half + k] + outflow)
+        schur = kept(schur_ref, k)
+        payload[k] = base[k : k + 1] + applied(schur, head)
+        payload[half + k] = base[half + k : half + k + 1] + applied_transposed(schur, relief)
+    rows_ref[...] = at_root(jnp.concatenate(ends))
     spread_rows(payload, spread_ref)
 
 
-def second_kernel(parts_ref, schur_ref, base_ref, spread_ref):
-    step(summed(parts_ref), None, schur_ref, 0.0, base_ref[0], spread_ref)
-
-
-def third_kernel(parts_ref, ends_ref, schur_ref, rows_ref, base_ref, tiles_ref, spread_ref):
-    piece = WIDTH // ends_ref.shape[0]
-    for k in range(tiles_ref.shape[1]):
-        keep(tiles_ref, k, jnp.concatenate([ends_ref[i, k, :piece] for i in range(ends_ref.shape[0])]))
-    step(summed(parts_ref), tiles_ref, schur_ref, rows_ref[...], base_ref[0], spread_ref)
-
-
 def step_kernel(parts_ref, tiles_ref, schur_ref, rows_ref, base_ref, spread_ref):
-    step(summed(parts_ref), tiles_ref, schur_ref, rows_ref[...], base_ref[0], spread_ref)
+    step(summed(parts_ref), tiles_ref, schur_ref, rows_ref[...], base_ref[...], spread_ref)
 
 
 def last_kernel(
-    parts_ref, tiles_ref, rows_ref, before_ref, after_ref, passing_ref,
-    inv_ref, residual_ref, cotangent_ref, shared_ref,
+    parts_ref, tiles_ref, rows_ref, inv_ref, residual_ref, cotangent_ref, spread_ref
 ):
-    half = before_ref.shape[1]
+    half = tiles_ref.shape[1] // 2
     c = lax.axis_index("c")
     total = summed(parts_ref)
     ends = total[:8] + rows_ref[...]
+    residuals, cotangents = at_root(residual_ref[...]), at_root(cotangent_ref[...])
     out = [jnp.zeros((1, WIDTH), F32)] * 16
     for k in range(half):
         other = half + k
-        head = applied(kept(tiles_ref, k), ends[k : k + 1])
-        relief = applied_transposed(kept(tiles_ref, other), ends[other : other + 1])
-        out[k] = applied(kept(before_ref, k), head) + passing_ref[k : k + 1]
-        out[other] = applied_transposed(kept(after_ref, k), relief) + passing_ref[other : other + 1]
-        residual = jnp.where(c == 1, residual_ref[other : other + 1], residual_ref[k : k + 1])
-        cotangent = jnp.where(c == 1, cotangent_ref[other : other + 1], cotangent_ref[k : k + 1])
+        out[k] = applied(kept(tiles_ref, k), ends[k : k + 1])
+        out[other] = applied_transposed(kept(tiles_ref, other), ends[other : other + 1])
+        residual = jnp.where(c == 1, residuals[other : other + 1], residuals[k : k + 1])
+        cotangent = jnp.where(c == 1, cotangents[other : other + 1], cotangents[k : k + 1])
         out[8 + k] = applied(inv_ref[c * half + k], residual + total[8 + k : 9 + k])
         out[8 + other] = cotangent + total[8 + other : 9 + other]
-    shared_ref[...] = jnp.concatenate(out)
+    spread_rows(out, spread_ref)
 
 
 def cells_kernel(
-    shared_ref, other_ref, passing_ref, maps_ref, vectors_ref,
+    shared_ref, enter_ref, leave_ref, rows_ref, maps_ref, vectors_ref,
     update_ref, sections_ref, adjoint_ref, junction_ref,
 ):
     members, blocks = update_ref.shape[:2]
     half = members // 2
-    c = lax.axis_index("c")
+    shared = []
+    for core in range(2):
+        total = shared_ref[core]
+        for i in range(core + 2, shared_ref.shape[0], 2):
+            total = total + shared_ref[i]
+        shared.append(total)
     for s in range(members):
         core, k = s // half, s % half
-        sections_ref[s : s + 1] = shared_ref[core, 8 + k : 9 + k]
-        junction_ref[s : s + 1] = shared_ref[core, 8 + half + k : 9 + half + k]
-        enter = shared_ref[core, k : k + 1]
-        leave = shared_ref[core, half + k : half + k + 1]
-        matrix = kept(other_ref, s)
-        further = applied(matrix, enter) + passing_ref[s, 0:1]
-        nearer = applied_transposed(matrix, leave) + passing_ref[s, 1:2]
-        enter = jnp.where(c == 1, further, enter)
-        leave = jnp.where(c == 0, nearer, leave)
+        sections_ref[s : s + 1] = shared[core][8 + k : 9 + k]
+        junction_ref[s : s + 1] = shared[core][8 + half + k : 9 + half + k]
+        enter = applied(kept(enter_ref, s), shared[core][k : k + 1]) + rows_ref[s, 0:1]
+        leave = (
+            applied_transposed(kept(leave_ref, s), shared[core][half + k : half + k + 1])
+            + rows_ref[s, 1:2]
+        )
         rows, back = [], []
         for i in range(blocks):
             rows.append(
@@ -484,13 +522,19 @@
     )
     chips = lax.all_gather(chip, "y")
     matrices = array(2, half, width, width, dtype=bf16)
-    schur, before, after, passing, first = run(
+    schur, ways, first = run(
         chain_kernel,
-        [matrices, matrices, matrices, array(8, width), array(zs, 8, width)],
+        [matrices, array(2, half, PACK, width), array(zs, 8, width)],
         lower, upper, chips, outlet_link, scalars=2,
     )
 
-    terms = exchanged(first)
+    shared_map = array(2, members, width, width, dtype=bf16)
+    joined = run(
+        join_kernel,
+        [shared_map, shared_map, array(members, 8, width)],
+        lax.all_gather(ways, "c"), other, other_rows,
+    )
+    terms, joined = lax.optimization_barrier((exchanged(first), joined))
     plane = lax.dynamic_slice(
         terms.reshape(cs, xs, zs, 8, width),
         (0, 0, lax.axis_index("z"), 2 * half, 0),
@@ -500,38 +544,41 @@
         pick_kernel, array(xs, owned, piece + 8, width), plane, table,
         scalars=1, where=hbm, limit=60, scratch=[pltpu.SemaphoreType.DMA((xs * owned,))],
     )
-    ids, rows, merged, parts = run(
+    ids, rows, base, merged, spread = run(
         partial_kernel,
         [
             array(zs, 8, width, dtype=jnp.int32),
             array(8, width),
+            array(8, width),
             array(owned, 3 * piece, width),
-            array(ys, 8, width),
+            array(zs, 8, width),
         ],
-        lower, upper, terms, swap(picked, "x"), scalars=2,
+        lower, upper, terms, swap(picked, "x"), schur, first, scalars=2,
         scratch=[pltpu.VMEM((owned, width, width), F32)],
     )
-    parts, merged = lax.optimization_barrier((parts, merged))
+    spread, merged = lax.optimization_barrier((spread, merged))
     ends = lax.all_gather(merged, "y")
     sides = ("x", "c")
-
-    def sums(spread, own):
-        kernel = functools.partial(sums_kernel, half=half, cores=cs, own=own)
-        shape = array(xs * cs, 16 if own else 8, width)
-        return swap(run(kernel, shape, plane, ids, swap(spread, "z"), scalars=1), sides)
-
-    spread = run(second_kernel, array(zs, 8, width), swap(parts, "y"), schur, first)
-    tiles, spread = run(
-        third_kernel,
-        [array(2, 2 * half, width, width, dtype=bf16), array(zs, 8, width)],
-        sums(spread, False), ends, schur, rows, first,
-    )
-    for sweep in range(3, SWEEPS):
+    sizes = dict(half=half, cores=cs)
+    sums, tiles = run(
+        functools.partial(sums_tiles_kernel, **sizes),
+        [array(xs * cs, 8, width), array(2, owned, width, width, dtype=bf16)],
+        plane, ids, swap(spread, "z"), ends,
+        scalars=1, where=[vmem, vmem, hbm], limit=60,
+        scratch=[pltpu.VMEM((ys, owned, piece, width), F32), pltpu.SemaphoreType.DMA((1,))],
+    )
+    for sweep in range(2, SWEEPS):
         spread = run(
-            step_kernel, array(zs, 8, width), sums(spread, False), tiles, schur, rows, first
+            step_kernel, array(zs, 8, width), swap(sums, sides), tiles, schur, rows, base
+        )
+        final = sweep == SWEEPS - 1
+        sums = run(
+            functools.partial(sums_kernel, own=final, **sizes),
+            array(xs * cs, 16 if final else 8, width),
+            plane, ids, swap(spread, "z"), scalars=1,
         )
     shared = run(
-        last_kernel, array(16, width), sums(spread, True), tiles, rows, before, after, passing,
+        last_kernel, array(ys * cs, 16, width), swap(sums, sides), tiles, rows,
         junction_inv, junction_residual, junction_cotangent,
     )
     cell_update, sections, cell_adjoint, adjoint = run(
@@ -540,7 +587,7 @@
             array(members, blocks, width), array(owned, width),
             array(members, blocks, width), array(owned, width),
         ],
-        lax.all_gather(shared, "c"), other, other_rows, maps, vectors,
+        swap(shared, ("y", "c")), *joined, maps, vectors,
     )
     return (cell_update, sections, cell_adjoint, adjoint)
 

time: 209 us -> 227 us (1.086)
  waiting for transfers between devices: 5.56 us -> 29.4 us
  blocking collectives: 157 us -> 137 us
  starting transfers between devices: 4.4 us -> 14.8 us
  Pallas kernels: 24.8 us -> 28.2 us
    all_to_all x9 -> x8, blocking collectives: 128 us -> 105 us  [swap(): return lax.all_to_all(spread, axis, 0, 0, tiled=False)]
    all_gather x1, waiting for transfers between devices: 0.01 us -> 17.8 us  [shards(): ends = lax.all_gather(merged, 'y')]
    all_to_all x1 -> x2, starting transfers between devices: 4.36 us -> 14.8 us  [swap(): return lax.all_to_all(spread, axis, 0, 0, tiled=False)]
    all_to_all x1 -> x2, waiting for transfers between devices: 5.53 us -> 11.6 us  [swap(): return lax.all_to_all(spread, axis, 0, 0, tiled=False)]
    all_gather x1, blocking collectives: 2.27 us -> 5.73 us  [shards(): lax.all_gather(ways, 'c')]
    pallas_call x14, Pallas kernels: 24.8 us -> 28.2 us  [run(): pl.pallas_call(kernel, out_shape=shapes, in_specs=[smem] * scalars + (whe...]
  transfers between devices with their start and end apart: 3 -> 4, of which waited for: 1 -> 2; matrix products, arithmetic and copies ran while one was open for 1% -> 1% of each run, Pallas kernels for 6% -> 6%
where the time goes in v7:
time: 227 us; the launch traced here: 226 us
  blocking collectives  137 us (60%)
  waiting for transfers between devices  29.4 us (13%)
  Pallas kernels  28.2 us (12%)
  starting transfers between devices  14.8 us (7%)
  between operations  14.2 us (6%)
  local copies, waits for them, and re-layouts  2.99 us (1%)
    all_to_all x8, blocking collectives, swap(): return lax.all_to_all(spread, axis, 0, 0, tiled=False)  105 us
    pallas_call x14, Pallas kernels, run(): pl.pallas_call(kernel, out_shape=shapes, in_specs=[smem] * scalars + (whe...  28.2 us
    all_gather x1, waiting for transfers between devices, shards(): ends = lax.all_gather(merged, 'y')  17.8 us
    all_to_all x2, starting transfers between devices, swap(): return lax.all_to_all(spread, axis, 0, 0, tiled=False)  14.8 us
    all_to_all x2, waiting for transfers between devices, swap(): return lax.all_to_all(spread, axis, 0, 0, tiled=False)  11.6 us
    all_gather x1, blocking collectives, shards(): chips = lax.all_gather(chip, 'y')  11.5 us
    all_gather x1, blocking collectives, shards(): pair = lax.all_gather(local, 'c')  9.12 us
    all_gather x1, blocking collectives, shards(): lax.all_gather(ways, 'c')  5.73 us
  transfers between devices with their start and end apart: 4, of which 2 were waited for; matrix products, arithmetic and copies ran while one was open for 1% of the time, Pallas kernels for 6%

profile of v7, /device:TPU:1, one launch (start us, length us, event | category | flops | bytes accessed | tf_op | source)
XLA Modules:
  0.0 226.4 jit_solution(9630711896084080226)
XLA Ops:
  7.2 0.0 all-gather.8.cloned.1.call-start
  7.2 1.6 shard_map.133
  8.8 0.0 all-gather.8.cloned.1.call-update
  8.8 7.7 %shard_map.129 = (bf16[2,6,5,128,128]{4,3,2,1,0:T(8,128)(2,1)}, f32[6,8,128]{2,1,0:T(8,128)}, f32[6,136,128]{2,1,0:T(8,128)}) custom-call(f32[6,3,128,128]{3,2,1,0:T(8,128)} %inv_hbm.1, f32[6,3,128,128]{3,2,1,0:T(8,128)} %link_hbm.1, f32[6,3,128]{2,1,0:T(4,128)} %residual_hbm.1, f32[6,3,128]{2,1,0:T(4,128)} %cotangent_hbm.1), custom_call_target="tpu_custom_call" | custom-call | flops 2000000000 | bytes 20000000 | tf_op jit(solution)/shard_map/pallas_call | solution.py:27
  16.5 9.1 %all-gather = f32[12,136,128]{2,1,0:T(8,128)S(1)} all-gather(f32[6,136,128]{2,1,0:T(8,128)} %get-tuple-element.29), channel_id=2, replica_groups=mesh['z'=16,'x'=4,'y'=4,'c'=2] {'c'}, dimensions={0}, use_global_device_ids=true | all-gather | bytes 1253376 | tf_op jit(solution)/shard_map/all_gather | solution.py:517
  25.6 0.0 copy-start.6
  25.6 0.0 copy-start.11
  25.6 0.0 copy-start.12
  25.6 0.4 shard_map.130
  26.0 11.5 %all-gather.1 = f32[12,136,128]{2,1,0:T(8,128)S(1)} all-gather(f32[3,136,128]{2,1,0:T(8,128)S(1)} %get-tuple-element.30), channel_id=3, replica_groups=mesh['z'=16,'x'=4,'y'=4,'c'=2] {'y'}, dimensions={0}, use_global_device_ids=true | all-gather | bytes 1044480 | tf_op jit(solution)/shard_map/all_gather | solution.py:523
  37.5 0.0 copy-done.6
  37.5 0.0 copy-done.11
  37.6 0.0 copy-done.12
  37.6 4.2 %shard_map.131 = (bf16[2,3,128,128]{3,2,1,0:T(8,128)(2,1)S(1)}, f32[2,3,136,128]{3,2,1,0:T(8,128)S(1)}, f32[16,8,128]{2,1,0:T(8,128)}) custom-call(s32[6]{0:T(128)S(1)} %copy-done.11, s32[6]{0:T(128)S(1)} %copy-done.12, f32[4,3,136,128]{3,2,1,0:T(8,128)S(1)} %bitcast.11, f32[6,128,128]{2,1,0:T(8,128)S(1)} %copy-done.6), custom_call_target="tpu_custom_call" | custom-call | tf_op jit(solution)/shard_map/pallas_call | solution.py:27
  41.8 10.5 %all-to-all-start = ((f32[16,8,128]{2,1,0:T(8,128)}), f32[16,8,128]{2,1,0:T(8,128)S(1)}, u32[]{:S(2)}, u32[]{:S(2)}) async-start(f32[16,8,128]{2,1,0:T(8,128)} %get-tuple-element.31.first_ref), calls=%async_computation | async-start | bytes 131072 | tf_op jit(solution)/shard_map/all_to_all | solution.py:454
  52.3 11.6 %all-to-all-done = f32[16,8,128]{2,1,0:T(8,128)S(1)} async-done(((f32[16,8,128]{2,1,0:T(8,128)}), f32[16,8,128]{2,1,0:T(8,128)S(1)}, u32[]{:S(2)}, u32[]{:S(2)}) %all-to-all-start) | async-done | bytes 65568 | tf_op jit(solution)/shard_map/all_to_all | solution.py:454
  63.9 0.7 broadcast_in_dim.2
  64.6 4.3 %all-to-all-start.1 = ((f32[4,16,8,128]{3,2,1,0:T(8,128)}), f32[4,16,8,128]{3,2,1,0:T(8,128)S(1)}, u32[]{:S(2)}, u32[]{:S(2)}) async-start(f32[4,16,8,128]{3,2,1,0:T(8,128)} %broadcast_in_dim.2), calls=%async_computation.1 | async-start | bytes 524288 | tf_op jit(solution)/shard_map/all_to_all | solution.py:454
  68.9 0.0 all-gather.10.cloned.1.call-start
  68.9 5.7 %all-gather.2 = f32[4,3,136,128]{3,2,1,0:T(8,128)S(1)} all-gather(f32[2,3,136,128]{3,2,1,0:T(8,128)S(1)} %get-tuple-element.32), channel_id=4, replica_groups=mesh['z'=16,'x'=4,'y'=4,'c'=2] {'c'}, dimensions={0}, use_global_device_ids=true | all-gather | bytes 1253376 | tf_op jit(solution)/shard_map/all_gather | solution.py:535
  74.6 0.9 shard_map.132
  75.5 0.0 all-to-all-done.1
  75.5 5.6 %all_gather.37.terms_ref = f32[2,512,128]{2,1,0:T(8,128)S(1)} all-gather(f32[1,512,128]{2,1,0:T(8,128)S(1)} %bitcast.14), channel_id=1, replica_groups=mesh['z'=16,'x'=4,'y'=4,'c'=2] {'c'}, dimensions={0}, use_global_device_ids=true | all-gather | bytes 786432 | tf_op jit(solution)/shard_map/all_gather | solution.py:463
  81.1 0.6 convert_element_type.6.ids_ref.plane_ref
  81.7 0.0 all-gather.8.cloned.1.call-done.table_ref
  81.7 2.7 %shard_map.134 = f32[4,6,40,128]{3,2,1,0:T(8,128)} custom-call(s32[48]{0:T(128)} %convert_element_type.6.ids_ref.plane_ref, f32[96,40,128]{2,1,0:T(8,128)} %all-gather.8.cloned.1.call-done.table_ref), custom_call_target="tpu_custom_call" | custom-call | tf_op jit(solution)/shard_map/pallas_call | solution.py:27
  84.4 10.2 %all_to_all.50.picked_ref = f32[4,6,40,128]{3,2,1,0:T(8,128)S(1)} all-to-all(f32[4,6,40,128]{3,2,1,0:T(8,128)} %shard_map.134), channel_id=1, replica_groups=mesh['z'=16,'x'=4,'y'=4,'c'=2] {'x'}, dimensions={0} | all-to-all | bytes 983040 | tf_op jit(solution)/shard_map/all_to_all | solution.py:454
  94.7 2.3 %shard_map.135 = (s32[16,8,128]{2,1,0:T(8,128)S(1)}, f32[8,128]{1,0:T(8,128)S(1)}, f32[8,128]{1,0:T(8,128)S(1)}, f32[6,96,128]{2,1,0:T(8,128)}, f32[16,8,128]{2,1,0:T(8,128)S(1)}) custom-call(s32[6]{0:T(128)S(1)} %copy-done.11, s32[6]{0:T(128)S(1)} %copy-done.12, f32[2,512,128]{2,1,0:T(8,128)S(1)} %all_gather.37.terms_ref, ...), custom_call_target="tpu_custom_call" | custom-call | tf_op jit(solution)/shard_map/pallas_call | solution.py:27
  97.0 0.0 copy-start.4
  97.0 0.6 copy-done.4
  97.6 0.0 all-gather.10.cloned.1.call-update
  97.6 0.0 copy-start.5
  97.7 0.0 copy-start.10
  97.7 18.7 %all_to_all.51.terms_ref = f32[16,8,128]{2,1,0:T(8,128)} all-to-all(f32[16,8,128]{2,1,0:T(8,128)S(1)} %get-tuple-element.43), channel_id=1, replica_groups=mesh['z'=16,'x'=4,'y'=4,'c'=2] {'z'}, dimensions={0} | all-to-all | bytes 131072 | tf_op jit(solution)/shard_map/all_to_all | solution.py:454
  116.4 17.8 %all-gather.10.cloned.1.call-done = f32[24,96,128]{2,1,0:T(8,128)} async-done(((f32[6,96,128]{2,1,0:T(8,128)}), f32[24,96,128]{2,1,0:T(8,128)}) %all-gather.10.cloned.1.call-update) | async-done | bytes 1179664 | tf_op jit(solution)/shard_map/all_gather | solution.py:560
  134.2 0.0 copy-start.3
  134.2 2.7 %shard_map.136 = (f32[8,8,128]{2,1,0:T(8,128)}, bf16[2,6,128,128]{3,2,1,0:T(8,128)(2,1)}) custom-call(s32[48]{0:T(128)} %convert_element_type.6.ids_ref.plane_ref, s32[16,8,128]{2,1,0:T(8,128)} %copy-done.4, f32[16,8,128]{2,1,0:T(8,128)} %all_to_all.51.terms_ref, f32[4,6,96,128]{3,2,1,0:T(8,128)} %bitcast.13), custom_call_target="tpu_custom_call" | custom-call | tf_op jit(solution)/shard_map/pallas_call | solution.py:27
  136.9 0.0 copy-start.8
  136.9 0.0 copy-start.9
  136.9 10.6 %all_to_all.52.parts_ref = f32[8,8,128]{2,1,0:T(8,128)S(1)} all-to-all(f32[8,8,128]{2,1,0:T(8,128)} %get-tuple-element.45), channel_id=1, replica_groups=mesh['z'=16,'x'=4,'y'=4,'c'=2] {'x','c'}, dimensions={0} | all-to-all | bytes 65536 | tf_op jit(solution)/shard_map/all_to_all | solution.py:454
  147.5 0.0 copy-start
  147.5 1.0 copy-done
  148.5 0.0 copy-start.1
  148.5 0.6 shard_map.137
  149.2 23.4 %all_to_all.53.terms_ref = f32[16,8,128]{2,1,0:T(8,128)S(1)} all-to-all(f32[16,8,128]{2,1,0:T(8,128)S(1)} %shard_map.137), channel_id=1, replica_groups=mesh['z'=16,'x'=4,'y'=4,'c'=2] {'z'}, dimensions={0} | all-to-all | bytes 131072 | tf_op jit(solution)/shard_map/all_to_all | solution.py:454
  172.6 0.0 copy-done.5
  172.6 0.0 copy-done.10
  172.6 0.7 shard_map.138
  173.3 0.0 copy-start.2
  173.3 0.0 copy-start.7
  173.3 9.4 %all_to_all.54.parts_ref = f32[8,8,128]{2,1,0:T(8,128)S(1)} all-to-all(f32[8,8,128]{2,1,0:T(8,128)S(1)} %shard_map.138), channel_id=1, replica_groups=mesh['z'=16,'x'=4,'y'=4,'c'=2] {'x','c'}, dimensions={0} | all-to-all | bytes 65536 | tf_op jit(solution)/shard_map/all_to_all | solution.py:454
  182.7 0.6 shard_map.139
  183.4 14.2 %all_to_all.55.terms_ref = f32[16,8,128]{2,1,0:T(8,128)S(1)} all-to-all(f32[16,8,128]{2,1,0:T(8,128)S(1)} %shard_map.139), channel_id=1, replica_groups=mesh['z'=16,'x'=4,'y'=4,'c'=2] {'z'}, dimensions={0} | all-to-all | bytes 131072 | tf_op jit(solution)/shard_map/all_to_all | solution.py:454
  197.6 0.9 shard_map.140
  198.5 9.3 %all_to_all.56.parts_ref = f32[8,16,128]{2,1,0:T(8,128)S(1)} all-to-all(f32[8,16,128]{2,1,0:T(8,128)S(1)} %shard_map.140), channel_id=1, replica_groups=mesh['z'=16,'x'=4,'y'=4,'c'=2] {'x','c'}, dimensions={0} | all-to-all | bytes 131072 | tf_op jit(solution)/shard_map/all_to_all | solution.py:454
  207.8 0.0 copy-done.3
  207.8 0.0 copy-done.8
  207.8 0.0 copy-done.9
  207.8 0.0 copy-done.1
  207.8 0.4 shard_map.141
  208.2 9.0 %all_to_all.57.shared_ref = f32[8,16,128]{2,1,0:T(8,128)S(1)} all-to-all(f32[8,16,128]{2,1,0:T(8,128)S(1)} %shard_map.141), channel_id=1, replica_groups=mesh['z'=16,'x'=4,'y'=4,'c'=2] {'y','c'}, dimensions={0} | all-to-all | bytes 131072 | tf_op jit(solution)/shard_map/all_to_all | solution.py:454
  217.2 0.0 copy-done.2
  217.2 0.0 copy-done.7
  217.2 2.3 %shard_map.142 = (f32[6,3,128]{2,1,0:T(4,128)}, f32[6,128]{1,0:T(8,128)}, f32[6,3,128]{2,1,0:T(4,128)}, f32[6,128]{1,0:T(8,128)}) custom-call(f32[8,16,128]{2,1,0:T(8,128)S(1)} %all_to_all.57.shared_ref, bf16[2,6,128,128]{3,2,1,0:T(8,128)(2,1)S(1)} %get-tuple-element.49.enter_ref, bf16[2,6,128,128]{3,2,1,0:T(8,128)(2,1)S(1)} %get-tuple-element.50.leave_ref, ...), custom_call_target="tpu_custom_call" | custom-call | tf_op jit(solution)/shard_map/pallas_call | solution.py:27
  (2 shorter events, 0.0 us)
Async XLA Ops:
  7.2 74.5 %all-gather.8.cloned.1.call-start = ((), (), s32[]{:S(2)}) async-start(), calls=%async_computation.10 | async-start | bytes 2088960 | tf_op jit(solution)/shard_map/all_gather | solution.py:497
  25.6 11.9 %copy-start.6 = (f32[6,128,128]{2,1,0:T(8,128)S(1)}, f32[6,128,128]{2,1,0:T(8,128)}, u32[]{:S(2)}) copy-start(f32[6,128,128]{2,1,0:T(8,128)} %outlet_ref.1) | copy-start | bytes 1179652
  25.6 11.9 %copy-start.11 = (s32[6]{0:T(128)S(1)}, s32[6]{0:T(128)}, u32[]{:S(2)}) copy-start(s32[6]{0:T(128)} %lower_ref.3) | copy-start | bytes 76
  25.6 11.9 %copy-start.12 = (s32[6]{0:T(128)S(1)}, s32[6]{0:T(128)}, u32[]{:S(2)}) copy-start(s32[6]{0:T(128)} %upper_ref.3) | copy-start | bytes 76
  41.8 22.1 %all-to-all-start = ((f32[16,8,128]{2,1,0:T(8,128)}), f32[16,8,128]{2,1,0:T(8,128)S(1)}, u32[]{:S(2)}, u32[]{:S(2)}) async-start(f32[16,8,128]{2,1,0:T(8,128)} %get-tuple-element.31.first_ref), calls=%async_computation | async-start | bytes 131072 | tf_op jit(solution)/shard_map/all_to_all | solution.py:454
  64.6 10.9 %all-to-all-start.1 = ((f32[4,16,8,128]{3,2,1,0:T(8,128)}), f32[4,16,8,128]{3,2,1,0:T(8,128)S(1)}, u32[]{:S(2)}, u32[]{:S(2)}) async-start(f32[4,16,8,128]{3,2,1,0:T(8,128)} %broadcast_in_dim.2), calls=%async_computation.1 | async-start | bytes 524288 | tf_op jit(solution)/shard_map/all_to_all | solution.py:454
  68.9 65.3 %all-gather.10.cloned.1.call-start = ((), (), s32[]{:S(2)}) async-start(), calls=%async_computation.11 | async-start | bytes 1474560 | tf_op jit(solution)/shard_map/all_gather | solution.py:560
  97.0 0.6 copy-start.4
  97.6 74.9 %copy-start.5 = (s32[16,8,128]{2,1,0:T(8,128)S(1)}, s32[16,8,128]{2,1,0:T(8,128)}, u32[]{:S(2)}) copy-start(s32[16,8,128]{2,1,0:T(8,128)} %copy-done.4) | copy-start | bytes 196612
  97.7 74.9 %copy-start.10 = (s32[48]{0:T(128)S(1)}, s32[48]{0:T(128)}, u32[]{:S(2)}) copy-start(s32[48]{0:T(128)} %convert_element_type.6.ids_ref.plane_ref) | copy-start | bytes 580
  134.2 73.6 %copy-start.3 = (f32[6,128,128]{2,1,0:T(8,128)S(1)}, f32[6,128,128]{2,1,0:T(8,128)}, u32[]{:S(2)}) copy-start(f32[6,128,128]{2,1,0:T(8,128)} %inv_ref.3) | copy-start | bytes 1179652
  136.9 70.9 %copy-start.8 = (f32[6,128]{1,0:T(8,128)S(1)}, f32[6,128]{1,0:T(8,128)}, u32[]{:S(2)}) copy-start(f32[6,128]{1,0:T(8,128)} %residual_ref.3) | copy-start | bytes 9220
  136.9 70.9 %copy-start.9 = (f32[6,128]{1,0:T(8,128)S(1)}, f32[6,128]{1,0:T(8,128)}, u32[]{:S(2)}) copy-start(f32[6,128]{1,0:T(8,128)} %cotangent_ref.3) | copy-start | bytes 9220
  147.5 1.0 copy-start
  148.5 59.3 %copy-start.1 = (bf16[2,6,128,128]{3,2,1,0:T(8,128)(2,1)S(1)}, bf16[2,6,128,128]{3,2,1,0:T(8,128)(2,1)}, u32[]{:S(2)}) copy-start(bf16[2,6,128,128]{3,2,1,0:T(8,128)(2,1)} %get-tuple-element.46.tiles_ref) | copy-start | bytes 1179652
  173.3 43.9 %copy-start.2 = (bf16[2,6,5,128,128]{4,3,2,1,0:T(8,128)(2,1)S(1)}, bf16[2,6,5,128,128]{4,3,2,1,0:T(8,128)(2,1)}, u32[]{:S(2)}) copy-start(bf16[2,6,5,128,128]{4,3,2,1,0:T(8,128)(2,1)} %get-tuple-element.52.maps_ref) | copy-start | bytes 5898244
  173.3 43.9 %copy-start.7 = (f32[6,8,128]{2,1,0:T(8,128)S(1)}, f32[6,8,128]{2,1,0:T(8,128)}, u32[]{:S(2)}) copy-start(f32[6,8,128]{2,1,0:T(8,128)} %get-tuple-element.53.vectors_ref) | copy-start | bytes 73732
Sparse Core Ops, SparseCore 0:
  10.1 70.3 all-gather.7
  97.8 36.3 all-gather.9

commit v8 on v7

--- a/solution.py
+++ b/solution.py
@@ -235,32 +235,18 @@
         )
 
 
-def pick_kernel(ids_ref, table_ref, out_ref, sems):
+def pick_kernel(ids_ref, table_ref, out_ref):
     dests, owned = out_ref.shape[:2]
     half = owned // 2
     x, c = lax.axis_index("x"), lax.axis_index("c")
-    pairs, here = [], []
     for d in range(dests):
         for t in range(owned):
             junction = ids_ref[(c * dests + d) * owned + (t + half) % owned]
             basin = lax.div(junction, owned)
             line = lax.div(basin, dests)
             at = line * owned + (junction - basin * owned)
-            here.append(basin - line * dests == x)
-            pairs.append((table_ref.at[at], out_ref.at[d, t]))
-    copies = [
-        pltpu.make_async_copy(source, target, sems.at[i])
-        for i, (source, target) in enumerate(pairs)
-    ]
-    for copy, found, (_, target) in zip(copies, here, pairs):
-        pl.when(found)(copy.start)
-
-        @pl.when(jnp.logical_not(found))
-        def _(target=target):
-            target[...] = jnp.zeros(target.shape, F32)
-
-    for copy, found in zip(copies, here):
-        pl.when(found)(copy.wait)
+            here = basin - line * dests == x
+            out_ref[d, t] = jnp.where(here, table_ref[at], 0.0)
 
 
 def rule(above, below, half):
@@ -305,17 +291,6 @@
         out_ref[d] = jnp.concatenate(rows)
 
 
-def sums_tiles_kernel(
-    plane_ref, ids_ref, terms_ref, ends_hbm, out_ref, tiles_ref, ends_ref, sems, *, half, cores
-):
-    piece = ends_ref.shape[2]
-    (copy,) = fetch([(ends_hbm.at[:, :, :piece], ends_ref)], sems)
-    sums_kernel(plane_ref, ids_ref, terms_ref, out_ref, half=half, cores=cores, own=False)
-    copy.wait()
-    for k in range(tiles_ref.shape[1]):
-        keep(tiles_ref, k, jnp.concatenate([ends_ref[i, k] for i in range(ends_ref.shape[0])]))
-
-
 def summed(parts_ref):
     total = parts_ref[0]
     for i in range(1, parts_ref.shape[0]):
@@ -347,21 +322,29 @@
     return jnp.where(lax.axis_index("y") == 0, values, 0.0)
 
 
+def flows_kernel(lower_ref, upper_ref, terms_ref, ids_ref, flows_ref):
+    count = ids_ref.shape[0]
+    half = flows_ref.shape[0] // 2 - 1
+    first_s = lax.axis_index("c") * half
+    values = terms_ref[...].reshape(-1, 8, WIDTH)
+    ids = source_ids(values, half)
+    column = pl.multiple_of(lax.axis_index("x") * count * 8, 8)
+    ids_ref[...] = source_ids(
+        terms_ref[lax.axis_index("c"), pl.ds(column, count * 8)].reshape(ids_ref.shape), half
+    )
+    rows = [jnp.zeros((1, WIDTH), F32)] * 8
+    for k in range(half):
+        pattern = rule(upper_ref[first_s + k], lower_ref[first_s + k], half)
+        rows[k], rows[half + k] = gathered(ids, values, pattern, half)
+    flows_ref[...] = jnp.concatenate(rows)
+
+
 def partial_kernel(
-    lower_ref, upper_ref, terms_ref, picked_ref, schur_ref, first_ref,
-    ids_ref, rows_ref, base_ref, merged_ref, spread_ref, tile_ref,
+    flows_ref, picked_ref, schur_ref, first_ref, rows_ref, base_ref, merged_ref, spread_ref, tile_ref
 ):
     half = picked_ref.shape[1] // 2
     piece = picked_ref.shape[2] - 8
-    first_s = lax.axis_index("c") * half
     start = pl.multiple_of(lax.axis_index("y") * piece, 8)
-    values = terms_ref[...].reshape(-1, 8, WIDTH)
-    ids = source_ids(values, half)
-    count = ids_ref.shape[0] * 8
-    column = pl.multiple_of(lax.axis_index("x") * count, 8)
-    ids_ref[...] = source_ids(
-        terms_ref[lax.axis_index("c"), pl.ds(column, count)].reshape(ids_ref.shape), half
-    )
     merged = picked_ref[0]
     for d in range(1, picked_ref.shape[0]):
         merged = merged + picked_ref[d]
@@ -375,19 +358,25 @@
     payload = [jnp.zeros((1, WIDTH), F32)] * 8
     ends = [jnp.zeros((1, WIDTH), F32)] * 8
     for k in range(half):
-        pattern = rule(upper_ref[first_s + k], lower_ref[first_s + k], half)
-        inflow, outflow = gathered(ids, values, pattern, half)
+        other = half + k
         ends[k] = merged[k, piece : piece + 1]
-        ends[half + k] = merged[half + k, piece + 1 : piece + 2]
+        ends[other] = merged[other, piece + 1 : piece + 2]
         tile_ref[k, pl.ds(start, piece)] = merged[k, :piece]
-        tile_ref[half + k, pl.ds(start, piece)] = merged[half + k, :piece]
-        head = applied(tile_ref[k], ends[k] + inflow)
-        relief = applied_transposed(tile_ref[half + k], ends[half + k] + outflow)
+        tile_ref[other, pl.ds(start, piece)] = merged[other, :piece]
+        head = applied(tile_ref[k], ends[k] + flows_ref[k : k + 1])
+        relief = applied_transposed(tile_ref[other], ends[other] + flows_ref[other : other + 1])
         schur = kept(schur_ref, k)
         payload[k] = base[k : k + 1] + applied(schur, head)
-        payload[half + k] = base[half + k : half + k + 1] + applied_transposed(schur, relief)
+        payload[other] = base[other : other + 1] + applied_transposed(schur, relief)
     rows_ref[...] = at_root(jnp.concatenate(ends))
     spread_rows(payload, spread_ref)
+
+
+def tiles_step_kernel(parts_ref, ends_ref, schur_ref, rows_ref, base_ref, tiles_ref, spread_ref):
+    piece = WIDTH // ends_ref.shape[0]
+    for k in range(tiles_ref.shape[1]):
+        keep(tiles_ref, k, jnp.concatenate([ends_ref[i, k, :piece] for i in range(ends_ref.shape[0])]))
+    step_kernel(parts_ref, tiles_ref, schur_ref, rows_ref, base_ref, spread_ref)
 
 
 def step_kernel(parts_ref, tiles_ref, schur_ref, rows_ref, base_ref, spread_ref):
@@ -540,45 +529,44 @@
         (0, 0, lax.axis_index("z"), 2 * half, 0),
         (cs, xs, 1, 1, owned),
     ).reshape(-1).astype(jnp.int32)
-    picked = run(
-        pick_kernel, array(xs, owned, piece + 8, width), plane, table,
-        scalars=1, where=hbm, limit=60, scratch=[pltpu.SemaphoreType.DMA((xs * owned,))],
-    )
-    ids, rows, base, merged, spread = run(
+    ids, flows = run(
+        flows_kernel,
+        [array(zs, 8, width, dtype=jnp.int32), array(8, width)],
+        lower, upper, terms, scalars=2,
+    )
+    plane, flows = lax.optimization_barrier((plane, flows))
+    picked = run(pick_kernel, array(xs, owned, piece + 8, width), plane, table, scalars=1)
+    rows, base, merged, spread = run(
         partial_kernel,
         [
-            array(zs, 8, width, dtype=jnp.int32),
             array(8, width),
             array(8, width),
-            array(owned, 3 * piece, width),
+            array(owned, 2 * piece + 24, width),
             array(zs, 8, width),
         ],
-        lower, upper, terms, swap(picked, "x"), schur, first, scalars=2,
+        flows, swap(picked, "x"), schur, first,
         scratch=[pltpu.VMEM((owned, width, width), F32)],
     )
     spread, merged = lax.optimization_barrier((spread, merged))
     ends = lax.all_gather(merged, "y")
     sides = ("x", "c")
-    sizes = dict(half=half, cores=cs)
-    sums, tiles = run(
-        functools.partial(sums_tiles_kernel, **sizes),
-        [array(xs * cs, 8, width), array(2, owned, width, width, dtype=bf16)],
-        plane, ids, swap(spread, "z"), ends,
-        scalars=1, where=[vmem, vmem, hbm], limit=60,
-        scratch=[pltpu.VMEM((ys, owned, piece, width), F32), pltpu.SemaphoreType.DMA((1,))],
-    )
-    for sweep in range(2, SWEEPS):
+
+    def sums(spread, own):
+        kernel = functools.partial(sums_kernel, half=half, cores=cs, own=own)
+        shape = array(xs * cs, 16 if own else 8, width)
+        return swap(run(kernel, shape, plane, ids, swap(spread, "z"), scalars=1), sides)
+
+    tiles, spread = run(
+        tiles_step_kernel,
+        [array(2, owned, width, width, dtype=bf16), array(zs, 8, width)],
+        sums(spread, False), ends, schur, rows, base,
+    )
+    for sweep in range(3, SWEEPS):
         spread = run(
-            step_kernel, array(zs, 8, width), swap(sums, sides), tiles, schur, rows, base
-        )
-        final = sweep == SWEEPS - 1
-        sums = run(
-            functools.partial(sums_kernel, own=final, **sizes),
-            array(xs * cs, 16 if final else 8, width),
-            plane, ids, swap(spread, "z"), scalars=1,
+            step_kernel, array(zs, 8, width), sums(spread, False), tiles, schur, rows, base
         )
     shared = run(
-        last_kernel, array(ys * cs, 16, width), swap(sums, sides), tiles, rows,
+        last_kernel, array(ys * cs, 16, width), sums(spread, True), tiles, rows,
         junction_inv, junction_residual, junction_cotangent,
     )
     cell_update, sections, cell_adjoint, adjoint = run(

time: 227 us -> 215 us (0.947)
  waiting for transfers between devices: 29.4 us -> 11.8 us
  blocking collectives: 137 us -> 145 us
  Pallas kernels: 28.2 us -> 24.7 us
    all_gather x1, waiting for transfers between devices: 17.8 us -> 0.01 us  [shards(): ends = lax.all_gather(merged, 'y')]
    all_to_all x8, blocking collectives: 105 us -> 113 us  [swap(): return lax.all_to_all(spread, axis, 0, 0, tiled=False)]
    pallas_call x14 -> x15, Pallas kernels: 28.2 us -> 24.7 us  [run(): pl.pallas_call(kernel, out_shape=shapes, in_specs=[smem] * scalars + (whe...]
  transfers between devices with their start and end apart: 4 -> 4, of which waited for: 2 -> 1; matrix products, arithmetic and copies ran while one was open for 1% -> 0% of each run, Pallas kernels for 6% -> 7%
where the time goes in v8:
time: 215 us; the launch traced here: 214 us
  blocking collectives  145 us (67%)
  Pallas kernels  24.7 us (11%)
  starting transfers between devices  14.6 us (7%)
  between operations  14.2 us (7%)
  waiting for transfers between devices  11.8 us (5%)
  local copies, waits for them, and re-layouts  3.63 us (2%)
    all_to_all x8, blocking collectives, swap(): return lax.all_to_all(spread, axis, 0, 0, tiled=False)  113 us
    pallas_call x15, Pallas kernels, run(): pl.pallas_call(kernel, out_shape=shapes, in_specs=[smem] * scalars + (whe...  24.7 us
    all_to_all x2, starting transfers between devices, swap(): return lax.all_to_all(spread, axis, 0, 0, tiled=False)  14.6 us
    all_to_all x2, waiting for transfers between devices, swap(): return lax.all_to_all(spread, axis, 0, 0, tiled=False)  11.8 us
    all_gather x1, blocking collectives, shards(): chips = lax.all_gather(chip, 'y')  11.5 us
    all_gather x1, blocking collectives, shards(): pair = lax.all_gather(local, 'c')  9.12 us
    all_gather x1, blocking collectives, shards(): lax.all_gather(ways, 'c')  5.85 us
    all_gather x1, blocking collectives, exchanged(): return lax.all_gather(along_x.reshape(-1, WIDTH), 'c')  5.57 us
  transfers between devices with their start and end apart: 4, of which 1 were waited for; matrix products, arithmetic and copies ran while one was open for 0% of the time, Pallas kernels for 7%

profile of v8, /device:TPU:1, one launch (start us, length us, event | category | flops | bytes accessed | tf_op | source)
XLA Modules:
  0.0 213.9 jit_solution(568636733835664255)
XLA Ops:
  7.2 0.0 all-gather.8.cloned.1.call-start
  7.2 1.6 shard_map.134
  8.8 0.0 all-gather.8.cloned.1.call-update
  8.8 7.7 %shard_map.129 = (bf16[2,6,5,128,128]{4,3,2,1,0:T(8,128)(2,1)}, f32[6,8,128]{2,1,0:T(8,128)}, f32[6,136,128]{2,1,0:T(8,128)}) custom-call(f32[6,3,128,128]{3,2,1,0:T(8,128)} %inv_hbm.1, f32[6,3,128,128]{3,2,1,0:T(8,128)} %link_hbm.1, f32[6,3,128]{2,1,0:T(4,128)} %residual_hbm.1, f32[6,3,128]{2,1,0:T(4,128)} %cotangent_hbm.1), custom_call_target="tpu_custom_call" | custom-call | flops 2000000000 | bytes 20000000 | tf_op jit(solution)/shard_map/pallas_call | solution.py:27
  16.5 9.1 %all-gather = f32[12,136,128]{2,1,0:T(8,128)S(1)} all-gather(f32[6,136,128]{2,1,0:T(8,128)} %get-tuple-element.32), channel_id=2, replica_groups=mesh['z'=16,'x'=4,'y'=4,'c'=2] {'c'}, dimensions={0}, use_global_device_ids=true | all-gather | bytes 1253376 | tf_op jit(solution)/shard_map/all_gather | solution.py:506
  25.6 0.0 copy-start.4
  25.6 0.0 copy-start.8
  25.6 0.0 copy-start.9
  25.6 0.4 shard_map.130
  26.0 11.5 %all-gather.1 = f32[12,136,128]{2,1,0:T(8,128)S(1)} all-gather(f32[3,136,128]{2,1,0:T(8,128)S(1)} %get-tuple-element.33), channel_id=3, replica_groups=mesh['z'=16,'x'=4,'y'=4,'c'=2] {'y'}, dimensions={0}, use_global_device_ids=true | all-gather | bytes 1044480 | tf_op jit(solution)/shard_map/all_gather | solution.py:512
  37.5 0.0 copy-done.4
  37.5 0.0 copy-done.8
  37.5 0.0 copy-done.9
  37.5 4.2 %shard_map.131 = (bf16[2,3,128,128]{3,2,1,0:T(8,128)(2,1)S(1)}, f32[2,3,136,128]{3,2,1,0:T(8,128)S(1)}, f32[16,8,128]{2,1,0:T(8,128)}) custom-call(s32[6]{0:T(128)S(1)} %copy-done.8, s32[6]{0:T(128)S(1)} %copy-done.9, f32[4,3,136,128]{3,2,1,0:T(8,128)S(1)} %bitcast.11, f32[6,128,128]{2,1,0:T(8,128)S(1)} %copy-done.4), custom_call_target="tpu_custom_call" | custom-call | tf_op jit(solution)/shard_map/pallas_call | solution.py:27
  41.8 10.5 %all-to-all-start = ((f32[16,8,128]{2,1,0:T(8,128)}), f32[16,8,128]{2,1,0:T(8,128)S(1)}, u32[]{:S(2)}, u32[]{:S(2)}) async-start(f32[16,8,128]{2,1,0:T(8,128)} %get-tuple-element.34.first_ref), calls=%async_computation | async-start | bytes 131072 | tf_op jit(solution)/shard_map/all_to_all | solution.py:443
  52.3 11.8 %all-to-all-done = f32[16,8,128]{2,1,0:T(8,128)S(1)} async-done(((f32[16,8,128]{2,1,0:T(8,128)}), f32[16,8,128]{2,1,0:T(8,128)S(1)}, u32[]{:S(2)}, u32[]{:S(2)}) %all-to-all-start) | async-done | bytes 65568 | tf_op jit(solution)/shard_map/all_to_all | solution.py:443
  64.1 0.7 broadcast_in_dim.2
  64.8 4.0 %all-to-all-start.1 = ((f32[4,16,8,128]{3,2,1,0:T(8,128)}), f32[4,16,8,128]{3,2,1,0:T(8,128)S(1)}, u32[]{:S(2)}, u32[]{:S(2)}) async-start(f32[4,16,8,128]{3,2,1,0:T(8,128)} %broadcast_in_dim.2), calls=%async_computation.1 | async-start | bytes 524288 | tf_op jit(solution)/shard_map/all_to_all | solution.py:443
  68.8 0.0 all-gather.10.cloned.1.call-start
  68.8 5.8 %all-gather.2 = f32[4,3,136,128]{3,2,1,0:T(8,128)S(1)} all-gather(f32[2,3,136,128]{3,2,1,0:T(8,128)S(1)} %get-tuple-element.35), channel_id=4, replica_groups=mesh['z'=16,'x'=4,'y'=4,'c'=2] {'c'}, dimensions={0}, use_global_device_ids=true | all-gather | bytes 1253376 | tf_op jit(solution)/shard_map/all_gather | solution.py:524
  74.7 0.9 shard_map.132
  75.6 0.0 all-to-all-done.1
  75.6 5.6 %all_gather.37.terms_ref = f32[2,512,128]{2,1,0:T(8,128)S(1)} all-gather(f32[1,512,128]{2,1,0:T(8,128)S(1)} %bitcast.14), channel_id=1, replica_groups=mesh['z'=16,'x'=4,'y'=4,'c'=2] {'c'}, dimensions={0}, use_global_device_ids=true | all-gather | bytes 786432 | tf_op jit(solution)/shard_map/all_gather | solution.py:452
  81.1 0.8 shard_map.133
  82.0 0.1 convert_element_type.7.ids_ref.plane_ref
  82.1 0.0 all-gather.8.cloned.1.call-done.table_ref
  82.1 0.0 copy-start.1
  82.1 1.5 copy-done.1
  83.6 0.7 shard_map.135
  84.4 9.1 %all_to_all.50.picked_ref = f32[4,6,40,128]{3,2,1,0:T(8,128)S(1)} all-to-all(f32[4,6,40,128]{3,2,1,0:T(8,128)S(1)} %shard_map.135), channel_id=1, replica_groups=mesh['z'=16,'x'=4,'y'=4,'c'=2] {'x'}, dimensions={0} | all-to-all | bytes 983040 | tf_op jit(solution)/shard_map/all_to_all | solution.py:443
  93.5 2.0 shard_map.136
  95.5 0.0 all-gather.10.cloned.1.call-update
  95.5 19.0 %all_to_all.51.terms_ref = f32[16,8,128]{2,1,0:T(8,128)S(1)} all-to-all(f32[16,8,128]{2,1,0:T(8,128)S(1)} %get-tuple-element.49), channel_id=1, replica_groups=mesh['z'=16,'x'=4,'y'=4,'c'=2] {'z'}, dimensions={0} | all-to-all | bytes 131072 | tf_op jit(solution)/shard_map/all_to_all | solution.py:443
  114.5 0.7 shard_map.137
  115.3 18.9 %all_to_all.52.parts_ref = f32[8,8,128]{2,1,0:T(8,128)S(1)} all-to-all(f32[8,8,128]{2,1,0:T(8,128)S(1)} %shard_map.137), channel_id=1, replica_groups=mesh['z'=16,'x'=4,'y'=4,'c'=2] {'x','c'}, dimensions={0} | all-to-all | bytes 65536 | tf_op jit(solution)/shard_map/all_to_all | solution.py:443
  134.2 0.0 all-gather.10.cloned.1.call-done
  134.2 0.0 copy-start.3
  134.2 1.2 copy-done.3
  135.4 0.0 copy-start.2
  135.4 0.0 copy-start.6
  135.4 0.0 copy-start.7
  135.4 0.7 shard_map.138
  136.1 21.5 %all_to_all.53.terms_ref = f32[16,8,128]{2,1,0:T(8,128)S(1)} all-to-all(f32[16,8,128]{2,1,0:T(8,128)S(1)} %get-tuple-element.53), channel_id=1, replica_groups=mesh['z'=16,'x'=4,'y'=4,'c'=2] {'z'}, dimensions={0} | all-to-all | bytes 131072 | tf_op jit(solution)/shard_map/all_to_all | solution.py:443
  157.6 0.7 shard_map.139
  158.3 0.0 copy-start
  158.3 0.0 copy-start.5
  158.3 12.1 %all_to_all.54.parts_ref = f32[8,8,128]{2,1,0:T(8,128)S(1)} all-to-all(f32[8,8,128]{2,1,0:T(8,128)S(1)} %shard_map.139), channel_id=1, replica_groups=mesh['z'=16,'x'=4,'y'=4,'c'=2] {'x','c'}, dimensions={0} | all-to-all | bytes 65536 | tf_op jit(solution)/shard_map/all_to_all | solution.py:443
  170.4 0.6 shard_map.140
  171.0 14.2 %all_to_all.55.terms_ref = f32[16,8,128]{2,1,0:T(8,128)S(1)} all-to-all(f32[16,8,128]{2,1,0:T(8,128)S(1)} %shard_map.140), channel_id=1, replica_groups=mesh['z'=16,'x'=4,'y'=4,'c'=2] {'z'}, dimensions={0} | all-to-all | bytes 131072 | tf_op jit(solution)/shard_map/all_to_all | solution.py:443
  185.3 0.9 shard_map.141
  186.2 9.2 %all_to_all.56.parts_ref = f32[8,16,128]{2,1,0:T(8,128)S(1)} all-to-all(f32[8,16,128]{2,1,0:T(8,128)S(1)} %shard_map.141), channel_id=1, replica_groups=mesh['z'=16,'x'=4,'y'=4,'c'=2] {'x','c'}, dimensions={0} | all-to-all | bytes 131072 | tf_op jit(solution)/shard_map/all_to_all | solution.py:443
  195.4 0.0 copy-done.2
  195.4 0.0 copy-done.6
  195.4 0.0 copy-done.7
  195.4 0.4 shard_map.142
  195.8 8.9 %all_to_all.57.shared_ref = f32[8,16,128]{2,1,0:T(8,128)S(1)} all-to-all(f32[8,16,128]{2,1,0:T(8,128)S(1)} %shard_map.142), channel_id=1, replica_groups=mesh['z'=16,'x'=4,'y'=4,'c'=2] {'y','c'}, dimensions={0} | all-to-all | bytes 131072 | tf_op jit(solution)/shard_map/all_to_all | solution.py:443
  204.7 0.0 copy-done
  204.7 0.0 copy-done.5
  204.7 2.3 %shard_map.143 = (f32[6,3,128]{2,1,0:T(4,128)}, f32[6,128]{1,0:T(8,128)}, f32[6,3,128]{2,1,0:T(4,128)}, f32[6,128]{1,0:T(8,128)}) custom-call(f32[8,16,128]{2,1,0:T(8,128)S(1)} %all_to_all.57.shared_ref, bf16[2,6,128,128]{3,2,1,0:T(8,128)(2,1)S(1)} %get-tuple-element.55.enter_ref, bf16[2,6,128,128]{3,2,1,0:T(8,128)(2,1)S(1)} %get-tuple-element.56.leave_ref, ...), custom_call_target="tpu_custom_call" | custom-call | tf_op jit(solution)/shard_map/pallas_call | solution.py:27
  (2 shorter events, 0.0 us)
Async XLA Ops:
  7.2 74.9 %all-gather.8.cloned.1.call-start = ((), (), s32[]{:S(2)}) async-start(), calls=%async_computation.10 | async-start | bytes 2088960 | tf_op jit(solution)/shard_map/all_gather | solution.py:486
  25.6 11.9 %copy-start.4 = (f32[6,128,128]{2,1,0:T(8,128)S(1)}, f32[6,128,128]{2,1,0:T(8,128)}, u32[]{:S(2)}) copy-start(f32[6,128,128]{2,1,0:T(8,128)} %outlet_ref.1) | copy-start | bytes 1179652
  25.6 11.9 %copy-start.8 = (s32[6]{0:T(128)S(1)}, s32[6]{0:T(128)}, u32[]{:S(2)}) copy-start(s32[6]{0:T(128)} %lower_ref.3) | copy-start | bytes 76
  25.6 11.9 %copy-start.9 = (s32[6]{0:T(128)S(1)}, s32[6]{0:T(128)}, u32[]{:S(2)}) copy-start(s32[6]{0:T(128)} %upper_ref.3) | copy-start | bytes 76
  41.8 22.3 %all-to-all-start = ((f32[16,8,128]{2,1,0:T(8,128)}), f32[16,8,128]{2,1,0:T(8,128)S(1)}, u32[]{:S(2)}, u32[]{:S(2)}) async-start(f32[16,8,128]{2,1,0:T(8,128)} %get-tuple-element.34.first_ref), calls=%async_computation | async-start | bytes 131072 | tf_op jit(solution)/shard_map/all_to_all | solution.py:443
  64.8 10.8 %all-to-all-start.1 = ((f32[4,16,8,128]{3,2,1,0:T(8,128)}), f32[4,16,8,128]{3,2,1,0:T(8,128)S(1)}, u32[]{:S(2)}, u32[]{:S(2)}) async-start(f32[4,16,8,128]{3,2,1,0:T(8,128)} %broadcast_in_dim.2), calls=%async_computation.1 | async-start | bytes 524288 | tf_op jit(solution)/shard_map/all_to_all | solution.py:443
  68.8 65.3 %all-gather.10.cloned.1.call-start = ((), (), s32[]{:S(2)}) async-start(), calls=%async_computation.11 | async-start | bytes 1351680 | tf_op jit(solution)/shard_map/all_gather | solution.py:551
  82.1 1.6 copy-start.1
  134.2 1.2 copy-start.3
  135.4 60.0 %copy-start.2 = (f32[6,128,128]{2,1,0:T(8,128)S(1)}, f32[6,128,128]{2,1,0:T(8,128)}, u32[]{:S(2)}) copy-start(f32[6,128,128]{2,1,0:T(8,128)} %inv_ref.3) | copy-start | bytes 1179652
  135.4 60.0 %copy-start.6 = (f32[6,128]{1,0:T(8,128)S(1)}, f32[6,128]{1,0:T(8,128)}, u32[]{:S(2)}) copy-start(f32[6,128]{1,0:T(8,128)} %residual_ref.3) | copy-start | bytes 9220
  135.4 60.0 %copy-start.7 = (f32[6,128]{1,0:T(8,128)S(1)}, f32[6,128]{1,0:T(8,128)}, u32[]{:S(2)}) copy-start(f32[6,128]{1,0:T(8,128)} %cotangent_ref.3) | copy-start | bytes 9220
  158.3 46.4 %copy-start = (bf16[2,6,5,128,128]{4,3,2,1,0:T(8,128)(2,1)S(1)}, bf16[2,6,5,128,128]{4,3,2,1,0:T(8,128)(2,1)}, u32[]{:S(2)}) copy-start(bf16[2,6,5,128,128]{4,3,2,1,0:T(8,128)(2,1)} %get-tuple-element.58.maps_ref) | copy-start | bytes 5898244
  158.3 46.4 %copy-start.5 = (f32[6,8,128]{2,1,0:T(8,128)S(1)}, f32[6,8,128]{2,1,0:T(8,128)}, u32[]{:S(2)}) copy-start(f32[6,8,128]{2,1,0:T(8,128)} %get-tuple-element.59.vectors_ref) | copy-start | bytes 73732
Sparse Core Ops, SparseCore 0:
  10.1 70.0 all-gather.7
  95.6 36.5 all-gather.9

commit v9 on v6

--- a/solution.py
+++ b/solution.py
@@ -215,25 +215,18 @@
         spread_ref[i] = full
 
 
-def pick_kernel(ids_ref, table_ref, out_ref, sems):
+def pick_kernel(ids_ref, table_ref, out_ref):
     dests, owned = out_ref.shape[:2]
     half = owned // 2
     x, c = lax.axis_index("x"), lax.axis_index("c")
-    pairs, here = [], []
     for d in range(dests):
         for t in range(owned):
             junction = ids_ref[(c * dests + d) * owned + (t + half) % owned]
             basin = lax.div(junction, owned)
             line = lax.div(basin, dests)
             at = line * owned + (junction - basin * owned)
-            here.append(basin - line * dests == x)
-            pairs.append((table_ref.at[at], out_ref.at[d, t]))
-    copies = fetch(pairs, sems)
-    for copy in copies:
-        copy.wait()
-    for d in range(dests):
-        for t in range(owned):
-            out_ref[d, t] = jnp.where(here[d * owned + t], out_ref[d, t], 0.0)
+            here = basin - line * dests == x
+            out_ref[d, t] = jnp.where(here, table_ref[at], 0.0)
 
 
 def rule(above, below, half):
@@ -307,18 +300,27 @@
     spread_rows(payload, spread_ref)
 
 
-def partial_kernel(lower_ref, upper_ref, terms_ref, picked_ref, ids_ref, rows_ref, merged_ref, spread_ref, tile_ref):
-    half = picked_ref.shape[1] // 2
-    piece = WIDTH // spread_ref.shape[0]
+def flows_kernel(lower_ref, upper_ref, terms_ref, ids_ref, flows_ref):
+    count = ids_ref.shape[0]
+    half = flows_ref.shape[0] // 2 - 1
     first_s = lax.axis_index("c") * half
-    start = pl.multiple_of(lax.axis_index("y") * piece, 8)
     values = terms_ref[...].reshape(-1, 8, WIDTH)
     ids = source_ids(values, half)
-    count = ids_ref.shape[0] * 8
-    column = pl.multiple_of(lax.axis_index("x") * count, 8)
+    column = pl.multiple_of(lax.axis_index("x") * count * 8, 8)
     ids_ref[...] = source_ids(
-        terms_ref[lax.axis_index("c"), pl.ds(column, count)].reshape(ids_ref.shape), half
-    )
+        terms_ref[lax.axis_index("c"), pl.ds(column, count * 8)].reshape(ids_ref.shape), half
+    )
+    rows = [jnp.zeros((1, WIDTH), F32)] * 8
+    for k in range(half):
+        pattern = rule(upper_ref[first_s + k], lower_ref[first_s + k], half)
+        rows[k], rows[half + k] = gathered(ids, values, pattern, half)
+    flows_ref[...] = jnp.concatenate(rows)
+
+
+def partial_kernel(flows_ref, picked_ref, rows_ref, merged_ref, spread_ref, tile_ref):
+    half = picked_ref.shape[1] // 2
+    piece = picked_ref.shape[2] - 8
+    start = pl.multiple_of(lax.axis_index("y") * piece, 8)
     merged = picked_ref[0]
     for d in range(1, picked_ref.shape[0]):
         merged = merged + picked_ref[d]
@@ -330,14 +332,15 @@
     payload = [jnp.zeros((1, WIDTH), F32)] * 8
     ends = [jnp.zeros((1, WIDTH), F32)] * 8
     for k in range(half):
-        pattern = rule(upper_ref[first_s + k], lower_ref[first_s + k], half)
-        inflow, outflow = gathered(ids, values, pattern, half)
+        other = half + k
         ends[k] = merged[k, piece : piece + 1]
-        ends[half + k] = merged[half + k, piece + 1 : piece + 2]
+        ends[other] = merged[other, piece + 1 : piece + 2]
         tile_ref[k, pl.ds(start, piece)] = merged[k, :piece]
-        tile_ref[half + k, pl.ds(start, piece)] = merged[half + k, :piece]
-        payload[k] = applied(tile_ref[k], ends[k] + inflow)
-        payload[half + k] = applied_transposed(tile_ref[half + k], ends[half + k] + outflow)
+        tile_ref[other, pl.ds(start, piece)] = merged[other, :piece]
+        payload[k] = applied(tile_ref[k], ends[k] + flows_ref[k : k + 1])
+        payload[other] = applied_transposed(
+            tile_ref[other], ends[other] + flows_ref[other : other + 1]
+        )
     rows_ref[...] = jnp.concatenate(ends)
     spread_rows(payload, spread_ref)
 
@@ -496,19 +499,17 @@
         (0, 0, lax.axis_index("z"), 2 * half, 0),
         (cs, xs, 1, 1, owned),
     ).reshape(-1).astype(jnp.int32)
-    picked = run(
-        pick_kernel, array(xs, owned, piece + 8, width), plane, table,
-        scalars=1, where=hbm, limit=60, scratch=[pltpu.SemaphoreType.DMA((xs * owned,))],
-    )
-    ids, rows, merged, parts = run(
+    ids, flows = run(
+        flows_kernel,
+        [array(zs, 8, width, dtype=jnp.int32), array(8, width)],
+        lower, upper, terms, scalars=2,
+    )
+    plane, flows = lax.optimization_barrier((plane, flows))
+    picked = run(pick_kernel, array(xs, owned, piece + 8, width), plane, table, scalars=1)
+    rows, merged, parts = run(
         partial_kernel,
-        [
-            array(zs, 8, width, dtype=jnp.int32),
-            array(8, width),
-            array(owned, 3 * piece, width),
-            array(ys, 8, width),
-        ],
-        lower, upper, terms, swap(picked, "x"), scalars=2,
+        [array(8, width), array(owned, 2 * piece + 24, width), array(ys, 8, width)],
+        flows, swap(picked, "x"),
         scratch=[pltpu.VMEM((owned, width, width), F32)],
     )
     parts, merged = lax.optimization_barrier((parts, merged))

time: 209 us -> 208 us (level)
    pallas_call x14 -> x15, Pallas kernels: 24.8 us -> 22.8 us  [run(): pl.pallas_call(kernel, out_shape=shapes, in_specs=[smem] * scalars + [whe...]
  transfers between devices with their start and end apart: 3 -> 3, of which waited for: 1 -> 1; matrix products, arithmetic and copies ran while one was open for 1% -> 0% of each run, Pallas kernels for 6% -> 7%
where the time goes in v9:
time: 208 us; the launch traced here: 207 us
  blocking collectives  157 us (75%)
  Pallas kernels  22.8 us (11%)
  between operations  14.1 us (7%)
  waiting for transfers between devices  5.56 us (3%)
  starting transfers between devices  4.38 us (2%)
  local copies, waits for them, and re-layouts  3.63 us (2%)
    all_to_all x9, blocking collectives, swap(): return lax.all_to_all(spread, axis, 0, 0, tiled=False)  127 us
    pallas_call x15, Pallas kernels, run(): pl.pallas_call(kernel, out_shape=shapes, in_specs=[smem] * scalars + [whe...  22.8 us
    all_gather x1, blocking collectives, shards(): chips = lax.all_gather(chip, 'y')  11.5 us
    all_gather x1, blocking collectives, shards(): pair = lax.all_gather(local, 'c')  9.12 us
    all_gather x1, blocking collectives, exchanged(): return lax.all_gather(along_x.reshape(-1, WIDTH), 'c')  6.38 us
    all_to_all x1, waiting for transfers between devices, swap(): return lax.all_to_all(spread, axis, 0, 0, tiled=False)  5.53 us
    all_to_all x1, starting transfers between devices, swap(): return lax.all_to_all(spread, axis, 0, 0, tiled=False)  4.34 us
  transfers between devices with their start and end apart: 3, of which 1 were waited for; matrix products, arithmetic and copies ran while one was open for 0% of the time, Pallas kernels for 7%

profile of v9, /device:TPU:1, one launch (start us, length us, event | category | flops | bytes accessed | tf_op | source)
XLA Modules:
  0.0 207.1 jit_solution(15785072804433384847)
XLA Ops:
  7.2 0.0 all-gather.8.cloned.1.call-start
  7.2 1.6 shard_map.133
  8.8 0.0 all-gather.8.cloned.1.call-update
  8.8 7.7 %shard_map.129 = (bf16[2,6,5,128,128]{4,3,2,1,0:T(8,128)(2,1)}, f32[6,8,128]{2,1,0:T(8,128)}, f32[6,136,128]{2,1,0:T(8,128)}) custom-call(f32[6,3,128,128]{3,2,1,0:T(8,128)} %inv_hbm.1, f32[6,3,128,128]{3,2,1,0:T(8,128)} %link_hbm.1, f32[6,3,128]{2,1,0:T(4,128)} %residual_hbm.1, f32[6,3,128]{2,1,0:T(4,128)} %cotangent_hbm.1), custom_call_target="tpu_custom_call" | custom-call | flops 2000000000 | bytes 20000000 | tf_op jit(solution)/shard_map/pallas_call | solution.py:27
  16.5 9.1 %all-gather = f32[12,136,128]{2,1,0:T(8,128)S(1)} all-gather(f32[6,136,128]{2,1,0:T(8,128)} %get-tuple-element.26), channel_id=2, replica_groups=mesh['z'=16,'x'=4,'y'=4,'c'=2] {'c'}, dimensions={0}, use_global_device_ids=true | all-gather | bytes 1253376 | tf_op jit(solution)/shard_map/all_gather | solution.py:482
  25.6 0.0 copy-start.4
  25.6 0.0 copy-start.8
  25.6 0.0 copy-start.9
  25.6 0.4 shard_map.130
  26.0 11.5 %all-gather.1 = f32[12,136,128]{2,1,0:T(8,128)S(1)} all-gather(f32[3,136,128]{2,1,0:T(8,128)S(1)} %get-tuple-element.27), channel_id=3, replica_groups=mesh['z'=16,'x'=4,'y'=4,'c'=2] {'y'}, dimensions={0}, use_global_device_ids=true | all-gather | bytes 1044480 | tf_op jit(solution)/shard_map/all_gather | solution.py:488
  37.6 0.0 copy-done.4
  37.6 0.0 copy-done.8
  37.6 0.0 copy-done.9
  37.6 3.7 %shard_map.131 = (bf16[2,3,128,128]{3,2,1,0:T(8,128)(2,1)S(1)}, bf16[2,3,128,128]{3,2,1,0:T(8,128)(2,1)S(1)}, bf16[2,3,128,128]{3,2,1,0:T(8,128)(2,1)S(1)}, f32[8,128]{1,0:T(8,128)S(1)}, f32[16,8,128]{2,1,0:T(8,128)S(1)}) custom-call(s32[6]{0:T(128)S(1)} %copy-done.8, s32[6]{0:T(128)S(1)} %copy-done.9, f32[4,3,136,128]{3,2,1,0:T(8,128)S(1)} %bitcast.9, ...), custom_call_target="tpu_custom_call" | custom-call | tf_op jit(solution)/shard_map/pallas_call | solution.py:27
  41.2 22.1 %all_to_all.50 = f32[16,8,128]{2,1,0:T(8,128)S(1)} all-to-all(f32[16,8,128]{2,1,0:T(8,128)S(1)} %get-tuple-element.28.base_ref), channel_id=1, replica_groups=mesh['z'=16,'x'=4,'y'=4,'c'=2] {'z'}, dimensions={0} | all-to-all | bytes 131072 | tf_op jit(solution)/shard_map/all_to_all | solution.py:419
  63.3 0.7 broadcast_in_dim.2
  64.0 4.3 %all-to-all-start.1 = ((f32[4,16,8,128]{3,2,1,0:T(8,128)}), f32[4,16,8,128]{3,2,1,0:T(8,128)S(1)}, u32[]{:S(2)}, u32[]{:S(2)}) async-start(f32[4,16,8,128]{3,2,1,0:T(8,128)} %broadcast_in_dim.2), calls=%async_computation.1 | async-start | bytes 524288 | tf_op jit(solution)/shard_map/all_to_all | solution.py:419
  68.4 0.0 all-gather.10.cloned.1.call-start
  68.4 5.5 %all-to-all-done.1 = f32[4,16,8,128]{3,2,1,0:T(8,128)S(1)} async-done(((f32[4,16,8,128]{3,2,1,0:T(8,128)}), f32[4,16,8,128]{3,2,1,0:T(8,128)S(1)}, u32[]{:S(2)}, u32[]{:S(2)}) %all-to-all-start.1) | async-done | bytes 262176 | tf_op jit(solution)/shard_map/all_to_all | solution.py:419
  73.9 6.4 %all_gather.37.terms_ref = f32[2,512,128]{2,1,0:T(8,128)S(1)} all-gather(f32[1,512,128]{2,1,0:T(8,128)S(1)} %bitcast.14), channel_id=1, replica_groups=mesh['z'=16,'x'=4,'y'=4,'c'=2] {'c'}, dimensions={0}, use_global_device_ids=true | all-gather | bytes 786432 | tf_op jit(solution)/shard_map/all_gather | solution.py:428
  80.3 0.8 shard_map.132
  81.1 0.1 convert_element_type.7.ids_ref.plane_ref
  81.2 0.0 all-gather.8.cloned.1.call-done.table_ref
  81.2 0.0 copy-start.1
  81.2 1.5 copy-done.1
  82.8 0.7 shard_map.134
  83.5 10.0 %all_to_all.51.picked_ref = f32[4,6,40,128]{3,2,1,0:T(8,128)S(1)} all-to-all(f32[4,6,40,128]{3,2,1,0:T(8,128)S(1)} %shard_map.134), channel_id=1, replica_groups=mesh['z'=16,'x'=4,'y'=4,'c'=2] {'x'}, dimensions={0} | all-to-all | bytes 983040 | tf_op jit(solution)/shard_map/all_to_all | solution.py:419
  93.5 0.9 shard_map.135
  94.4 0.0 all-gather.10.cloned.1.call-update
  94.4 8.5 %all_to_all.52.parts_ref = f32[4,8,128]{2,1,0:T(8,128)S(1)} all-to-all(f32[4,8,128]{2,1,0:T(8,128)S(1)} %get-tuple-element.35), channel_id=1, replica_groups=mesh['z'=16,'x'=4,'y'=4,'c'=2] {'y'}, dimensions={0} | all-to-all | bytes 32768 | tf_op jit(solution)/shard_map/all_to_all | solution.py:419
  102.9 0.3 shard_map.136
  103.1 18.2 %all_to_all.53.terms_ref = f32[16,8,128]{2,1,0:T(8,128)S(1)} all-to-all(f32[16,8,128]{2,1,0:T(8,128)S(1)} %shard_map.136), channel_id=1, replica_groups=mesh['z'=16,'x'=4,'y'=4,'c'=2] {'z'}, dimensions={0} | all-to-all | bytes 131072 | tf_op jit(solution)/shard_map/all_to_all | solution.py:419
  121.3 0.7 shard_map.137
  122.1 21.8 %all_to_all.54.parts_ref = f32[8,8,128]{2,1,0:T(8,128)S(1)} all-to-all(f32[8,8,128]{2,1,0:T(8,128)S(1)} %shard_map.137), channel_id=1, replica_groups=mesh['z'=16,'x'=4,'y'=4,'c'=2] {'x','c'}, dimensions={0} | all-to-all | bytes 65536 | tf_op jit(solution)/shard_map/all_to_all | solution.py:419
  143.8 0.0 all-gather.10.cloned.1.call-done
  143.8 0.0 copy-start.3
  143.8 1.2 copy-done.3
  145.1 0.0 copy-start.2
  145.1 0.0 copy-start.6
  145.1 0.0 copy-start.7
  145.1 0.7 shard_map.138
  145.8 14.2 %all_to_all.55.terms_ref = f32[16,8,128]{2,1,0:T(8,128)S(1)} all-to-all(f32[16,8,128]{2,1,0:T(8,128)S(1)} %get-tuple-element.39), channel_id=1, replica_groups=mesh['z'=16,'x'=4,'y'=4,'c'=2] {'z'}, dimensions={0} | all-to-all | bytes 131072 | tf_op jit(solution)/shard_map/all_to_all | solution.py:419
  160.0 0.7 shard_map.139
  160.7 9.0 %all_to_all.56.parts_ref = f32[8,8,128]{2,1,0:T(8,128)S(1)} all-to-all(f32[8,8,128]{2,1,0:T(8,128)S(1)} %shard_map.139), channel_id=1, replica_groups=mesh['z'=16,'x'=4,'y'=4,'c'=2] {'x','c'}, dimensions={0} | all-to-all | bytes 65536 | tf_op jit(solution)/shard_map/all_to_all | solution.py:419
  169.8 0.0 copy-start
  169.8 0.0 copy-start.5
  169.8 0.6 shard_map.140
  170.4 14.2 %all_to_all.57.terms_ref = f32[16,8,128]{2,1,0:T(8,128)S(1)} all-to-all(f32[16,8,128]{2,1,0:T(8,128)S(1)} %shard_map.140), channel_id=1, replica_groups=mesh['z'=16,'x'=4,'y'=4,'c'=2] {'z'}, dimensions={0} | all-to-all | bytes 131072 | tf_op jit(solution)/shard_map/all_to_all | solution.py:419
  184.6 0.9 shard_map.141
  185.6 9.3 %all_to_all.58.parts_ref = f32[8,16,128]{2,1,0:T(8,128)S(1)} all-to-all(f32[8,16,128]{2,1,0:T(8,128)S(1)} %shard_map.141), channel_id=1, replica_groups=mesh['z'=16,'x'=4,'y'=4,'c'=2] {'x','c'}, dimensions={0} | all-to-all | bytes 131072 | tf_op jit(solution)/shard_map/all_to_all | solution.py:419
  194.9 0.0 copy-done.2
  194.9 0.0 copy-done.6
  194.9 0.0 copy-done.7
  194.9 0.7 shard_map.142
  195.6 2.3 %all-gather.4 = f32[32,128]{1,0:T(8,128)S(1)} all-gather(f32[16,128]{1,0:T(8,128)S(1)} %shard_map.142), channel_id=6, replica_groups=mesh['z'=16,'x'=4,'y'=4,'c'=2] {'c'}, dimensions={0}, use_global_device_ids=true | all-gather | bytes 24576 | tf_op jit(solution)/shard_map/all_gather | solution.py:544
  197.9 0.0 copy-done
  197.9 0.0 copy-done.5
  197.9 2.3 %shard_map.143 = (f32[6,3,128]{2,1,0:T(4,128)}, f32[6,128]{1,0:T(8,128)}, f32[6,3,128]{2,1,0:T(4,128)}, f32[6,128]{1,0:T(8,128)}) custom-call(f32[2,16,128]{2,1,0:T(8,128)S(1)} %bitcast.13, bf16[2,6,128,128]{3,2,1,0:T(8,128)(2,1)S(1)} %get-tuple-element.44.other_ref, f32[6,8,128]{2,1,0:T(8,128)S(1)} %get-tuple-element.45.passing_ref, ...), custom_call_target="tpu_custom_call" | custom-call | tf_op jit(solution)/shard_map/pallas_call | solution.py:27
  (2 shorter events, 0.0 us)
Async XLA Ops:
  7.2 74.1 %all-gather.8.cloned.1.call-start = ((), (), s32[]{:S(2)}) async-start(), calls=%async_computation.10 | async-start | bytes 2088960 | tf_op jit(solution)/shard_map/all_gather | solution.py:462
  25.6 11.9 %copy-start.4 = (f32[6,128,128]{2,1,0:T(8,128)S(1)}, f32[6,128,128]{2,1,0:T(8,128)}, u32[]{:S(2)}) copy-start(f32[6,128,128]{2,1,0:T(8,128)} %outlet_ref.1) | copy-start | bytes 1179652
  25.6 11.9 %copy-start.8 = (s32[6]{0:T(128)S(1)}, s32[6]{0:T(128)}, u32[]{:S(2)}) copy-start(s32[6]{0:T(128)} %lower_ref.3) | copy-start | bytes 76
  25.6 11.9 %copy-start.9 = (s32[6]{0:T(128)S(1)}, s32[6]{0:T(128)}, u32[]{:S(2)}) copy-start(s32[6]{0:T(128)} %upper_ref.3) | copy-start | bytes 76
  64.0 9.9 %all-to-all-start.1 = ((f32[4,16,8,128]{3,2,1,0:T(8,128)}), f32[4,16,8,128]{3,2,1,0:T(8,128)S(1)}, u32[]{:S(2)}, u32[]{:S(2)}) async-start(f32[4,16,8,128]{3,2,1,0:T(8,128)} %broadcast_in_dim.2), calls=%async_computation.1 | async-start | bytes 524288 | tf_op jit(solution)/shard_map/all_to_all | solution.py:419
  68.4 75.5 %all-gather.10.cloned.1.call-start = ((), (), s32[]{:S(2)}) async-start(), calls=%async_computation.11 | async-start | bytes 1351680 | tf_op jit(solution)/shard_map/all_gather | solution.py:516
  81.2 1.6 copy-start.1
  143.8 1.2 copy-start.3
  145.1 49.8 %copy-start.2 = (f32[6,128,128]{2,1,0:T(8,128)S(1)}, f32[6,128,128]{2,1,0:T(8,128)}, u32[]{:S(2)}) copy-start(f32[6,128,128]{2,1,0:T(8,128)} %inv_ref.3) | copy-start | bytes 1179652
  145.1 49.8 %copy-start.6 = (f32[6,128]{1,0:T(8,128)S(1)}, f32[6,128]{1,0:T(8,128)}, u32[]{:S(2)}) copy-start(f32[6,128]{1,0:T(8,128)} %residual_ref.3) | copy-start | bytes 9220
  145.1 49.8 %copy-start.7 = (f32[6,128]{1,0:T(8,128)S(1)}, f32[6,128]{1,0:T(8,128)}, u32[]{:S(2)}) copy-start(f32[6,128]{1,0:T(8,128)} %cotangent_ref.3) | copy-start | bytes 9220
  169.8 28.2 %copy-start = (bf16[2,6,5,128,128]{4,3,2,1,0:T(8,128)(2,1)S(1)}, bf16[2,6,5,128,128]{4,3,2,1,0:T(8,128)(2,1)}, u32[]{:S(2)}) copy-start(bf16[2,6,5,128,128]{4,3,2,1,0:T(8,128)(2,1)} %get-tuple-element.46.maps_ref) | copy-start | bytes 5898244
  169.8 28.2 %copy-start.5 = (f32[6,8,128]{2,1,0:T(8,128)S(1)}, f32[6,8,128]{2,1,0:T(8,128)}, u32[]{:S(2)}) copy-start(f32[6,8,128]{2,1,0:T(8,128)} %get-tuple-element.47.vectors_ref) | copy-start | bytes 73732
Sparse Core Ops, SparseCore 0:
  10.1 69.9 all-gather.7
  94.5 36.6 all-gather.9

commit v10 on v9

--- a/solution.py
+++ b/solution.py
@@ -216,17 +216,24 @@
 
 
 def pick_kernel(ids_ref, table_ref, out_ref):
-    dests, owned = out_ref.shape[:2]
+    dests = out_ref.shape[0]
+    piece = table_ref.shape[1] - 8
+    owned = (out_ref.shape[1] - 8) // piece
     half = owned // 2
     x, c = lax.axis_index("x"), lax.axis_index("c")
     for d in range(dests):
+        ends = []
         for t in range(owned):
             junction = ids_ref[(c * dests + d) * owned + (t + half) % owned]
             basin = lax.div(junction, owned)
             line = lax.div(basin, dests)
             at = line * owned + (junction - basin * owned)
             here = basin - line * dests == x
-            out_ref[d, t] = jnp.where(here, table_ref[at], 0.0)
+            found = jnp.where(here, table_ref[at], 0.0)
+            out_ref[d, t * piece : (t + 1) * piece] = found[:piece]
+            row = piece + (0 if t < half else 1)
+            ends.append(found[row : row + 1])
+        out_ref[d, owned * piece :] = jnp.concatenate(ends + [jnp.zeros((2, WIDTH), F32)])
 
 
 def rule(above, below, half):
@@ -318,30 +325,27 @@
 
 
 def partial_kernel(flows_ref, picked_ref, rows_ref, merged_ref, spread_ref, tile_ref):
-    half = picked_ref.shape[1] // 2
-    piece = picked_ref.shape[2] - 8
+    owned = merged_ref.shape[0]
+    half = owned // 2
+    piece = (picked_ref.shape[1] - 8) // owned
     start = pl.multiple_of(lax.axis_index("y") * piece, 8)
     merged = picked_ref[0]
     for d in range(1, picked_ref.shape[0]):
         merged = merged + picked_ref[d]
-    merged_ref[:, : piece + 8] = merged
-    merged_ref[:, piece + 8 :] = jnp.zeros(
-        (2 * half, merged_ref.shape[1] - piece - 8, WIDTH), F32
-    )
+    ends = merged[owned * piece :]
+    rows_ref[...] = ends
+    merged_ref[:, piece:] = jnp.zeros((owned, merged_ref.shape[1] - piece, WIDTH), F32)
     tile_ref[...] = jnp.zeros(tile_ref.shape, F32)
+    for k in range(owned):
+        rows = merged[k * piece : (k + 1) * piece]
+        merged_ref[k, :piece] = rows
+        tile_ref[k, pl.ds(start, piece)] = rows
+    full = ends + flows_ref[...]
     payload = [jnp.zeros((1, WIDTH), F32)] * 8
-    ends = [jnp.zeros((1, WIDTH), F32)] * 8
     for k in range(half):
         other = half + k
-        ends[k] = merged[k, piece : piece + 1]
-        ends[other] = merged[other, piece + 1 : piece + 2]
-        tile_ref[k, pl.ds(start, piece)] = merged[k, :piece]
-        tile_ref[other, pl.ds(start, piece)] = merged[other, :piece]
-        payload[k] = applied(tile_ref[k], ends[k] + flows_ref[k : k + 1])
-        payload[other] = applied_transposed(
-            tile_ref[other], ends[other] + flows_ref[other : other + 1]
-        )
-    rows_ref[...] = jnp.concatenate(ends)
+        payload[k] = applied(tile_ref[k], full[k : k + 1])
+        payload[other] = applied_transposed(tile_ref[other], full[other : other + 1])
     spread_rows(payload, spread_ref)
 
 
@@ -505,7 +509,7 @@
         lower, upper, terms, scalars=2,
     )
     plane, flows = lax.optimization_barrier((plane, flows))
-    picked = run(pick_kernel, array(xs, owned, piece + 8, width), plane, table, scalars=1)
+    picked = run(pick_kernel, array(xs, owned * piece + 8, width), plane, table, scalars=1)
     rows, merged, parts = run(
         partial_kernel,
         [array(8, width), array(owned, 2 * piece + 24, width), array(ys, 8, width)],

time: 208 us -> 207 us (level)
  no operation moved by 1% of the time
where the time goes in v10:
time: 207 us
  blocking collectives  156 us (75%)
  Pallas kernels  22.7 us (11%)
  between operations  14.1 us (7%)
  waiting for transfers between devices  5.56 us (3%)
  starting transfers between devices  4.38 us (2%)
  local copies, waits for them, and re-layouts  3.63 us (2%)
    all_to_all x9, blocking collectives, swap(): return lax.all_to_all(spread, axis, 0, 0, tiled=False)  127 us
    pallas_call x15, Pallas kernels, run(): pl.pallas_call(kernel, out_shape=shapes, in_specs=[smem] * scalars + [whe...  22.7 us
    all_gather x1, blocking collectives, shards(): chips = lax.all_gather(chip, 'y')  11.5 us
    all_gather x1, blocking collectives, shards(): pair = lax.all_gather(local, 'c')  9.12 us
    all_gather x1, blocking collectives, exchanged(): return lax.all_gather(along_x.reshape(-1, WIDTH), 'c')  6.38 us
    all_to_all x1, waiting for transfers between devices, swap(): return lax.all_to_all(spread, axis, 0, 0, tiled=False)  5.53 us
    all_to_all x1, starting transfers between devices, swap(): return lax.all_to_all(spread, axis, 0, 0, tiled=False)  4.34 us
  transfers between devices with their start and end apart: 3, of which 1 were waited for; matrix products, arithmetic and copies ran while one was open for 0% of the time, Pallas kernels for 7%

profile of v10, /device:TPU:1, one launch (start us, length us, event | category | flops | bytes accessed | tf_op | source)
XLA Modules:
  0.0 206.6 jit_solution(12737031582704145044)
XLA Ops:
  7.2 0.0 all-gather.8.cloned.1.call-start
  7.2 1.6 shard_map.133
  8.8 0.0 all-gather.8.cloned.1.call-update
  8.8 7.7 %shard_map.129 = (bf16[2,6,5,128,128]{4,3,2,1,0:T(8,128)(2,1)}, f32[6,8,128]{2,1,0:T(8,128)}, f32[6,136,128]{2,1,0:T(8,128)}) custom-call(f32[6,3,128,128]{3,2,1,0:T(8,128)} %inv_hbm.1, f32[6,3,128,128]{3,2,1,0:T(8,128)} %link_hbm.1, f32[6,3,128]{2,1,0:T(4,128)} %residual_hbm.1, f32[6,3,128]{2,1,0:T(4,128)} %cotangent_hbm.1), custom_call_target="tpu_custom_call" | custom-call | flops 2000000000 | bytes 20000000 | tf_op jit(solution)/shard_map/pallas_call | solution.py:27
  16.5 9.1 %all-gather = f32[12,136,128]{2,1,0:T(8,128)S(1)} all-gather(f32[6,136,128]{2,1,0:T(8,128)} %get-tuple-element.26), channel_id=2, replica_groups=mesh['z'=16,'x'=4,'y'=4,'c'=2] {'c'}, dimensions={0}, use_global_device_ids=true | all-gather | bytes 1253376 | tf_op jit(solution)/shard_map/all_gather | solution.py:486
  25.6 0.0 copy-start.4
  25.6 0.0 copy-start.8
  25.6 0.0 copy-start.9
  25.6 0.4 shard_map.130
  26.0 11.5 %all-gather.1 = f32[12,136,128]{2,1,0:T(8,128)S(1)} all-gather(f32[3,136,128]{2,1,0:T(8,128)S(1)} %get-tuple-element.27), channel_id=3, replica_groups=mesh['z'=16,'x'=4,'y'=4,'c'=2] {'y'}, dimensions={0}, use_global_device_ids=true | all-gather | bytes 1044480 | tf_op jit(solution)/shard_map/all_gather | solution.py:492
  37.6 0.0 copy-done.4
  37.6 0.0 copy-done.8
  37.6 0.0 copy-done.9
  37.6 3.7 %shard_map.131 = (bf16[2,3,128,128]{3,2,1,0:T(8,128)(2,1)S(1)}, bf16[2,3,128,128]{3,2,1,0:T(8,128)(2,1)S(1)}, bf16[2,3,128,128]{3,2,1,0:T(8,128)(2,1)S(1)}, f32[8,128]{1,0:T(8,128)S(1)}, f32[16,8,128]{2,1,0:T(8,128)S(1)}) custom-call(s32[6]{0:T(128)S(1)} %copy-done.8, s32[6]{0:T(128)S(1)} %copy-done.9, f32[4,3,136,128]{3,2,1,0:T(8,128)S(1)} %bitcast.9, ...), custom_call_target="tpu_custom_call" | custom-call | tf_op jit(solution)/shard_map/pallas_call | solution.py:27
  41.2 22.1 %all_to_all.50 = f32[16,8,128]{2,1,0:T(8,128)S(1)} all-to-all(f32[16,8,128]{2,1,0:T(8,128)S(1)} %get-tuple-element.28.base_ref), channel_id=1, replica_groups=mesh['z'=16,'x'=4,'y'=4,'c'=2] {'z'}, dimensions={0} | all-to-all | bytes 131072 | tf_op jit(solution)/shard_map/all_to_all | solution.py:423
  63.3 0.7 broadcast_in_dim.2
  64.0 4.3 %all-to-all-start.1 = ((f32[4,16,8,128]{3,2,1,0:T(8,128)}), f32[4,16,8,128]{3,2,1,0:T(8,128)S(1)}, u32[]{:S(2)}, u32[]{:S(2)}) async-start(f32[4,16,8,128]{3,2,1,0:T(8,128)} %broadcast_in_dim.2), calls=%async_computation.1 | async-start | bytes 524288 | tf_op jit(solution)/shard_map/all_to_all | solution.py:423
  68.4 0.0 all-gather.10.cloned.1.call-start
  68.4 5.5 %all-to-all-done.1 = f32[4,16,8,128]{3,2,1,0:T(8,128)S(1)} async-done(((f32[4,16,8,128]{3,2,1,0:T(8,128)}), f32[4,16,8,128]{3,2,1,0:T(8,128)S(1)}, u32[]{:S(2)}, u32[]{:S(2)}) %all-to-all-start.1) | async-done | bytes 262176 | tf_op jit(solution)/shard_map/all_to_all | solution.py:423
  73.9 6.4 %all_gather.37.terms_ref = f32[2,512,128]{2,1,0:T(8,128)S(1)} all-gather(f32[1,512,128]{2,1,0:T(8,128)S(1)} %bitcast.14), channel_id=1, replica_groups=mesh['z'=16,'x'=4,'y'=4,'c'=2] {'c'}, dimensions={0}, use_global_device_ids=true | all-gather | bytes 786432 | tf_op jit(solution)/shard_map/all_gather | solution.py:432
  80.3 0.8 shard_map.132
  81.1 0.1 convert_element_type.7.ids_ref.plane_ref
  81.2 0.0 all-gather.8.cloned.1.call-done.table_ref
  81.2 0.0 copy-start.1
  81.2 1.5 copy-done.1
  82.8 0.7 shard_map.134
  83.5 9.5 %all_to_all.51.picked_ref = f32[4,200,128]{2,1,0:T(8,128)S(1)} all-to-all(f32[4,200,128]{2,1,0:T(8,128)S(1)} %shard_map.134), channel_id=1, replica_groups=mesh['z'=16,'x'=4,'y'=4,'c'=2] {'x'}, dimensions={0} | all-to-all | bytes 819200 | tf_op jit(solution)/shard_map/all_to_all | solution.py:423
  93.1 0.8 shard_map.135
  93.8 0.0 all-gather.10.cloned.1.call-update
  93.9 8.3 %all_to_all.52.parts_ref = f32[4,8,128]{2,1,0:T(8,128)S(1)} all-to-all(f32[4,8,128]{2,1,0:T(8,128)S(1)} %get-tuple-element.35), channel_id=1, replica_groups=mesh['z'=16,'x'=4,'y'=4,'c'=2] {'y'}, dimensions={0} | all-to-all | bytes 32768 | tf_op jit(solution)/shard_map/all_to_all | solution.py:423
  102.2 0.3 shard_map.136
  102.5 18.2 %all_to_all.53.terms_ref = f32[16,8,128]{2,1,0:T(8,128)S(1)} all-to-all(f32[16,8,128]{2,1,0:T(8,128)S(1)} %shard_map.136), channel_id=1, replica_groups=mesh['z'=16,'x'=4,'y'=4,'c'=2] {'z'}, dimensions={0} | all-to-all | bytes 131072 | tf_op jit(solution)/shard_map/all_to_all | solution.py:423
  120.7 0.7 shard_map.137
  121.4 21.9 %all_to_all.54.parts_ref = f32[8,8,128]{2,1,0:T(8,128)S(1)} all-to-all(f32[8,8,128]{2,1,0:T(8,128)S(1)} %shard_map.137), channel_id=1, replica_groups=mesh['z'=16,'x'=4,'y'=4,'c'=2] {'x','c'}, dimensions={0} | all-to-all | bytes 65536 | tf_op jit(solution)/shard_map/all_to_all | solution.py:423
  143.3 0.0 all-gather.10.cloned.1.call-done
  143.3 0.0 copy-start.3
  143.3 1.2 copy-done.3
  144.6 0.0 copy-start.2
  144.6 0.0 copy-start.6
  144.6 0.0 copy-start.7
  144.6 0.7 shard_map.138
  145.2 14.2 %all_to_all.55.terms_ref = f32[16,8,128]{2,1,0:T(8,128)S(1)} all-to-all(f32[16,8,128]{2,1,0:T(8,128)S(1)} %get-tuple-element.39), channel_id=1, replica_groups=mesh['z'=16,'x'=4,'y'=4,'c'=2] {'z'}, dimensions={0} | all-to-all | bytes 131072 | tf_op jit(solution)/shard_map/all_to_all | solution.py:423
  159.5 0.7 shard_map.139
  160.2 9.0 %all_to_all.56.parts_ref = f32[8,8,128]{2,1,0:T(8,128)S(1)} all-to-all(f32[8,8,128]{2,1,0:T(8,128)S(1)} %shard_map.139), channel_id=1, replica_groups=mesh['z'=16,'x'=4,'y'=4,'c'=2] {'x','c'}, dimensions={0} | all-to-all | bytes 65536 | tf_op jit(solution)/shard_map/all_to_all | solution.py:423
  169.2 0.0 copy-start
  169.2 0.0 copy-start.5
  169.2 0.6 shard_map.140
  169.9 14.2 %all_to_all.57.terms_ref = f32[16,8,128]{2,1,0:T(8,128)S(1)} all-to-all(f32[16,8,128]{2,1,0:T(8,128)S(1)} %shard_map.140), channel_id=1, replica_groups=mesh['z'=16,'x'=4,'y'=4,'c'=2] {'z'}, dimensions={0} | all-to-all | bytes 131072 | tf_op jit(solution)/shard_map/all_to_all | solution.py:423
  184.1 0.9 shard_map.141
  185.1 9.3 %all_to_all.58.parts_ref = f32[8,16,128]{2,1,0:T(8,128)S(1)} all-to-all(f32[8,16,128]{2,1,0:T(8,128)S(1)} %shard_map.141), channel_id=1, replica_groups=mesh['z'=16,'x'=4,'y'=4,'c'=2] {'x','c'}, dimensions={0} | all-to-all | bytes 131072 | tf_op jit(solution)/shard_map/all_to_all | solution.py:423
  194.4 0.0 copy-done.2
  194.4 0.0 copy-done.6
  194.4 0.0 copy-done.7
  194.4 0.7 shard_map.142
  195.1 2.3 %all-gather.4 = f32[32,128]{1,0:T(8,128)S(1)} all-gather(f32[16,128]{1,0:T(8,128)S(1)} %shard_map.142), channel_id=6, replica_groups=mesh['z'=16,'x'=4,'y'=4,'c'=2] {'c'}, dimensions={0}, use_global_device_ids=true | all-gather | bytes 24576 | tf_op jit(solution)/shard_map/all_gather | solution.py:548
  197.4 0.0 copy-done
  197.4 0.0 copy-done.5
  197.4 2.3 %shard_map.143 = (f32[6,3,128]{2,1,0:T(4,128)}, f32[6,128]{1,0:T(8,128)}, f32[6,3,128]{2,1,0:T(4,128)}, f32[6,128]{1,0:T(8,128)}) custom-call(f32[2,16,128]{2,1,0:T(8,128)S(1)} %bitcast.13, bf16[2,6,128,128]{3,2,1,0:T(8,128)(2,1)S(1)} %get-tuple-element.44.other_ref, f32[6,8,128]{2,1,0:T(8,128)S(1)} %get-tuple-element.45.passing_ref, ...), custom_call_target="tpu_custom_call" | custom-call | tf_op jit(solution)/shard_map/pallas_call | solution.py:27
  (2 shorter events, 0.0 us)
Async XLA Ops:
  7.2 74.1 %all-gather.8.cloned.1.call-start = ((), (), s32[]{:S(2)}) async-start(), calls=%async_computation.10 | async-start | bytes 2088960 | tf_op jit(solution)/shard_map/all_gather | solution.py:466
  25.6 11.9 %copy-start.4 = (f32[6,128,128]{2,1,0:T(8,128)S(1)}, f32[6,128,128]{2,1,0:T(8,128)}, u32[]{:S(2)}) copy-start(f32[6,128,128]{2,1,0:T(8,128)} %outlet_ref.1) | copy-start | bytes 1179652
  25.6 11.9 %copy-start.8 = (s32[6]{0:T(128)S(1)}, s32[6]{0:T(128)}, u32[]{:S(2)}) copy-start(s32[6]{0:T(128)} %lower_ref.3) | copy-start | bytes 76
  25.6 11.9 %copy-start.9 = (s32[6]{0:T(128)S(1)}, s32[6]{0:T(128)}, u32[]{:S(2)}) copy-start(s32[6]{0:T(128)} %upper_ref.3) | copy-start | bytes 76
  64.0 9.9 %all-to-all-start.1 = ((f32[4,16,8,128]{3,2,1,0:T(8,128)}), f32[4,16,8,128]{3,2,1,0:T(8,128)S(1)}, u32[]{:S(2)}, u32[]{:S(2)}) async-start(f32[4,16,8,128]{3,2,1,0:T(8,128)} %broadcast_in_dim.2), calls=%async_computation.1 | async-start | bytes 524288 | tf_op jit(solution)/shard_map/all_to_all | solution.py:423
  68.4 75.0 %all-gather.10.cloned.1.call-start = ((), (), s32[]{:S(2)}) async-start(), calls=%async_computation.11 | async-start | bytes 1351680 | tf_op jit(solution)/shard_map/all_gather | solution.py:520
  81.2 1.6 copy-start.1
  143.3 1.2 copy-start.3
  144.6 49.8 %copy-start.2 = (f32[6,128,128]{2,1,0:T(8,128)S(1)}, f32[6,128,128]{2,1,0:T(8,128)}, u32[]{:S(2)}) copy-start(f32[6,128,128]{2,1,0:T(8,128)} %inv_ref.3) | copy-start | bytes 1179652
  144.6 49.8 %copy-start.6 = (f32[6,128]{1,0:T(8,128)S(1)}, f32[6,128]{1,0:T(8,128)}, u32[]{:S(2)}) copy-start(f32[6,128]{1,0:T(8,128)} %residual_ref.3) | copy-start | bytes 9220
  144.6 49.8 %copy-start.7 = (f32[6,128]{1,0:T(8,128)S(1)}, f32[6,128]{1,0:T(8,128)}, u32[]{:S(2)}) copy-start(f32[6,128]{1,0:T(8,128)} %cotangent_ref.3) | copy-start | bytes 9220
  169.2 28.2 %copy-start = (bf16[2,6,5,128,128]{4,3,2,1,0:T(8,128)(2,1)S(1)}, bf16[2,6,5,128,128]{4,3,2,1,0:T(8,128)(2,1)}, u32[]{:S(2)}) copy-start(bf16[2,6,5,128,128]{4,3,2,1,0:T(8,128)(2,1)} %get-tuple-element.46.maps_ref) | copy-start | bytes 5898244
  169.2 28.2 %copy-start.5 = (f32[6,8,128]{2,1,0:T(8,128)S(1)}, f32[6,8,128]{2,1,0:T(8,128)}, u32[]{:S(2)}) copy-start(f32[6,8,128]{2,1,0:T(8,128)} %get-tuple-element.47.vectors_ref) | copy-start | bytes 73732
Sparse Core Ops, SparseCore 0:
  10.1 69.9 all-gather.7
  94.0 36.6 all-gather.9
